TPU v7x, 32 devices: a whole 2x2x4 slice. The times are simulated.
32 devices in a mesh: batch: 16 (over z, y, x), seq: 2 (over core).
Axes of the slice: x: 2, y: 2, z: 4, core: 2. Of those that a mesh axis runs over, the one named last changes fastest.
Arguments:
- word_ids: int32 [64, 1024], P('batch', 'seq'), may hold values from 0 to 3839
- buckets: int32 [64], P('batch'), may hold values from 0 to 7
- noise: bfloat16 [64, 1024, 128], P('batch', 'seq'), may hold values from -6 to 6
- table: bfloat16 [3840, 128], P(('batch', 'seq')), may hold values from -10 to 10
- w_in: bfloat16 [128, 768], replicated, may hold values from -0.5 to 0.5
- time_table: float32 [8, 768], replicated, may hold values from -6 to 6
- pos_table: float32 [1024, 768], replicated, may hold values from -6 to 6
- gain_attn: float32 [768], replicated, may hold values from 0.1 to 1.9
- w_qkv: bfloat16 [768, 2304], replicated, may hold values from -0.3125 to 0.3125
- w_out: bfloat16 [768, 768], replicated, may hold values from -0.875 to 0.875
- gain_mlp: float32 [768], replicated, may hold values from 0.1 to 1.9
- w_up: bfloat16 [768, 3072], replicated, may hold values from -0.21875 to 0.21875
- w_down: bfloat16 [3072, 768], replicated, may hold values from -0.109375 to 0.109375
- w_head: bfloat16 [768, 128], replicated, may hold values from -0.21875 to 0.21875
Outputs:
- output: bfloat16 [64, 1024, 768], P('batch', 'seq')
- grad_table: float32 [3840, 128], P(('batch', 'seq'))
- grad_w_in: float32 [128, 768], replicated
- grad_time: float32 [8, 768], replicated
- grad_pos: float32 [1024, 768], replicated
- grad_gain_attn: float32 [768], replicated
- grad_qkv: float32 [768, 2304], replicated
- grad_out: float32 [768, 768], replicated
- grad_gain_mlp: float32 [768], replicated
- grad_up: float32 [768, 3072], replicated
- grad_down: float32 [3072, 768], replicated
- grad_head: float32 [768, 128], replicated
- mean_norm: float32 [], replicated
All inputs are finite; a program needn't handle non-finite values.
Results may differ from a plain program's by a relative error of at most 0.0065.
Values may be sent and summed in bfloat16 or wider, within the bound.
No kernel may reach another device: no remote copies, remote signals or barrier semaphores. Data moves between devices by JAX's collectives and lax.ppermute only.
A program may use at most 256 MiB of HBM per device.

v0:
```python
import math

import jax
import jax.numpy as jnp
from jax import lax
from jax.sharding import PartitionSpec as P

HEAD = 64


def layer_norm(hidden, gain_vec):
    centre = hidden - jnp.mean(hidden, axis=-1, keepdims=True)
    return centre * lax.rsqrt(jnp.mean(centre * centre, axis=-1, keepdims=True) + 1e-05) * gain_vec


def dense(left, right):
    return jnp.dot(left, right, preferred_element_type=jnp.float32)


def outer(left, right):
    return lax.dot_general(
        left, right, (((0,), (0,)), ((), ())), preferred_element_type=jnp.float32
    )


def dense_back(left, right):
    return lax.dot_general(
        left, right, (((1,), (1,)), ((), ())), preferred_element_type=jnp.float32
    )


def attend_block(query_block, key_rows, value_rows):
    scores = jnp.einsum(
        "qhd,khd->hqk", query_block, key_rows, preferred_element_type=jnp.float32
    ) * HEAD ** (-0.5)
    row_peak = jnp.max(scores, axis=-1, keepdims=True)
    raised = jnp.exp(scores - row_peak)
    denominator = jnp.sum(raised, axis=-1, keepdims=True)
    prob_block = (raised / denominator).astype(jnp.bfloat16)
    mixed_out = jnp.einsum(
        "hqk,khd->qhd", prob_block, value_rows, preferred_element_type=jnp.float32
    )
    return (mixed_out.astype(jnp.bfloat16), (row_peak + jnp.log(denominator))[..., 0])


def attend_sequence(packed):
    seq_len, head_width = (packed.shape[0], packed.shape[2])
    local_heads = head_width // HEAD
    block_rows = min(512, seq_len)
    split_parts = packed.reshape(seq_len, 3, local_heads, HEAD)
    queries = split_parts[:, 0].reshape(seq_len // block_rows, block_rows, local_heads, HEAD)

    def single(query_block):
        return attend_block(query_block, split_parts[:, 1], split_parts[:, 2])

    mixed_out, log_totals = lax.map(single, queries)
    log_totals = jnp.transpose(log_totals, (1, 0, 2)).reshape(local_heads, seq_len)
    return (mixed_out.reshape(seq_len, head_width), log_totals)


def attend_items(item_list):
    mixed_out, log_totals = lax.map(attend_sequence, item_list)
    return (mixed_out, log_totals, item_list)


def attend_back(item_list):
    packed, log_totals, grad_mixed = item_list
    seq_len, head_width = (packed.shape[0], packed.shape[2])
    local_heads = head_width // HEAD
    block_rows = min(512, seq_len)
    blocks = seq_len // block_rows
    scale_head = HEAD ** (-0.5)
    split_parts = packed.reshape(seq_len, 3, local_heads, HEAD)
    key_rows, value_rows = (split_parts[:, 1], split_parts[:, 2])
    queries = split_parts[:, 0].reshape(blocks, block_rows, local_heads, HEAD)
    grad_blocks = grad_mixed.reshape(blocks, block_rows, local_heads, HEAD)
    total_blocks = jnp.transpose(log_totals.reshape(local_heads, blocks, block_rows), (1, 0, 2))

    def advance(running, block_items):
        grad_keys, grad_values = running
        query_block, grad_block, total_block = block_items
        scores = (
            jnp.einsum("qhd,khd->hqk", query_block, key_rows, preferred_element_type=jnp.float32)
            * scale_head
        )
        prob_block = jnp.exp(scores - total_block[:, :, None])
        grad_values = grad_values + jnp.einsum(
            "hqk,qhd->khd",
            prob_block.astype(jnp.bfloat16),
            grad_block,
            preferred_element_type=jnp.float32,
        )
        grad_probs = jnp.einsum(
            "qhd,khd->hqk", grad_block, value_rows, preferred_element_type=jnp.float32
        )
        inner = jnp.sum(prob_block * grad_probs, axis=-1, keepdims=True)
        grad_scores = (prob_block * (grad_probs - inner)).astype(jnp.bfloat16)
        grad_query = (
            jnp.einsum("hqk,khd->qhd", grad_scores, key_rows, preferred_element_type=jnp.float32)
            * scale_head
        )
        grad_keys = (
            grad_keys
            + jnp.einsum(
                "hqk,qhd->khd", grad_scores, query_block, preferred_element_type=jnp.float32
            )
            * scale_head
        )
        return ((grad_keys, grad_values), grad_query)

    zeros_state = jnp.zeros((seq_len, local_heads, HEAD), jnp.float32)
    final_state, grad_queries = lax.scan(
        advance, (zeros_state, zeros_state), (queries, grad_blocks, total_blocks)
    )
    stacked = jnp.stack(
        [
            grad_queries.reshape(seq_len, head_width),
            final_state[0].reshape(seq_len, head_width),
            final_state[1].reshape(seq_len, head_width),
        ],
        axis=1,
    )
    return stacked.astype(jnp.bfloat16)


def reduce_mlp(grad_up, grad_down):
    joined = jnp.concatenate([grad_up.reshape(-1, 128), grad_down.reshape(-1, 128)], axis=0)
    shared = lax.psum_scatter(joined, ("batch", "seq"), scatter_dimension=0, tiled=True)
    whole = lax.all_gather(
        shared.astype(jnp.bfloat16), ("batch", "seq"), axis=0, tiled=True
    ).astype(shared.dtype)
    border = grad_up.size // 128
    return (whole[:border].reshape(grad_up.shape), whole[border:].reshape(grad_down.shape))


def reduce_attn(grad_qkv, grad_out):
    joined = jnp.concatenate([grad_qkv.reshape(-1, 128), grad_out.reshape(-1, 128)], axis=0)
    shared = lax.psum_scatter(joined, ("batch", "seq"), scatter_dimension=0, tiled=True)
    whole = lax.all_gather(
        shared.astype(jnp.bfloat16), ("batch", "seq"), axis=0, tiled=True
    ).astype(shared.dtype)
    border = grad_qkv.size // 128
    return (whole[:border].reshape(grad_qkv.shape), whole[border:].reshape(grad_out.shape))


def local(
    word_ids,
    buckets,
    noise,
    table,
    w_in,
    time_table,
    pos_table,
    gain_attn,
    w_qkv,
    w_out,
    gain_mlp,
    w_up,
    w_down,
    w_head,
):
    seq_rows, half_len = word_ids.shape
    token_rows = seq_rows * half_len
    model_width = w_qkv.shape[0]
    embed_width = table.shape[1]
    table_span = table.shape[0]
    vocab_rows = table_span * lax.axis_size(("batch", "seq"))
    bucket_count = time_table.shape[0]
    seq_group = lax.axis_size("seq")
    full_len = half_len * seq_group
    head_width = model_width // seq_group
    table_data = table.astype(jnp.float32)
    row_norms = jnp.sqrt(jnp.sum(table_data * table_data, axis=1) + 1e-06)
    bucket_hot = (buckets[:, None] == jnp.arange(bucket_count, dtype=jnp.int32)[None, :]).astype(
        jnp.float32
    )
    norm_total, count_total = lax.psum(
        (jnp.sum(row_norms), jnp.sum(bucket_hot, axis=0)), ("batch", "seq")
    )
    count_total = count_total / seq_group
    mean_norm = norm_total / vocab_rows
    factor = math.sqrt(embed_width) / mean_norm
    flat_ids = word_ids.reshape(token_rows)
    whole_table = lax.all_gather(table, ("batch", "seq"), axis=0, tiled=True)
    gathered = jnp.take(whole_table, flat_ids, axis=0).astype(jnp.float32)
    clean_emb = gathered * factor
    angles = math.pi / 2 * (buckets.astype(jnp.float32) + 1.0) / (bucket_count + 1)
    signal = jnp.repeat(jnp.cos(angles), half_len)[:, None]
    spread = jnp.repeat(jnp.sin(angles), half_len)[:, None]
    noisy_low = (
        signal * clean_emb + spread * noise.reshape(token_rows, embed_width).astype(jnp.float32)
    ).astype(jnp.bfloat16)
    time_rows = jnp.dot(bucket_hot, time_table, precision=lax.Precision.HIGHEST)
    position_start = lax.axis_index("seq") * half_len
    pos_local = lax.dynamic_slice_in_dim(pos_table, position_start, half_len, 0)
    stream_in = dense(noisy_low, w_in) + jnp.repeat(time_rows, half_len, axis=0)
    stream_in = (
        stream_in.reshape(seq_rows, half_len, model_width) + pos_local[None, :, :]
    ).reshape(token_rows, model_width)
    attn_in = layer_norm(stream_in, gain_attn).astype(jnp.bfloat16)
    head_start = lax.axis_index("seq") * head_width
    w_local = lax.dynamic_slice_in_dim(
        w_qkv.reshape(model_width, 3, model_width), head_start, head_width, 2
    )
    w_local = w_local.reshape(model_width, 3 * head_width)
    packed = dense(attn_in, w_qkv).astype(jnp.bfloat16).reshape(seq_rows, half_len, 3, model_width)
    mixed_heads, log_totals, packed_heads = attend_items(
        lax.all_to_all(packed, "seq", split_axis=3, concat_axis=1, tiled=True)
    )
    mixed_out = lax.all_to_all(mixed_heads, "seq", split_axis=1, concat_axis=2, tiled=True).reshape(
        token_rows, model_width
    )
    stream_mid = stream_in + dense(mixed_out, w_out)
    mlp_in = layer_norm(stream_mid, gain_mlp).astype(jnp.bfloat16)
    up_proj = dense(mlp_in, w_up)
    activated, gelu_back = jax.vjp(jax.nn.gelu, up_proj)
    activated_low = activated.astype(jnp.bfloat16)
    stream_out = stream_mid + dense(activated_low, w_down)
    output_low = stream_out.astype(jnp.bfloat16)
    prediction = dense(output_low, w_head)
    seq_weight = 1.0 / jnp.sum(bucket_hot * count_total[None, :], axis=1)
    grad_pred = (prediction - clean_emb) * jnp.repeat(seq_weight, half_len)[:, None]
    grad_pred_low = grad_pred.astype(jnp.bfloat16)
    grad_head = outer(output_low, grad_pred_low)
    grad_stream_out = dense_back(grad_pred_low, w_head)
    grad_branch = grad_stream_out.astype(jnp.bfloat16)
    grad_down = outer(activated_low, grad_branch)
    grad_upin = gelu_back(dense_back(grad_branch, w_down))[0].astype(jnp.bfloat16)
    grad_up = outer(mlp_in, grad_upin)
    second_back = jax.vjp(layer_norm, stream_mid, gain_mlp)[1]
    grad_mid_part, grad_gain_mlp = second_back(dense_back(grad_upin, w_up))
    grad_mid = grad_stream_out + grad_mid_part
    grad_attn = grad_mid.astype(jnp.bfloat16)
    grad_out = outer(mixed_out, grad_attn)
    grad_mixed = (
        dense_back(grad_attn, w_out).astype(jnp.bfloat16).reshape(seq_rows, half_len, model_width)
    )
    grad_heads = lax.all_to_all(grad_mixed, "seq", split_axis=2, concat_axis=1, tiled=True)
    grad_packed_heads = lax.map(attend_back, (packed_heads, log_totals, grad_heads))
    grad_packed = lax.all_to_all(
        grad_packed_heads, "seq", split_axis=1, concat_axis=3, tiled=True
    ).reshape(token_rows, 3 * model_width)
    grad_qkv = outer(attn_in, grad_packed)
    grad_attn_in = dense_back(grad_packed, w_qkv)
    first_back = jax.vjp(layer_norm, stream_in, gain_attn)[1]
    grad_in_part, grad_gain_attn = first_back(grad_attn_in)
    grad_in = grad_mid + grad_in_part
    grad_in_low = grad_in.astype(jnp.bfloat16)
    grad_w_in = outer(noisy_low, grad_in_low)
    grad_seq = grad_in.reshape(seq_rows, half_len, model_width)
    grad_time = jnp.dot(bucket_hot.T, jnp.sum(grad_seq, axis=1), precision=lax.Precision.HIGHEST)
    pos_part = lax.dynamic_update_slice(
        jnp.zeros((full_len, model_width), jnp.float32),
        jnp.sum(grad_seq, axis=0),
        (position_start, jnp.zeros((), jnp.int32)),
    )
    grad_clean = signal * dense_back(grad_in_low, w_in) - grad_pred
    grad_rows = grad_clean * factor
    scale_part = jnp.sum(gathered * grad_clean)
    summed = lax.psum(
        (grad_w_in, grad_time, pos_part, grad_gain_attn, grad_gain_mlp, grad_head, scale_part),
        ("batch", "seq"),
    )
    grad_mean = -math.sqrt(embed_width) / (mean_norm * mean_norm) * summed[6]
    whole_qkv, whole_out = reduce_attn(grad_qkv, grad_out)
    whole_up, whole_down = reduce_mlp(grad_up, grad_down)
    full_grad = jnp.zeros((vocab_rows, embed_width), jnp.float32).at[flat_ids].add(grad_rows)
    grad_table = lax.psum_scatter(full_grad, ("batch", "seq"), scatter_dimension=0, tiled=True)
    grad_table = grad_table + grad_mean / vocab_rows * table_data / row_norms[:, None]
    return (
        output_low.reshape(seq_rows, half_len, model_width),
        grad_table,
        summed[0],
        summed[1],
        summed[2],
        summed[3],
        whole_qkv,
        whole_out,
        summed[4],
        whole_up,
        whole_down,
        summed[5],
        mean_norm,
    )


def solution(mesh):
    in_specs = (
        P("batch", "seq"),
        P("batch"),
        P("batch", "seq", None),
        P(("batch", "seq"), None),
        P(),
        P(),
        P(),
        P(),
        P(),
        P(),
        P(),
        P(),
        P(),
        P(),
    )
    out_specs = (
        P("batch", "seq", None),
        P(("batch", "seq"), None),
        P(),
        P(),
        P(),
        P(),
        P(),
        P(),
        P(),
        P(),
        P(),
        P(),
        P(),
    )
    return jax.shard_map(local, mesh=mesh, in_specs=in_specs, out_specs=out_specs, check_vma=False)
```

profile of v0, /device:TPU:0, one launch (start us, length us, event | category | flops | bytes accessed | tf_op | source)
XLA Modules:
  0.0 1755.8 jit_solution(10328966486713025821)
XLA Ops:
  10.7 48.9 %all_gather.9 = bf16[3840,128]{1,0:T(8,128)(2,1)} all-gather(bf16[120,128]{1,0:T(8,128)(2,1)} %param.25), channel_id=1, replica_groups=mesh['batch'=16,'seq'=2] {'batch','seq'}, dimensions={0}, use_global_device_ids=true | all-gather | bytes 1013760 | tf_op jit(solution)/shard_map/all_gather | solution.py:184
  66.3 37.1 %all-reduce.2 = (f32[]{:T(128)}, f32[8]{0:T(128)}) all-reduce(f32[]{:T(128)} %get-tuple-element.354, f32[8]{0:T(128)} %convert_reduce_fusion), channel_id=1, replica_groups=mesh['batch'=16,'seq'=2] {'batch','seq'}, use_global_device_ids=true, to_apply=%region_2.0 | all-reduce | flops 9 | bytes 72 | tf_op jit(solution)/shard_map/psum | solution.py:177
  104.1 9.8 gather_fusion
  126.8 9.8 convolution_convert_fusion
  136.7 21.3 %reshape.315 = bf16[4,512,3,768]{3,2,1,0:T(4,128)(2,1)} reshape(bf16[2048,2304]{1,0:T(8,128)(2,1)} %convolution_convert_fusion) | data formatting | bytes 18874368 | tf_op jit(solution)/shard_map/reshape | solution.py:206
  157.9 19.9 %copy.94 = bf16[4,512,3,768]{1,0,2,3:T(4,128)(2,1)} copy(bf16[4,512,3,768]{3,2,1,0:T(4,128)(2,1)} %reshape.315) | data formatting | bytes 18874368 | tf_op jit(solution)/shard_map/reshape | solution.py:206
  177.8 7.5 all-to-all-start
  185.3 8.2 all-to-all-done
  193.5 9.5 copy.95
  203.0 12.6 copy.96
  215.6 12.6 copy.97
  228.2 170.2 %while.50 = (s32[]{:T(128)}, bf16[4,1024,384]{1,2,0:T(8,128)(2,1)}, f32[4,6,1024]{2,1,0:T(8,128)}, bf16[4,1024,3,384]{1,3,2,0:T(8,128)(2,1)}, s32[]{:T(128)}, /*index=5*/s32[]{:T(128)}, s32[]{:T(128)}) while((s32[]{:T(128)}, bf16[4,1024,384]{1,2,0:T(8,128)(2,1)}, f32[4,6,1024]{2,1,0:T(8,128)}, bf16[4,1024,3,384]{1,3,2,0:T(8,128)(2,1)}, ...), condition=%wide.region_10.11_spmd, body=%wide.region_5.10_spmd.sunk | while | flops 833811456 | bytes 70373744 | solution.py:62
  237.7 23.5 %while.53 = (s32[]{:T(128)}, bf16[2,512,6,64]{1,3,2,0:T(8,128)(2,1)}, f32[2,6,512]{2,1,0:T(8,128)}, bf16[2,512,6,64]{1,3,2,0:T(8,128)(2,1)}, bf16[1024,3,6,64]{0,3,2,1:T(8,128)(2,1)}, /*index=5*/s32[]{:T(128)}) while((s32[]{:T(128)}, bf16[2,512,6,64]{1,3,2,0:T(8,128)(2,1)}, f32[2,6,512]{2,1,0:T(8,128)}, bf16[2,512,6,64]{1,3,2,0:T(8,128)(2,1)}, ...), condition=%wide.region_9.9_spmd, body=%wide.region_6.8_spmd.sunk | while | flops 833811456 | bytes 46715080 | solution.py:56
  280.3 23.5 %while.53 = (s32[]{:T(128)}, bf16[2,512,6,64]{1,3,2,0:T(8,128)(2,1)}, f32[2,6,512]{2,1,0:T(8,128)}, bf16[2,512,6,64]{1,3,2,0:T(8,128)(2,1)}, bf16[1024,3,6,64]{0,3,2,1:T(8,128)(2,1)}, /*index=5*/s32[]{:T(128)}) while((s32[]{:T(128)}, bf16[2,512,6,64]{1,3,2,0:T(8,128)(2,1)}, f32[2,6,512]{2,1,0:T(8,128)}, bf16[2,512,6,64]{1,3,2,0:T(8,128)(2,1)}, ...), condition=%wide.region_9.9_spmd, body=%wide.region_6.8_spmd.sunk | while | flops 833811456 | bytes 46715080 | solution.py:56
  322.8 23.5 %while.53 = (s32[]{:T(128)}, bf16[2,512,6,64]{1,3,2,0:T(8,128)(2,1)}, f32[2,6,512]{2,1,0:T(8,128)}, bf16[2,512,6,64]{1,3,2,0:T(8,128)(2,1)}, bf16[1024,3,6,64]{0,3,2,1:T(8,128)(2,1)}, /*index=5*/s32[]{:T(128)}) while((s32[]{:T(128)}, bf16[2,512,6,64]{1,3,2,0:T(8,128)(2,1)}, f32[2,6,512]{2,1,0:T(8,128)}, bf16[2,512,6,64]{1,3,2,0:T(8,128)(2,1)}, ...), condition=%wide.region_9.9_spmd, body=%wide.region_6.8_spmd.sunk | while | flops 833811456 | bytes 46715080 | solution.py:56
  365.3 23.5 %while.53 = (s32[]{:T(128)}, bf16[2,512,6,64]{1,3,2,0:T(8,128)(2,1)}, f32[2,6,512]{2,1,0:T(8,128)}, bf16[2,512,6,64]{1,3,2,0:T(8,128)(2,1)}, bf16[1024,3,6,64]{0,3,2,1:T(8,128)(2,1)}, /*index=5*/s32[]{:T(128)}) while((s32[]{:T(128)}, bf16[2,512,6,64]{1,3,2,0:T(8,128)(2,1)}, f32[2,6,512]{2,1,0:T(8,128)}, bf16[2,512,6,64]{1,3,2,0:T(8,128)(2,1)}, ...), condition=%wide.region_9.9_spmd, body=%wide.region_6.8_spmd.sunk | while | flops 833811456 | bytes 46715080 | solution.py:56
  419.3 6.5 fusion.90
  428.4 16.2 fusion.86
  444.6 22.7 %add_convert_fusion = bf16[2048,768]{1,0:T(8,128)(2,1)} fusion(f32[2048,768]{1,0:T(8,128)} %copy-done.13, bf16[3072,768]{1,0:T(8,128)(2,1)} %param.34, f32[2048,3072]{1,0:T(8,128)} %fusion.86), kind=kOutput, calls=%fused_computation.81 | convolution fusion | flops 9723445248 | bytes 39321600 | tf_op jit(solution)/shard_map/dot_general | solution.py:17
  474.7 32.6 %fusion.44 = bf16[2048,3072]{1,0:T(8,128)(2,1)} fusion(f32[2048,3072]{1,0:T(8,128)} %fusion.86, bf16[3072,768]{1,0:T(8,128)(2,1)} %param.34, f32[2048,768]{1,0:T(8,128)} %fusion.69), kind=kOutput, calls=%fused_computation.65 | convolution fusion | flops 9791078400 | bytes 48758784 | tf_op jit(solution)/shard_map/dot_general | solution.py:27
  507.2 18.5 %multiply_reduce_fusion.2 = (f32[768]{0:T(1024)}, f32[2048]{0:T(1024)S(1)}, f32[2048,768]{1,0:T(8,128)}) fusion(f32[2048,768]{1,0:T(8,128)} %copy-done.13, f32[2048]{0:T(1024)S(1)} %fusion.75, f32[2048]{0:T(1024)S(1)} %broadcast_multiply_fusion, f32[768]{0:T(1024)S(1)} %copy-done.56, bf16[2048,3072]{1,0:T(8,128)(2,1)} %fusion.44, bf16[768,3072]{1,0:T(8,128)(2,1)} %param.33), kind=kOutput, calls=%fused_computation.75 | convolution fusion | flops 9674683392 | bytes 29915136 | tf_op jit(solution)/shard_map/dot_general | solution.py:27
  525.7 7.5 fusion.87
  557.5 6.8 copy.101
  570.4 314.1 %while.52 = (s32[]{:T(128)}, bf16[4,1024,3,384]{1,3,2,0:T(8,128)(2,1)}, bf16[4,1024,3,384]{1,3,2,0:T(8,128)(2,1)}, bf16[4,1024,384]{1,2,0:T(8,128)(2,1)}, f32[4,...) while((s32[]{:T(128)}, bf16[4,1024,3,384]{1,3,2,0:T(8,128)(2,1)}, ...), condition=%wide.region_22.23_spmd, body=%wide.region_18.22_spmd.sunk | while | flops 2061038592 | bytes 179450544 | solution.py:239
  588.3 49.0 %while.54 = (s32[]{:T(128)}, f32[1024,6,64]{0,2,1:T(8,128)}, f32[1024,6,64]{0,2,1:T(8,128)}, bf16[2,512,6,64]{1,3,2,0:T(8,128)(2,1)}, bf16[2,512,6,64]{1,3,2,0:T...) while((s32[]{:T(128)}, f32[1024,6,64]{0,2,1:T(8,128)}, ...), condition=%wide.region_21.21_spmd.clone, body=%wide.region_19.20_spmd.clone.sunk | while | flops 2053174272 | bytes 149516752 | solution.py:112
  595.2 6.4 multiply_reduce_fusion.10
  601.6 6.6 multiply_convert_fusion.11
  626.1 6.6 multiply_convert_fusion.11
  666.7 49.0 %while.54 = (s32[]{:T(128)}, f32[1024,6,64]{0,2,1:T(8,128)}, f32[1024,6,64]{0,2,1:T(8,128)}, bf16[2,512,6,64]{1,3,2,0:T(8,128)(2,1)}, bf16[2,512,6,64]{1,3,2,0:T...) while((s32[]{:T(128)}, f32[1024,6,64]{0,2,1:T(8,128)}, ...), condition=%wide.region_21.21_spmd.clone, body=%wide.region_19.20_spmd.clone.sunk | while | flops 2053174272 | bytes 149516752 | solution.py:112
  680.0 6.6 multiply_convert_fusion.11
  704.5 6.6 multiply_convert_fusion.11
  745.1 49.0 %while.54 = (s32[]{:T(128)}, f32[1024,6,64]{0,2,1:T(8,128)}, f32[1024,6,64]{0,2,1:T(8,128)}, bf16[2,512,6,64]{1,3,2,0:T(8,128)(2,1)}, bf16[2,512,6,64]{1,3,2,0:T...) while((s32[]{:T(128)}, f32[1024,6,64]{0,2,1:T(8,128)}, ...), condition=%wide.region_21.21_spmd.clone, body=%wide.region_19.20_spmd.clone.sunk | while | flops 2053174272 | bytes 149516752 | solution.py:112
  758.4 6.6 multiply_convert_fusion.11
  782.9 6.6 multiply_convert_fusion.11
  823.5 49.0 %while.54 = (s32[]{:T(128)}, f32[1024,6,64]{0,2,1:T(8,128)}, f32[1024,6,64]{0,2,1:T(8,128)}, bf16[2,512,6,64]{1,3,2,0:T(8,128)(2,1)}, bf16[2,512,6,64]{1,3,2,0:T...) while((s32[]{:T(128)}, f32[1024,6,64]{0,2,1:T(8,128)}, ...), condition=%wide.region_21.21_spmd.clone, body=%wide.region_19.20_spmd.clone.sunk | while | flops 2053174272 | bytes 149516752 | solution.py:112
  830.4 6.4 multiply_reduce_fusion.10
  836.8 6.6 multiply_convert_fusion.11
  861.3 6.6 multiply_convert_fusion.11
  884.5 15.3 copy.103
  899.8 7.3 all-to-all-start.3
  907.2 7.8 fusion.53
  918.3 18.4 %copy.114 = bf16[4,2,512,3,384]{4,1,3,2,0:T(2,128)(2,1)} copy(bf16[4,2,512,3,384]{4,0,3,2,1:T(4,128)(2,1)} %bitcast.29) | data formatting | bytes 18874368 | tf_op jit(solution)/shard_map/all_to_all | solution.py:240
  936.7 20.8 %reshape.288 = bf16[2048,2304]{1,0:T(8,128)(2,1)} reshape(bf16[4,512,3,2,384]{4,3,2,1,0:T(2,128)(2,1)} %bitcast.221) | data formatting | bytes 18874368 | tf_op jit(solution)/shard_map/reshape | solution.py:242
  957.5 14.4 fusion.83
  971.9 7.9 reshape.290
  979.8 9.0 pad_maximum_fusion.1
  988.9 22.9 %fusion.56 = f32[3072,768]{1,0:T(8,128)} fusion(f32[2048,768]{1,0:T(8,128)} %fusion.69, f32[2048,3072]{1,0:T(8,128)} %fusion.86), kind=kOutput, calls=%fused_computation.100 | convolution fusion | flops 9721872384 | bytes 40894464 | tf_op jit(solution)/shard_map/dot_general | solution.py:21
  1011.8 11.0 reshape.295
  1022.9 18.1 %fusion.85 = f32[768,3072]{1,0:T(8,128)} fusion(bf16[2048,3072]{1,0:T(8,128)(2,1)} %fusion.44, f32[2048,768]{1,0:T(8,128)} %copy-done.13, f32[768]{0:T(1024)} %param.32, f32[2048]{0:T(1024)} %copy-done.47, f32[2048]{0:T(1024)S(1)} %copy-done.43), kind=kOutput, calls=%fused_computation.160 | convolution fusion | flops 9669967872 | bytes 28331008 | tf_op jit(solution)/shard_map/dot_general | solution.py:21
  1041.0 11.5 reshape.294
  1052.4 17.4 pad_maximum_fusion
  1069.9 13.3 multiply_reduce_fusion.4
  1099.5 12.2 scatter_custom_fusion
  1111.7 13.7 reduce-scatter.6.cloned.1.call-done
  1127.1 211.6 %reduce-scatter.8.cloned.1.call-done = f32[1152,128]{1,0:T(8,128)} async-done(((f32[36864,128]{1,0:T(8,128)}), f32[1152,128]{1,0:T(8,128)}) %reduce-scatter.8.cloned.1.call-update) | async-done | bytes 589840 | tf_op jit(solution)/shard_map/reduce_scatter | solution.py:128
  1359.3 40.5 %all-reduce.1 = (f32[]{:T(128)}, f32[8,768]{1,0:T(8,128)}, f32[768]{0:T(1024)}, f32[768]{0:T(1024)}) all-reduce(f32[]{:T(128)} %get-tuple-element.364, f32[8,768]{1,0:T(8,128)} %fusion.76, f32[768]{0:T(1024)S(1)} %get-tuple-element.281, f32[768]{0:T(1024)S(1)} %copy-done.55), channel_id=1, replica_groups=mesh['batch'=16,'seq'=2] {'batch','seq'}, use_global_device_ids=true, to_apply=%region_28.29 | all-reduce | flops 7681 | bytes 61448 | tf_op jit(solution)/shard_map/psum | solution.py:260
  1400.5 42.1 %reduce-scatter.10.cloned.1.call-done = f32[120,128]{1,0:T(8,128)} async-done(((f32[3840,128]{1,0:T(8,128)}), f32[120,128]{1,0:T(8,128)}) %reduce-scatter.10.cloned.1.call-update) | async-done | bytes 61456
  1444.2 64.3 %all-gather.3.cloned.1.call-done = bf16[18432,128]{1,0:T(8,128)(2,1)} async-done(((bf16[576,128]{1,0:T(8,128)(2,1)}), bf16[18432,128]{1,0:T(8,128)(2,1)}) %all-gather.3.cloned.1.call-update) | async-done | bytes 4718608 | tf_op jit(solution)/shard_map/all_gather | solution.py:139
  1519.3 8.3 reshape.292
  1527.6 65.5 %all-gather.5.cloned.1.call-done = bf16[36864,128]{1,0:T(8,128)(2,1)} async-done(((bf16[1152,128]{1,0:T(8,128)(2,1)}), bf16[36864,128]{1,0:T(8,128)(2,1)}) %all-gather.5.cloned.1.call-update) | async-done | bytes 9437200 | tf_op jit(solution)/shard_map/all_gather | solution.py:129
  1593.1 9.6 fusion.89
  1602.7 11.4 reshape.297
  1614.1 11.0 reshape.296
  1625.1 116.2 %all-reduce.6.cloned.1.call-done = (f32[128,768]{1,0:T(8,128)}, f32[1024,768]{1,0:T(8,128)}, f32[768,128]{1,0:T(8,128)}) async-done(((f32[128,768]{1,0:T(8,128)}, f32[1024,768]{1,0:T(8,128)}, f32[768,128]{1,0:T(8,128)}), (f32[128,768]{1,0:T(8,128)}, f32[1024,768]{1,0:T(8,128)}, f32[768,128]{1,0:T(8,128)})) %all-reduce.6.cloned.1.call-update) | async-done | bytes 3932176 | tf_op jit(solution)/shard_map/psum | solution.py:260
  (585 shorter events, 560.0 us)
Async XLA Ops:
  7.2 119.6 %copy-start = (bf16[768,2304]{1,0:T(8,128)(2,1)S(1)}, bf16[768,2304]{1,0:T(8,128)(2,1)}, u32[]{:S(2)}) copy-start(bf16[768,2304]{1,0:T(8,128)(2,1)} %param.30) | copy-start | bytes 10616836
  61.4 60.1 %copy-start.49 = (pred[2048]{0:T(1024)(128)(4,1)}, pred[2048]{0:T(1024)(128)(4,1)S(1)}, u32[]{:S(2)}) copy-start(pred[2048]{0:T(1024)(128)(4,1)S(1)} %compare_and_fusion) | copy-start | bytes 6148
  64.3 57.2 %copy-start.38 = (f32[4,768]{1,0:T(4,128)}, f32[4,768]{1,0:T(4,128)S(1)}, u32[]{:S(2)}) copy-start(f32[4,768]{1,0:T(4,128)S(1)} %fusion.77) | copy-start | bytes 36868
  115.3 7.7 copy-start.17
  177.8 15.7 all-to-all-start
  398.3 11.2 copy-start.60
  398.3 11.2 copy-start.58
  404.3 9.0 all-to-all-start.1
  413.3 6.0 copy-start.18
  413.3 6.0 copy-start.31
  413.3 6.0 copy-start.39
  419.2 6.6 copy-start.16
  425.8 99.9 %copy-start.42 = (f32[2048]{0:T(1024)}, f32[2048]{0:T(1024)S(1)}, u32[]{:S(2)}) copy-start(f32[2048]{0:T(1024)S(1)} %broadcast_multiply_fusion) | copy-start | bytes 24580
  428.4 97.3 %copy-start.47 = (f32[2048]{0:T(1024)}, f32[2048]{0:T(1024)S(1)}, u32[]{:S(2)}) copy-start(f32[2048]{0:T(1024)S(1)} %fusion.75) | copy-start | bytes 24580
  444.6 22.7 %copy-start.26 = (bf16[2048,128]{1,0:T(8,128)(2,1)S(1)}, bf16[2048,128]{1,0:T(8,128)(2,1)}, u32[]{:S(2)}) copy-start(bf16[2048,128]{1,0:T(8,128)(2,1)} %gather_fusion) | copy-start | bytes 1572868
  444.6 22.7 %copy-start.37 = (bf16[768,128]{1,0:T(8,128)(2,1)S(1)}, bf16[768,128]{1,0:T(8,128)(2,1)}, u32[]{:S(2)}) copy-start(bf16[768,128]{1,0:T(8,128)(2,1)} %param.35) | copy-start | bytes 589828
  444.6 22.7 %copy-start.50 = (pred[2048]{0:T(1024)(128)(4,1)S(1)}, pred[2048]{0:T(1024)(128)(4,1)}, u32[]{:S(2)}) copy-start(pred[2048]{0:T(1024)(128)(4,1)} %copy-done.49) | copy-start | bytes 6148
  525.7 8.7 copy-start.15
  548.6 9.0 all-to-all-start.2
  595.2 6.4 copy-start.5
  601.6 6.6 copy-start.1
  601.6 6.6 copy-start.19
  619.7 6.4 copy-start.5
  626.1 6.6 copy-start.1
  626.1 6.6 copy-start.19
  673.6 6.4 copy-start.5
  680.0 6.6 copy-start.1
  680.0 6.6 copy-start.19
  698.1 6.4 copy-start.5
  704.5 6.6 copy-start.1
  704.5 6.6 copy-start.19
  752.0 6.4 copy-start.5
  758.4 6.6 copy-start.1
  758.4 6.6 copy-start.19
  776.5 6.4 copy-start.5
  782.9 6.6 copy-start.1
  782.9 6.6 copy-start.19
  830.4 6.4 copy-start.5
  836.8 6.6 copy-start.1
  836.8 6.6 copy-start.19
  854.9 6.4 copy-start.5
  861.3 6.6 copy-start.1
  861.3 6.6 copy-start.19
  899.8 18.4 %all-to-all-start.3 = ((bf16[4,1024,3,384]{3,0,2,1:T(4,128)(2,1)}), bf16[4,1024,3,384]{3,0,2,1:T(4,128)(2,1)}, u32[]{:S(2)}, u32[]{:S(2)}) async-start(bf16[4,1024,3,384]{3,0,2,1:T(4,128)(2,1)} %copy.103), calls=%async_computation.3 | async-start | bytes 18874368 | tf_op jit(solution)/shard_map/all_to_all | solution.py:240
  907.2 218.3 %reduce-scatter.6.cloned.1.call-start = ((), (), s32[]{:S(2)}) async-start(), calls=%async_computation.7 | async-start | bytes 9732096 | tf_op jit(solution)/shard_map/reduce_scatter | solution.py:138
  936.7 20.8 %copy-start.41 = (f32[2048]{0:T(1024)S(1)}, f32[2048]{0:T(1024)}, u32[]{:S(2)}) copy-start(f32[2048]{0:T(1024)} %copy-done.40) | copy-start | bytes 24580
  936.7 20.8 %copy-start.53 = (f32[768]{0:T(1024)S(1)}, f32[768]{0:T(1024)}, u32[]{:S(2)}) copy-start(f32[768]{0:T(1024)} %param.29) | copy-start | bytes 9220
  988.9 349.9 %reduce-scatter.8.cloned.1.call-start = ((), (), s32[]{:S(2)}) async-start(), calls=%async_computation.9 | async-start | bytes 19464192 | tf_op jit(solution)/shard_map/reduce_scatter | solution.py:128
  1011.8 11.0 copy-start.43
  1069.8 13.4 copy-start.45
  1069.8 372.8 %reduce-scatter.10.cloned.1.call-start = ((), (), s32[]{:S(2)}) async-start(), calls=%async_computation.11 | async-start | bytes 2027520
  1069.9 13.3 copy-start.54
  1087.7 9.1 copy-start.24
  1087.7 9.1 copy-start.27
  1087.7 9.1 copy-start.35
  1087.7 9.1 copy-start.46
  1087.7 9.1 copy-start.51
  1111.7 396.8 %all-gather.3.cloned.1.call-start = ((), (), s32[]{:S(2)}) async-start(), calls=%async_computation.8 | async-start | bytes 4866048 | tf_op jit(solution)/shard_map/all_gather | solution.py:139
  1127.1 466.0 %all-gather.5.cloned.1.call-start = ((), (), s32[]{:S(2)}) async-start(), calls=%async_computation.10 | async-start | bytes 9732096 | tf_op jit(solution)/shard_map/all_gather | solution.py:129
  1340.6 400.7 %all-reduce.6.cloned.1.call-start = ((), (), s32[]{:S(2)}) async-start(), calls=%async_computation.12 | async-start | bytes 7864320 | tf_op jit(solution)/shard_map/psum | solution.py:260
  1345.2 7.0 copy-start.29
  1352.1 7.2 copy-start.55
  1352.1 90.5 %copy-start.57 = (f32[120]{0:T(128)S(1)}, f32[120]{0:T(128)}, u32[]{:S(2)}) copy-start(f32[120]{0:T(128)} %get-tuple-element.353) | copy-start | bytes 1444
  1741.3 5.6 copy-start.36
  (108 other events, 251.0 us)
Sparse Core Ops, SparseCore 0:
  989.0 136.4 reduce-scatter.5
  1133.0 205.7 reduce-scatter.7
  1345.4 97.1 reduce-scatter.9
  1445.8 62.6 all-gather.2
  1512.2 80.8 all-gather.4
  1601.1 140.1 all-reduce.5
where the time goes:
time: 1780 us; the launch traced here: 1760 us
  waiting for transfers between devices  529 us (30%)
  local copies, waits for them, and re-layouts  481 us (27%)
  matrix products  393 us (22%)
  other arithmetic  180 us (10%)
  blocking collectives  127 us (7%)
  starting transfers between devices  25.6 us (1%)
  between operations  18.6 us (1%)
    reduce_scatter x1, waiting for transfers between devices, reduce_mlp(): lax.psum_scatter(joined, ('batch', 'seq'), scatter_dimension=0, tiled=True)  212 us
    psum x1, waiting for transfers between devices, local(): lax.psum((grad_w_in, grad_time, pos_part, grad_gain_attn, grad_gain_mlp,...  116 us
    dot_general x6, matrix products, dense_back(): lax.dot_general(left, right, (((1,), (1,)), ((), ())), preferred_element_...  74.7 us
    dot_general x6, matrix products, outer(): lax.dot_general(left, right, (((0,), (0,)), ((), ())), preferred_element_...  69.3 us
    all_gather x1, waiting for transfers between devices, reduce_mlp(): lax.all_gather(shared.astype(jnp.bfloat16), ('batch', 'seq'), axis=0, til...  65.5 us
    all_gather x1, waiting for transfers between devices, reduce_attn(): lax.all_gather(shared.astype(jnp.bfloat16), ('batch', 'seq'), axis=0, til...  64.3 us
    dot_general x6, matrix products, dense(): return jnp.dot(left, right, preferred_element_type=jnp.float32)  60.1 us
    convert_element_type x8, other arithmetic, advance(): grad_scores = (prob_block * (grad_probs - inner)).astype(jnp.bfloat16)  52.6 us
  transfers between devices with their start and end apart: 10, of which 9 were waited for; matrix products, arithmetic and copies ran while one was open for 12% of the time, Pallas kernels for 0%

commit v1 on v0

v1 whole, which is shorter than its diff:
```python
import functools
import math

import jax
import jax.numpy as jnp
from jax import lax
from jax.experimental import pallas as pl
from jax.experimental.pallas import tpu as pltpu
from jax.sharding import PartitionSpec as P

HEAD = 64
BF = jnp.bfloat16
F32 = jnp.float32
NN = (((1,), (0,)), ((), ()))
NT = (((1,), (1,)), ((), ()))
VMEM_BYTES = 60 * 2**20
GELU_A = math.sqrt(2 / math.pi)
GELU_B = 0.044715


def dot(left, right, dims=NN):
    return lax.dot_general(left, right, dims, preferred_element_type=F32)


def params():
    return pltpu.CompilerParams(vmem_limit_bytes=VMEM_BYTES)


def cost(flops, moved, trans=0):
    return pl.CostEstimate(flops=int(flops), bytes_accessed=int(moved), transcendentals=int(trans))


def whole(shape):
    return pl.BlockSpec(shape, lambda *_: (0,) * len(shape), pipeline_mode=pl.Buffered(1))


def smem():
    return pl.BlockSpec(memory_space=pltpu.SMEM)


def normalise(hidden):
    centre = hidden - jnp.mean(hidden, axis=-1, keepdims=True)
    inv = lax.rsqrt(jnp.mean(centre * centre, axis=-1, keepdims=True) + 1e-05)
    return centre * inv, inv


def norm_back(hidden, gain, grad):
    unit, inv = normalise(hidden)
    scaled = grad * gain
    part = inv * (
        scaled
        - jnp.mean(scaled, axis=-1, keepdims=True)
        - unit * jnp.mean(scaled * unit, axis=-1, keepdims=True)
    )
    return part, jnp.sum(grad * unit, axis=0, keepdims=True)


def turned(block):
    return block.astype(F32).T.astype(BF)


def accumulate(ref, first, value):
    @pl.when(first)
    def _():
        ref[...] = value

    @pl.when(jnp.logical_not(first))
    def _():
        ref[...] += value


def embed_kernel(
    scal, ids_ref, table_ref, noise_ref, win_ref, time_ref, pos_ref, gain_ref, wqkv_ref,
    word_ref, noisy_ref, stream_ref, attn_ref, packed_ref, *, tiles, hot,
):
    seq = pl.program_id(0) // tiles
    if hot:
        ids = ids_ref[...]
        rows = table_ref.shape[0]
        step = 1024
        word = None
        for start in range(0, rows, step):
            lane = lax.broadcasted_iota(jnp.int32, (ids.shape[0], step), 1) + start
            one = jnp.where(ids == lane, 1.0, 0.0).astype(BF)
            part = dot(one, table_ref[start : start + step, :])
            word = part if word is None else word + part
        word_ref[...] = word.astype(BF)
    else:
        word = table_ref[...].astype(F32)
        word_ref[...] = table_ref[...]
    clean = word * scal[0, 3]
    noisy = (scal[seq, 0] * clean + scal[seq, 1] * noise_ref[...].astype(F32)).astype(BF)
    noisy_ref[...] = noisy
    stream = dot(noisy, win_ref[...]) + time_ref[pl.ds(seq, 1), :] + pos_ref[...]
    stream_ref[...] = stream
    attn = (normalise(stream)[0] * gain_ref[...]).astype(BF)
    attn_ref[...] = turned(attn)
    packed_ref[...] = dot(attn, wqkv_ref[...]).astype(BF)


def embed(scal, ids, table, noise, w_in, time_rows, pos_table, gain, w_qkv, hot, tm=256):
    tokens, width = noise.shape
    length, model = pos_table.shape
    tiles = length // tm
    wide = w_qkv.shape[1]
    row = lambda cols: pl.BlockSpec((tm, cols), lambda i: (i, 0))
    return pl.pallas_call(
        functools.partial(embed_kernel, tiles=tiles, hot=hot),
        grid=(tokens // tm,),
        in_specs=[
            smem(), pl.BlockSpec((tm, 1), lambda i: (i, 0)),
            whole(table.shape) if hot else row(width), row(width), whole(w_in.shape),
            whole(time_rows.shape), pl.BlockSpec((tm, model), lambda i: (i % tiles, 0)),
            whole(gain.shape), whole(w_qkv.shape),
        ],
        out_specs=[
            row(width), row(width), row(model), pl.BlockSpec((model, tm), lambda i: (0, i)), row(wide),
        ],
        out_shape=[
            jax.ShapeDtypeStruct((tokens, width), BF),
            jax.ShapeDtypeStruct((tokens, width), BF),
            jax.ShapeDtypeStruct((tokens, model), F32),
            jax.ShapeDtypeStruct((model, tokens), BF),
            jax.ShapeDtypeStruct((tokens, wide), BF),
        ],
        compiler_params=params(),
        cost_estimate=cost(2 * tokens * model * (wide + width), 30e6),
        name="embed",
    )(scal, ids, table, noise, w_in, time_rows, pos_table, gain, w_qkv)


def attend_kernel(q_ref, k_ref, v_ref, mixed_ref, probs_ref, inv_ref, *, tq):
    length = q_ref.shape[0]
    lane = lax.broadcasted_iota(jnp.int32, (1, 2 * HEAD), 1)
    keys = k_ref[...]
    values = jnp.concatenate([v_ref[...], jnp.ones_like(v_ref[...])], axis=1)
    scale = math.log2(math.e) * HEAD**-0.5
    for start in range(0, length, tq):
        rows = slice(start, start + tq)
        query = q_ref[rows, :]
        parts = []
        for head in range(2):
            own = jnp.where(lane // HEAD == head, query, jnp.zeros_like(query))
            scores = dot(own, keys, NT)
            peak = jnp.max(scores, axis=1, keepdims=True)
            raised = jnp.exp2(scores * scale - peak * scale).astype(BF)
            probs_ref[head, rows, :] = raised
            sums = dot(raised, values)
            inv = 1.0 / sums[:, 2 * HEAD :]
            parts.append((sums[:, : 2 * HEAD] * inv, inv))
        low = lane < HEAD
        mixed_ref[rows, :] = jnp.where(low, parts[0][0], parts[1][0]).astype(BF)
        inv_ref[rows, :] = jnp.where(low, parts[0][1], parts[1][1])


def attend(packed, length, tq=256):
    tokens = packed.shape[0]
    seqs, pairs = tokens // length, packed.shape[1] // (6 * HEAD)
    spec = lambda part: pl.BlockSpec((length, 2 * HEAD), lambda s, j: (s, part * pairs + j))
    return pl.pallas_call(
        functools.partial(attend_kernel, tq=tq),
        grid=(seqs, pairs),
        in_specs=[spec(0), spec(1), spec(2)],
        out_specs=[
            spec(0), pl.BlockSpec((2, length, length), lambda s, j: (s * pairs + j, 0, 0)), spec(0),
        ],
        out_shape=[
            jax.ShapeDtypeStruct((tokens, pairs * 2 * HEAD), BF),
            jax.ShapeDtypeStruct((seqs * pairs * 2, length, length), BF),
            jax.ShapeDtypeStruct((tokens, pairs * 2 * HEAD), F32),
        ],
        compiler_params=params(),
        cost_estimate=cost(16 * seqs * pairs * length * length * 2 * HEAD, 80e6, 25e6),
        name="attend",
    )(packed, packed, packed)


def attend_back_kernel(
    q_ref, k_ref, v_ref, grad_ref, mixed_ref, inv_ref, probs_ref, dq_ref, dk_ref, dv_ref, *, tq
):
    length = q_ref.shape[0]
    lane = lax.broadcasted_iota(jnp.int32, (1, 2 * HEAD), 1)
    keys, values = k_ref[...], v_ref[...]
    scale = HEAD**-0.5
    held = [None] * (length // tq)
    key_parts, value_parts = [], []
    for head in range(2):
        mask = lane // HEAD == head
        grad_k, grad_v = None, None
        cut = slice(head * HEAD, (head + 1) * HEAD)
        for tile in range(length // tq):
            rows = slice(tile * tq, (tile + 1) * tq)
            grad = grad_ref[rows, :]
            inv = inv_ref[rows, :]
            wide = grad.astype(F32)
            inner = jnp.sum(
                jnp.where(mask, wide * mixed_ref[rows, :].astype(F32), 0.0), axis=1, keepdims=True
            )
            grad_probs = dot(jnp.where(mask, grad, jnp.zeros_like(grad)), values, NT)
            raised = probs_ref[head, rows, :]
            grad_scores = (raised.astype(F32) * (grad_probs - inner)).astype(BF)
            grad_q = dot(grad_scores, keys) * (inv * scale)
            if head == 0:
                held[tile] = grad_q
            else:
                dq_ref[rows, :] = jnp.where(lane < HEAD, held[tile], grad_q).astype(BF)
            query = (q_ref[rows, :].astype(F32) * (inv * scale)).T[cut, :].astype(BF)
            outer = (wide * inv).T[cut, :].astype(BF)
            part_k, part_v = dot(query, grad_scores), dot(outer, raised)
            grad_k = part_k if grad_k is None else grad_k + part_k
            grad_v = part_v if grad_v is None else grad_v + part_v
        key_parts.append(grad_k)
        value_parts.append(grad_v)
    dk_ref[...] = jnp.concatenate(key_parts, axis=0).T.astype(BF)
    dv_ref[...] = jnp.concatenate(value_parts, axis=0).T.astype(BF)


def attend_back(packed, grad_mixed, mixed, inv, probs, length, tq=256):
    tokens = packed.shape[0]
    seqs, pairs = tokens // length, packed.shape[1] // (6 * HEAD)
    spec = lambda part: pl.BlockSpec((length, 2 * HEAD), lambda s, j: (s, part * pairs + j))
    return pl.pallas_call(
        functools.partial(attend_back_kernel, tq=tq),
        grid=(seqs, pairs),
        in_specs=[
            spec(0), spec(1), spec(2), spec(0), spec(0), spec(0),
            pl.BlockSpec((2, length, length), lambda s, j: (s * pairs + j, 0, 0)),
        ],
        out_specs=[spec(0)] * 3,
        out_shape=[jax.ShapeDtypeStruct((tokens, pairs * 2 * HEAD), BF)] * 3,
        compiler_params=params(),
        cost_estimate=cost(32 * seqs * pairs * length * length * 2 * HEAD, 80e6),
        name="attend_back",
    )(packed, packed, packed, grad_mixed, mixed, inv, probs)


def forward_kernel(
    scal, mixed_ref, stream_ref, word_ref, wout_ref, gain_ref, wup_ref, wdown_ref, whead_ref,
    mid_ref, mlp_ref, act_ref, slope_ref, out_ref, gpred_ref, branch_ref, turned_ref, mixed_t_ref,
    ghead_ref,
    *, tiles, step,
):
    index = pl.program_id(0)
    seq = index // tiles
    mid = stream_ref[...] + dot(mixed_ref[...], wout_ref[...])
    mid_ref[...] = mid
    mlp = (normalise(mid)[0] * gain_ref[...]).astype(BF)
    mlp_ref[...] = turned(mlp)
    mixed_t_ref[...] = turned(mixed_ref[...])
    total = mid
    for start in range(0, wup_ref.shape[1], step):
        cols = slice(start, start + step)
        up = dot(mlp, wup_ref[:, cols])
        square = up * up
        bent = jnp.tanh(up * (GELU_A + GELU_A * GELU_B * square))
        half = 0.5 * up
        act = (half + half * bent).astype(BF)
        act_ref[:, cols] = act
        slope = (0.5 + 0.5 * bent) + half * (1.0 - bent * bent) * (
            GELU_A + 3.0 * GELU_A * GELU_B * square
        )
        slope_ref[:, cols] = slope.astype(BF)
        total = total + dot(act, wdown_ref[cols, :])
    low = total.astype(BF)
    out_ref[...] = low
    clean = word_ref[...].astype(F32) * scal[0, 3]
    gpred = (dot(low, whead_ref[...]) - clean) * scal[seq, 2]
    gpred_ref[...] = gpred
    gpred_low = gpred.astype(BF)
    branch = dot(gpred_low, whead_ref[...], NT)
    branch_ref[...] = branch.astype(BF)
    turned_ref[...] = branch.T.astype(BF)
    accumulate(ghead_ref, index == 0, dot(gpred.T.astype(BF), low))


def forward(scal, mixed, stream, word, w_out, gain, w_up, w_down, w_head, length, tm=256, step=768):
    tokens, model = mixed.shape
    inner, width = w_up.shape[1], w_head.shape[1]
    row = lambda cols: pl.BlockSpec((tm, cols), lambda i: (i, 0))
    shape = lambda cols, kind: jax.ShapeDtypeStruct((tokens, cols), kind)
    flip = pl.BlockSpec((model, tm), lambda i: (0, i))
    flipped = jax.ShapeDtypeStruct((model, tokens), BF)
    return pl.pallas_call(
        functools.partial(forward_kernel, tiles=length // tm, step=step),
        grid=(tokens // tm,),
        in_specs=[
            smem(), row(model), row(model), row(width), whole(w_out.shape), whole(gain.shape),
            whole(w_up.shape), whole(w_down.shape), whole(w_head.shape),
        ],
        out_specs=[
            row(model), flip, row(inner), row(inner), row(model), row(width), row(model), flip, flip,
            pl.BlockSpec((width, model), lambda i: (0, 0)),
        ],
        out_shape=[
            shape(model, F32), flipped, shape(inner, BF), shape(inner, BF),
            shape(model, BF), shape(width, F32), shape(model, BF), flipped, flipped,
            jax.ShapeDtypeStruct((width, model), F32),
        ],
        compiler_params=params(),
        cost_estimate=cost(2 * tokens * model * (model + 2 * inner + 3 * width), 60e6),
        name="feed_forward",
    )(scal, mixed, stream, word, w_out, gain, w_up, w_down, w_head)


def back_kernel(
    mid_ref, slope_ref, gpred_ref, branch_ref, wout_ref, gain_ref, wup_ref, wdown_ref, whead_ref,
    upin_ref, gmid_ref, gattn_ref, gmixed_ref, ggain_ref, *, step,
):
    index = pl.program_id(0)
    branch = branch_ref[...]
    grad = None
    for start in range(0, wup_ref.shape[1], step):
        cols = slice(start, start + step)
        upin = (dot(branch, wdown_ref[cols, :], NT) * slope_ref[:, cols].astype(F32)).astype(BF)
        upin_ref[:, cols] = upin
        part = dot(upin, wup_ref[:, cols], NT)
        grad = part if grad is None else grad + part
    part, gain_part = norm_back(mid_ref[...], gain_ref[...], grad)
    accumulate(ggain_ref, index == 0, gain_part)
    gmid = dot(gpred_ref[...].astype(BF), whead_ref[...], NT) + part
    gmid_ref[...] = gmid
    low = gmid.astype(BF)
    gattn_ref[...] = low
    gmixed_ref[...] = dot(low, wout_ref[...], NT).astype(BF)


def back(mid, slope, gpred, branch, w_out, gain, w_up, w_down, w_head, tm=256, step=768):
    tokens, model = mid.shape
    inner, width = w_up.shape[1], w_head.shape[1]
    row = lambda cols: pl.BlockSpec((tm, cols), lambda i: (i, 0))
    shape = lambda cols, kind: jax.ShapeDtypeStruct((tokens, cols), kind)
    return pl.pallas_call(
        functools.partial(back_kernel, step=step),
        grid=(tokens // tm,),
        in_specs=[
            row(model), row(inner), row(width), row(model), whole(w_out.shape), whole(gain.shape),
            whole(w_up.shape), whole(w_down.shape), whole(w_head.shape),
        ],
        out_specs=[
            row(inner), row(model), row(model), row(model),
            pl.BlockSpec((1, model), lambda i: (0, 0)),
        ],
        out_shape=[
            shape(inner, BF), shape(model, F32), shape(model, BF), shape(model, BF),
            jax.ShapeDtypeStruct((1, model), F32),
        ],
        compiler_params=params(),
        cost_estimate=cost(2 * tokens * model * (model + 2 * inner + width), 60e6),
        name="feed_forward_back",
    )(mid, slope, gpred, branch, w_out, gain, w_up, w_down, w_head)


def input_back_kernel(
    scal, gmid_ref, dq_ref, dk_ref, dv_ref, stream_ref, noisy_ref, word_ref, gpred_ref, gain_ref,
    wqkv_ref, win_ref, gpos_ref, gtime_ref, ggain_ref, gwin_ref, grows_ref, gscale_ref,
):
    tile, seq = pl.program_id(0), pl.program_id(1)
    first = jnp.logical_and(tile == 0, seq == 0)
    model = win_ref.shape[1]
    grad = (
        dot(dq_ref[...], wqkv_ref[:, :model], NT)
        + dot(dk_ref[...], wqkv_ref[:, model : 2 * model], NT)
        + dot(dv_ref[...], wqkv_ref[:, 2 * model :], NT)
    )
    part, gain_part = norm_back(stream_ref[...], gain_ref[...], grad)
    accumulate(ggain_ref, first, gain_part)
    gin = gmid_ref[...] + part
    accumulate(gpos_ref, seq == 0, gin)
    sums = jnp.sum(gin, axis=0, keepdims=True)
    @pl.when(tile == 0)
    def _():
        gtime_ref[pl.ds(seq, 1), :] = sums

    @pl.when(tile > 0)
    def _():
        gtime_ref[pl.ds(seq, 1), :] += sums

    low = gin.astype(BF)
    accumulate(gwin_ref, first, dot(noisy_ref[...].astype(F32).T.astype(BF), low))
    gclean = scal[seq, 0] * dot(low, win_ref[...], NT) - gpred_ref[...]
    grows_ref[...] = (gclean * scal[0, 3]).astype(BF)
    accumulate(
        gscale_ref, first, jnp.sum(word_ref[...].astype(F32) * gclean, axis=0, keepdims=True)
    )


def input_back(scal, gmid, dq, dk, dv, stream, noisy, word, gpred, gain, w_qkv, w_in, length, tm=256):
    tokens, model = gmid.shape
    width = w_in.shape[0]
    seqs, tiles = tokens // length, length // tm
    row = lambda cols: pl.BlockSpec((tm, cols), lambda i, s: (s * tiles + i, 0))
    fixed = lambda rows, cols: pl.BlockSpec((rows, cols), lambda i, s: (0, 0))
    return pl.pallas_call(
        input_back_kernel,
        grid=(tiles, seqs),
        in_specs=[
            smem(), row(model), row(model), row(model), row(model), row(model), row(width),
            row(width), row(width), whole(gain.shape), whole(w_qkv.shape), whole(w_in.shape),
        ],
        out_specs=[
            pl.BlockSpec((tm, model), lambda i, s: (i, 0)), fixed(seqs, model), fixed(1, model),
            fixed(width, model), row(width), fixed(1, width),
        ],
        out_shape=[
            jax.ShapeDtypeStruct((length, model), F32),
            jax.ShapeDtypeStruct((seqs, model), F32),
            jax.ShapeDtypeStruct((1, model), F32),
            jax.ShapeDtypeStruct((width, model), F32),
            jax.ShapeDtypeStruct((tokens, width), BF),
            jax.ShapeDtypeStruct((1, width), F32),
        ],
        compiler_params=params(),
        cost_estimate=cost(2 * tokens * model * (3 * model + 2 * width), 30e6),
        name="input_back",
    )(scal, gmid, dq, dk, dv, stream, noisy, word, gpred, gain, w_qkv, w_in)


def rows_kernel(ids_ref, grows_ref, out_ref, *, tv):
    start = pl.program_id(0) * tv
    row = lax.broadcasted_iota(jnp.int32, (tv, ids_ref.shape[1]), 0) + start
    one = jnp.where(row == ids_ref[...], 1.0, 0.0).astype(BF)
    out_ref[...] = dot(one, grows_ref[...])


def table_rows(ids, grows, rows, tv=512):
    tokens, width = grows.shape
    return pl.pallas_call(
        functools.partial(rows_kernel, tv=tv),
        grid=(rows // tv,),
        in_specs=[whole((1, tokens)), whole(grows.shape)],
        out_specs=pl.BlockSpec((tv, width), lambda i: (i, 0)),
        out_shape=jax.ShapeDtypeStruct((rows, width), F32),
        compiler_params=params(),
        cost_estimate=cost(4 * tokens * rows * width, 3e6),
        name="table_rows",
    )(ids, grows)


def bit_orders(batch):
    bits = list(range(batch.bit_length() - 1))
    other = bits[1::-1] + bits[2:] if len(bits) > 1 else bits
    return bits, other


def place(owner, me, order):
    apart = jnp.bitwise_xor(owner, me)
    spot = 0
    for bit in order:
        spot = spot * 2 + jnp.bitwise_and(lax.shift_right_logical(apart, bit), 1)
    return spot


def outer_kernel(where, left_ref, right_ref, out_ref, *, tw, orders, send, row_blocks):
    me, core = where[0], where[1]
    half = 1 - core if send else core
    chunks, rows, cols = out_ref.shape
    col_blocks = chunks // row_blocks
    step = pl.program_id(0)
    acc = dot(left_ref[...], right_ref[...])
    per = cols // tw
    block = step // per
    offset = pl.multiple_of((step % per) * tw, 128)
    for index in range(row_blocks):
        owner = index * col_blocks + block
        spot = jnp.where(half == 0, place(owner, me, orders[0]), place(owner, me, orders[1]))
        out_ref[spot, :, pl.ds(offset, tw)] = acc[index * rows : (index + 1) * rows, :].astype(
            out_ref.dtype
        )


def chunk_shape(batch, rows, cols):
    row_blocks = min(batch, 16 if batch <= 16 else 32)
    return row_blocks, rows // row_blocks, cols * row_blocks // batch


def outer(where, left, right, batch, send, tw=768):
    rows, tokens = left.shape
    half_cols = right.shape[1] // 2
    row_blocks, chunk_rows, chunk_cols = chunk_shape(batch, rows, half_cols)
    tw = min(tw, chunk_cols)
    steps = half_cols // tw
    pick = (lambda i, w: (0, (1 - w[1]) * steps + i)) if send else (lambda i, w: (0, w[1] * steps + i))
    return pl.pallas_call(
        functools.partial(
            outer_kernel, tw=tw, orders=bit_orders(batch), send=send, row_blocks=row_blocks
        ),
        grid_spec=pltpu.PrefetchScalarGridSpec(
            num_scalar_prefetch=1,
            grid=(steps,),
            in_specs=[whole(left.shape), pl.BlockSpec((tokens, tw), pick)],
            out_specs=pl.BlockSpec((batch, chunk_rows, chunk_cols), lambda i, w: (0, 0, 0)),
        ),
        out_shape=jax.ShapeDtypeStruct((batch, chunk_rows, chunk_cols), BF if send else F32),
        compiler_params=params(),
        cost_estimate=cost(2 * tokens * rows * half_cols, 14e6),
        name="weight_grad_send" if send else "weight_grad_keep",
    )(where, left, right)


def outer_attn_kernel(where, attn_ref, mixed_ref, *refs, orders, row_blocks):
    rights, keep_ref, send_ref = refs[:4], refs[4], refs[5]
    me, core = where[0], where[1]
    chunks, rows, cols = keep_ref.shape
    col_blocks = chunks // row_blocks
    model = attn_ref.shape[0]
    tw = min(cols, model)
    for part in range(4):
        half = part // 2
        left_ref = mixed_ref if part == 3 else attn_ref
        for start in range(0, model, tw):
            acc = dot(left_ref[...], rights[part][:, start : start + tw])
            place_at = (part % 2) * model + start
            block, offset = place_at // cols, place_at % cols

            def write(ref):
                for index in range(row_blocks):
                    spot = place(index * col_blocks + block, me, orders[half])
                    ref[spot, :, offset : offset + tw] = acc[
                        index * rows : (index + 1) * rows, :
                    ].astype(ref.dtype)

            @pl.when(core == half)
            def _():
                write(keep_ref)

            @pl.when(core != half)
            def _():
                write(send_ref)


def outer_attn(where, attn, mixed, dq, dk, dv, gattn, batch):
    model, tokens = attn.shape
    row_blocks, chunk_rows, chunk_cols = chunk_shape(batch, model, 2 * model)
    shape = (batch, chunk_rows, chunk_cols)
    return pl.pallas_call(
        functools.partial(outer_attn_kernel, orders=bit_orders(batch), row_blocks=row_blocks),
        grid_spec=pltpu.PrefetchScalarGridSpec(
            num_scalar_prefetch=1,
            grid=(1,),
            in_specs=[whole(attn.shape)] * 2 + [whole(dq.shape)] * 4,
            out_specs=[whole(shape)] * 2,
        ),
        out_shape=[jax.ShapeDtypeStruct(shape, F32), jax.ShapeDtypeStruct(shape, BF)],
        compiler_params=params(),
        cost_estimate=cost(8 * tokens * model * model, 30e6),
        name="attn_weight_grad",
    )(where, attn, mixed, dq, dk, dv, gattn)


def swap(array):
    return lax.ppermute(array, "seq", [(0, 1), (1, 0)])


def hop(array, step):
    batch = lax.axis_size("batch")
    orders = bit_orders(batch)
    pairs = [
        (2 * me + core, 2 * (me ^ (1 << orders[core][step])) + core)
        for me in range(batch)
        for core in range(2)
    ]
    return lax.ppermute(array, ("batch", "seq"), pairs)


def reduce_chunks(keep, send):
    got = swap(send)
    for step in range(lax.axis_size("batch").bit_length() - 1):
        count = keep.shape[0] // 2
        low = (keep[count:] + got[count:].astype(F32)).astype(BF)
        keep = keep[:count] + got[:count].astype(F32)
        got = hop(low, step)
    return keep[0] + got[0].astype(F32)


def share(chunk):
    return lax.all_gather(chunk.astype(BF), ("batch", "seq"), axis=0)


def spread_kernel(in_ref, out_ref, *, flip):
    row_blocks, _, _, rows, cols = in_ref.shape
    whole_rows = in_ref[...].reshape(row_blocks * rows, cols).astype(F32)
    out_ref[...] = whole_rows.T if flip else whole_rows


def spread(gathered, batch, rows, cols, first=0, last=None, flip=False, tw=256):
    last = cols if last is None else last
    row_blocks, chunk_rows, chunk_cols = chunk_shape(batch, rows, cols // 2)
    view = gathered.reshape(row_blocks, batch // row_blocks, 2, chunk_rows, chunk_cols)
    per = chunk_cols // tw if chunk_cols % tw == 0 else 0
    if not per:
        tw = 128
        per = chunk_cols // tw
    half = cols // 2 // tw

    def pick(i):
        at = i + first // tw
        return (0, (at % half) // per, at // half, 0, at % per)

    shape = (last - first, rows) if flip else (rows, last - first)
    return pl.pallas_call(
        functools.partial(spread_kernel, flip=flip),
        grid=((last - first) // tw,),
        in_specs=[pl.BlockSpec((row_blocks, 1, 1, chunk_rows, tw), pick)],
        out_specs=pl.BlockSpec((tw, rows), lambda i: (i, 0))
        if flip
        else pl.BlockSpec((rows, tw), lambda i: (0, i)),
        out_shape=jax.ShapeDtypeStruct(shape, F32),
        compiler_params=params(),
        cost_estimate=cost(0, 6 * rows * (last - first)),
        name="spread",
    )(view)


def small_plan(rows, devices):
    each = -(-sum(rows) // devices // 16) * 16
    plan = [[] for _ in range(devices)]
    start = 0
    for source, count in enumerate(rows):
        done = 0
        while done < count:
            chunk, at = divmod(start + done, each)
            size = min(count - done, each - at)
            plan[chunk].append((source, done, at, size))
            done += size
        start += count
    return each, plan


def pack_kernel(where, *refs, each, plan, orders, span):
    sources, table_ref, keep_ref, send_ref = refs[:-3], refs[-3], refs[-2], refs[-1]
    me, core = where[0], where[1]
    batch = keep_ref.shape[0]
    panels = sources[0].shape[1] // 128
    for chunk, pieces in enumerate(plan):
        half, owner = divmod(chunk, batch)
        spot = place(owner, me, orders[half])

        def write(ref):
            for panel in range(panels):
                base = panel * each
                filled = 0
                for source, first, at, size in pieces:
                    ref[spot, base + at : base + at + size, :] = sources[source][
                        first : first + size, panel * 128 : (panel + 1) * 128
                    ].astype(ref.dtype)
                    filled = at + size
                if filled < each:
                    ref[spot, base + filled : base + each, :] = jnp.zeros(
                        (each - filled, 128), ref.dtype
                    )
            at = (owner * 2 + half) * span
            ref[spot, panels * each :, :] = table_ref[at : at + span, :].astype(ref.dtype)

        @pl.when(core == half)
        def _():
            write(keep_ref)

        @pl.when(core != half)
        def _():
            write(send_ref)


def pack(where, sources, table, batch):
    devices = 2 * batch
    each, plan = small_plan([source.shape[0] for source in sources], devices)
    span = table.shape[0] // devices
    shape = (batch, each * (sources[0].shape[1] // 128) + span, 128)
    return pl.pallas_call(
        functools.partial(pack_kernel, each=each, plan=plan, orders=bit_orders(batch), span=span),
        grid_spec=pltpu.PrefetchScalarGridSpec(
            num_scalar_prefetch=1,
            grid=(1,),
            in_specs=[whole(source.shape) for source in sources] + [whole(table.shape)],
            out_specs=[whole(shape)] * 2,
        ),
        out_shape=[jax.ShapeDtypeStruct(shape, F32), jax.ShapeDtypeStruct(shape, BF)],
        compiler_params=params(),
        cost_estimate=cost(0, 15e6),
        name="pack_small",
    )(where, *sources, table)


def unpack_kernel(in_ref, *outs, each, plan, batch):
    panels = outs[0].shape[1] // 128
    for chunk, pieces in enumerate(plan):
        half, owner = divmod(chunk, batch)
        for panel in range(panels):
            for source, first, at, size in pieces:
                base = panel * each + at
                outs[source][first : first + size, panel * 128 : (panel + 1) * 128] = in_ref[
                    owner * 2 + half, base : base + size, :
                ].astype(F32)


def unpack(gathered, shapes):
    devices = gathered.shape[0]
    each, plan = small_plan([shape[0] for shape in shapes], devices)
    return pl.pallas_call(
        functools.partial(unpack_kernel, each=each, plan=plan, batch=devices // 2),
        grid=(1,),
        in_specs=[whole(gathered.shape)],
        out_specs=[whole(shape) for shape in shapes],
        out_shape=[jax.ShapeDtypeStruct(shape, F32) for shape in shapes],
        compiler_params=params(),
        cost_estimate=cost(0, 8e6),
        name="unpack_small",
    )(gathered)


def local(
    word_ids, buckets, noise, table, w_in, time_table, pos_table, gain_attn, w_qkv, w_out,
    gain_mlp, w_up, w_down, w_head,
):
    seq_rows, half_len = word_ids.shape
    table_span, embed_width = table.shape
    model = w_qkv.shape[0]
    bucket_count = time_table.shape[0]
    batch, cores = lax.axis_size("batch"), lax.axis_size("seq")
    devices = batch * cores
    vocab = table_span * devices
    length = half_len * cores
    seqs = seq_rows // cores
    tokens = seqs * length
    me = lax.axis_index("batch").astype(jnp.int32)
    core = lax.axis_index("seq").astype(jnp.int32)
    where = jnp.stack([me, core])

    def regroup(array):
        own = lax.dynamic_slice_in_dim(array, core * seqs, seqs, 0)
        other = swap(lax.dynamic_slice_in_dim(array, (1 - core) * seqs, seqs, 0))
        return jnp.concatenate(
            [jnp.where(core == 0, own, other), jnp.where(core == 0, other, own)], axis=1
        )

    bucket_hot = (buckets[:, None] == jnp.arange(bucket_count, dtype=jnp.int32)[None, :]).astype(F32)
    span = -(-(table_span + 1) // 16) * 16
    extra = jnp.zeros((span - table_span, embed_width), BF)
    extra = lax.dynamic_update_slice(extra, jnp.sum(bucket_hot, axis=0).astype(BF)[None, :], (0, 0))
    gathered = lax.all_gather(
        jnp.concatenate([table, extra], axis=0), ("batch", "seq"), axis=0
    )
    ids = regroup(word_ids).reshape(tokens, 1)
    ids = (ids // table_span) * span + ids % table_span
    noise_rows = regroup(noise).reshape(tokens, embed_width)
    counts = jnp.sum(gathered[:, table_span, :bucket_count].astype(F32), axis=0) / cores
    body = gathered[:, :table_span, :].astype(F32)
    mean_norm = jnp.sum(jnp.sqrt(jnp.sum(body * body, axis=2) + 1e-06)) / vocab
    factor = math.sqrt(embed_width) / mean_norm

    own_buckets = lax.dynamic_slice_in_dim(buckets, core * seqs, seqs, 0)
    own_hot = (own_buckets[:, None] == jnp.arange(bucket_count, dtype=jnp.int32)[None, :]).astype(F32)
    angles = math.pi / 2 * (own_buckets.astype(F32) + 1.0) / (bucket_count + 1)
    weight = 1.0 / jnp.sum(own_hot * counts[None, :], axis=1)
    scal = jnp.stack(
        [jnp.cos(angles), jnp.sin(angles), weight, jnp.broadcast_to(factor, (seqs,))], axis=1
    )
    time_rows = jnp.dot(own_hot, time_table, precision=lax.Precision.HIGHEST)

    flat_table = gathered.reshape(devices * span, embed_width)
    hot = devices * span <= 8192
    words = flat_table if hot else jnp.take(flat_table, ids[:, 0], axis=0)
    gain_a, gain_m = gain_attn.reshape(1, model), gain_mlp.reshape(1, model)
    word, noisy, stream, attn_t, packed = embed(
        scal, ids, words, noise_rows, w_in, time_rows, pos_table, gain_a, w_qkv, hot
    )
    mixed, probs, inv = attend(packed, length)
    mid, mlp_t, act, slope, low, gpred, branch, branch_t, mixed_t, ghead = forward(
        scal, mixed, stream, word, w_out, gain_m, w_up, w_down, w_head, length
    )
    down_send = outer(where, branch_t, act, batch, True)
    down_keep = outer(where, branch_t, act, batch, False)
    upin, gmid, gattn, gmixed, ggain_m = back(
        mid, slope, gpred, branch, w_out, gain_m, w_up, w_down, w_head
    )
    up_send = outer(where, mlp_t, upin, batch, True)
    up_keep = outer(where, mlp_t, upin, batch, False)
    dq, dk, dv = attend_back(packed, gmixed, mixed, inv, probs, length)
    attn_keep, attn_send = outer_attn(where, attn_t, mixed_t, dq, dk, dv, gattn, batch)
    gpos, gtime, ggain_a, gwin, grows, gscale = input_back(
        scal, gmid, dq, dk, dv, stream, noisy, word, gpred, gain_a, w_qkv, w_in, length
    )
    rows = table_rows(ids.reshape(1, tokens), grows, devices * span)

    down_all = share(reduce_chunks(down_keep, down_send))
    up_all = share(reduce_chunks(up_keep, up_send))
    attn_all = share(reduce_chunks(attn_keep, attn_send))
    grad_time = jnp.dot(own_hot.T, gtime, precision=lax.Precision.HIGHEST)
    extras = jnp.concatenate(
        [
            grad_time, ggain_a, ggain_m,
            jnp.pad(jnp.sum(gscale).reshape(1, 1), ((0, 0), (0, model - 1))),
            jnp.zeros((16 - bucket_count - 3, model), F32),
        ],
        axis=0,
    )
    small = [gpos, gwin, ghead, extras]
    keep, send = pack(where, small, rows, batch)
    mine = reduce_chunks(keep, send)
    cut = mine.shape[0] - span
    pos_sum, win_sum, head_sum, extra_sum = unpack(share(mine[:cut]), [a.shape for a in small])

    table_data = table.astype(F32)
    own_norms = jnp.sqrt(jnp.sum(table_data * table_data, axis=1, keepdims=True) + 1e-06)
    grad_mean = -math.sqrt(embed_width) / (mean_norm * mean_norm) * extra_sum[bucket_count + 2, 0]
    grad_table = mine[cut : cut + table_span] + grad_mean / vocab * table_data / own_norms

    low = low.reshape(seqs, length, model)
    own = lax.dynamic_slice_in_dim(low, core * half_len, half_len, 1)
    other = swap(lax.dynamic_slice_in_dim(low, (1 - core) * half_len, half_len, 1))
    output = jnp.concatenate(
        [jnp.where(core == 0, own, other), jnp.where(core == 0, other, own)], axis=0
    )
    inner = w_up.shape[1]
    return (
        output,
        grad_table,
        win_sum,
        extra_sum[:bucket_count],
        pos_sum,
        extra_sum[bucket_count],
        spread(attn_all, batch, model, 4 * model, 0, 3 * model),
        spread(attn_all, batch, model, 4 * model, 3 * model, 4 * model),
        extra_sum[bucket_count + 1],
        spread(up_all, batch, model, inner),
        spread(down_all, batch, model, inner, flip=True),
        head_sum.T,
        mean_norm,
    )


def solution(mesh):
    rows = P(("batch", "seq"), None)
    in_specs = (P("batch", "seq"), P("batch"), P("batch", "seq", None), rows) + (P(),) * 10
    out_specs = (P("batch", "seq", None), rows) + (P(),) * 11
    return jax.shard_map(local, mesh=mesh, in_specs=in_specs, out_specs=out_specs, check_vma=False)
```

time: 1780 us -> 675 us (0.38); the launches traced: 1760 us -> 670 us
  local copies, waits for them, and re-layouts: 481 us -> 16.2 us
  matrix products: 393 us -> 1.75 us
  Pallas kernels: 0 us -> 341 us
  waiting for transfers between devices: 529 us -> 241 us
  other arithmetic: 180 us -> 36.1 us
  blocking collectives: 127 us -> 0 us
    dot_general x76 -> x2, matrix products: 393 us -> 1.75 us  [the longest x1 0.96 us: local(): grad_time = jnp.dot(own_hot.T, gtime, precision=lax.Precision.HIGHEST)]
    pallas_call x0 -> x18, Pallas kernels: none -> 341 us  [the longest x1 52.6 us: attend_back(): pl.pallas_call(functools.partial(attend_back_kernel, tq=tq), grid=(seqs,...]
    reduce_scatter x2 -> x0, waiting for transfers between devices: 225 us -> none  [the longest x1 212 us: reduce_mlp(): lax.psum_scatter(joined, ('batch', 'seq'), scatter_dimension=0, tiled=True)]
    ppermute x0 -> x23, waiting for transfers between devices: none -> 174 us  [the longest x16 168 us: hop(): return lax.ppermute(array, ('batch', 'seq'), pairs)]
    reshape x16 -> x2, local copies, waits for them, and re-layouts: 149 us -> 2.53 us  [local(): gain_a, gain_m = (gain_attn.reshape(1, model), gain_mlp.reshape(1, model))]
    psum x1 -> x0, waiting for transfers between devices: 116 us -> none  [local(): lax.psum((grad_w_in, grad_time, pos_part, grad_gain_attn, grad_gain_mlp,...]
    while x251 -> x0, local copies, waits for them, and re-layouts: 97.5 us -> none
    psum x2 -> x0, blocking collectives: 77.6 us -> none  [the longest x1 40.5 us: local(): lax.psum((grad_w_in, grad_time, pos_part, grad_gain_attn, grad_gain_mlp,...]
  transfers between devices with their start and end apart: 10 -> 28, of which waited for: 9 -> 19; matrix products, arithmetic and copies ran while one was open for 12% -> 6% of each run, Pallas kernels for 0% -> 14%
where the time goes in v1:
time: 675 us; the launch traced here: 670 us
  Pallas kernels  341 us (51%)
  waiting for transfers between devices  241 us (36%)
  other arithmetic  36.1 us (5%)
  between operations  18.1 us (3%)
  local copies, waits for them, and re-layouts  16.2 us (2%)
  starting transfers between devices  16.1 us (2%)
    ppermute x16, waiting for transfers between devices, hop(): return lax.ppermute(array, ('batch', 'seq'), pairs)  168 us
    pallas_call x1, Pallas kernels, attend_back(): pl.pallas_call(functools.partial(attend_back_kernel, tq=tq), grid=(seqs,...  52.6 us
    pallas_call x1, Pallas kernels, forward(): pl.pallas_call(functools.partial(forward_kernel, tiles=length // tm, step...  46.8 us
    all_gather x1, waiting for transfers between devices, local(): lax.all_gather(jnp.concatenate([table, extra], axis=0), ('batch', 'seq'),...  46.4 us
    pallas_call x4, Pallas kernels, outer(): pl.pallas_call(functools.partial(outer_kernel, tw=tw, orders=bit_orders(b...  42.3 us
    pallas_call x1, Pallas kernels, attend(): pl.pallas_call(functools.partial(attend_kernel, tq=tq), grid=(seqs, pairs...  41.5 us
    pallas_call x1, Pallas kernels, back(): pl.pallas_call(functools.partial(back_kernel, step=step), grid=(tokens //...  37.9 us
    pallas_call x4, Pallas kernels, spread(): pl.pallas_call(functools.partial(spread_kernel, flip=flip), grid=((last -...  30.7 us
  transfers between devices with their start and end apart: 28, of which 19 were waited for; matrix products, arithmetic and copies ran while one was open for 6% of the time, Pallas kernels for 14%

profile of v1, /device:TPU:0, one launch (start us, length us, event | category | flops | bytes accessed | tf_op | source)
XLA Modules:
  0.0 670.1 jit_solution(6458190282751145425)
XLA Ops:
  10.2 1.4 fusion.28
  14.1 1.3 reshape.255.gain_ref
  15.4 1.3 reshape.256.gain_ref
  18.7 1.5 fusion.6.ids_ref
  21.7 46.4 %all-gather.15.cloned.1.call-done.table_ref = bf16[4096,128]{1,0:T(8,128)(2,1)} async-done(((bf16[128,128]{1,0:T(8,128)(2,1)}), bf16[4096,128]{1,0:T(8,128)(2,1)}) %all-gather.15.cloned.1.call-update) | async-done | bytes 1048592 | tf_op jit(solution)/shard_map/all_gather | solution.py:739
  69.0 1.8 multiply_reduce_fusion
  73.2 23.9 %embed.1 = (bf16[2048,128]{1,0:T(8,128)(2,1)}, bf16[2048,128]{1,0:T(8,128)(2,1)}, f32[2048,768]{1,0:T(8,128)}, bf16[768,2048]{1,0:T(8,128)(2,1)}, bf16[2048,2304]{1,0:T(8,128)(2,1)}) custom-call(f32[2,4]{1,0:T(2,128)} %maximum_maximum_fusion.scal, s32[2048,1]{1,0:T(8,128)} %fusion.6.ids_ref, bf16[4096,128]{1,0:T(8,128)(2,1)} %all-gather.15.cloned.1.call-done.table_ref, ...), custom_call_target="tpu_custom_call" | custom-call | flops 7650410496 | bytes 30000000 | tf_op jit(solution)/shard_map/embed/pallas_call | solution.py:107
  97.1 41.5 %attend.1 = (bf16[2048,768]{1,0:T(8,128)(2,1)}, bf16[24,1024,1024]{2,1,0:T(8,128)(2,1)}, f32[2048,768]{1,0:T(8,128)}) custom-call(bf16[2048,2304]{1,0:T(8,128)(2,1)} %get-tuple-element.53.q_ref.k_ref.v_ref, bf16[2048,2304]{1,0:T(8,128)(2,1)} %get-tuple-element.53.q_ref.k_ref.v_ref, bf16[2048,2304]{1,0:T(8,128)(2,1)} %get-tuple-element.53.q_ref.k_ref.v_ref), custom_call_target="tpu_custom_call" | custom-call | flops 25769803776 | bytes 80000000 | tf_op jit(solution)/shard_map/attend/pallas_call | solution.py:160
  138.5 46.8 %feed_forward.1 = (f32[2048,768]{1,0:T(8,128)}, bf16[768,2048]{1,0:T(8,128)(2,1)}, bf16[2048,3072]{1,0:T(8,128)(2,1)}, bf16[2048,3072]{1,0:T(8,128)(2,1)}, bf16[...) custom-call(f32[2,4]{1,0:T(2,128)} %maximum_maximum_fusion.scal, ...), custom_call_target="tpu_custom_call" | custom-call | flops 22951231488 | bytes 60000000 | tf_op jit(solution)/shard_map/feed_forward/pallas_call | solution.py:283
  185.3 37.9 %feed_forward_back.1 = (bf16[2048,3072]{1,0:T(8,128)(2,1)}, f32[2048,768]{1,0:T(8,128)}, bf16[2048,768]{1,0:T(8,128)(2,1)}, bf16[2048,768]{1,0:T(8,128)(2,1)}, f32[1,768]{1,0:T(1,128)}) custom-call(f32[2048,768]{1,0:T(8,128)} %get-tuple-element.58.mid_ref, bf16[2048,3072]{1,0:T(8,128)(2,1)} %get-tuple-element.59.slope_ref, ...), custom_call_target="tpu_custom_call" | custom-call | flops 22145925120 | bytes 60000000 | tf_op jit(solution)/shard_map/feed_forward_back/pallas_call | solution.py:332
  223.3 52.6 %attend_back.1 = (bf16[2048,768]{1,0:T(8,128)(2,1)}, bf16[2048,768]{1,0:T(8,128)(2,1)}, bf16[2048,768]{1,0:T(8,128)(2,1)}) custom-call(bf16[2048,2304]{1,0:T(8,128)(2,1)} %get-tuple-element.53.q_ref.k_ref.v_ref, bf16[2048,2304]{1,0:T(8,128)(2,1)} %get-tuple-element.53.q_ref.k_ref.v_ref, bf16[2048,2304]{1,0:T(8,128)(2,1)} %get-tuple-element.53.q_ref.k_ref.v_ref, ...), custom_call_target="tpu_custom_call" | custom-call | flops 51539607552 | bytes 80000000 | tf_op jit(solution)/shard_map/attend_back/pallas_call | solution.py:222
  275.8 23.3 %input_back.1 = (f32[1024,768]{1,0:T(8,128)}, f32[2,768]{1,0:T(2,128)}, f32[1,768]{1,0:T(1,128)}, f32[128,768]{1,0:T(8,128)}, bf16[2048,128]{1,0:T(8,128)(2,1)}, /*index=5*/f32[1,128]{1,0:T(1,128)}) custom-call(f32[2,4]{1,0:T(2,128)} %maximum_maximum_fusion.scal, f32[2048,768]{1,0:T(8,128)} %get-tuple-element.62.gmid_ref, ...), custom_call_target="tpu_custom_call" | custom-call | flops 8053063680 | bytes 30000000 | tf_op jit(solution)/shard_map/input_back/pallas_call | solution.py:393
  300.1 1.3 reduce_sum.68
  302.1 7.5 %table_rows.1.refs_4_ = f32[4096,128]{1,0:T(8,128)} custom-call(s32[1,2048]{1,0:T(1,128)} %fusion.30.ids_ref, bf16[2048,128]{1,0:T(8,128)(2,1)} %get-tuple-element.77.grows_ref), custom_call_target="tpu_custom_call" | custom-call | flops 4294967296 | bytes 3000000 | tf_op jit(solution)/shard_map/table_rows/pallas_call | solution.py:427
  309.6 1.2 concatenate.19.refs_3_
  310.9 7.0 %pack_small.1 = (f32[16,416,128]{2,1,0:T(8,128)}, bf16[16,416,128]{2,1,0:T(8,128)(2,1)}) custom-call(s32[2]{0:T(128)} %pad_add_fusion.1.where, f32[1024,768]{1,0:T(8,128)} %get-tuple-element.70.refs_0_, f32[128,768]{1,0:T(8,128)} %get-tuple-element.71.refs_1_, f32[128,768]{1,0:T(8,128)} %get-tuple-element.72.refs_2_, f32[16,768]{1,0:T(8,128)} %concatenate.19.refs_3_, ...), custom_call_target="tpu_custom_call" | custom-call | bytes 15000000 | tf_op jit(solution)/shard_map/pack_small/pallas_call | solution.py:668
  318.1 3.5 collective-permute-done.3
  321.6 3.2 add_convert_fusion.1
  324.9 1.3 collective-permute-start.4
  326.1 24.1 %attn_weight_grad.1 = (f32[16,48,1536]{2,1,0:T(8,128)}, bf16[16,48,1536]{2,1,0:T(8,128)(2,1)}) custom-call(s32[2]{0:T(128)} %pad_add_fusion.1.where, bf16[768,2048]{1,0:T(8,128)(2,1)} %get-tuple-element.83.attn_ref, bf16[768,2048]{1,0:T(8,128)(2,1)} %get-tuple-element.84.mixed_ref, bf16[2048,768]{1,0:T(8,128)(2,1)} %get-tuple-element.66.dq_ref.refs_0_, ...), custom_call_target="tpu_custom_call" | custom-call | flops 9663676416 | bytes 30000000 | tf_op jit(solution)/shard_map/attn_weight_grad/pallas_call | solution.py:535
  350.5 1.3 fusion.8
  352.6 7.4 %collective-permute-done.5 = bf16[4,416,128]{2,1,0:T(8,128)(2,1)S(1)} collective-permute-done((bf16[4,416,128]{2,1,0:T(8,128)(2,1)S(1)}, bf16[4,416,128]{2,1,0:T(8,128)(2,1)S(1)}, u32[]{:S(2)}, u32[]{:S(2)}) %collective-permute-start.5) | collective-permute-done | bytes 426016 | tf_op jit(solution)/shard_map/ppermute | solution.py:562
  360.9 5.9 collective-permute-done.6
  366.8 1.4 collective-permute-start.7
  368.2 5.4 collective-permute-done.7
  375.1 3.1 add_convert_fusion
  379.0 16.4 %collective-permute-done.9 = bf16[8,48,1536]{2,1,0:T(8,128)(2,1)S(1)} collective-permute-done((bf16[8,48,1536]{2,1,0:T(8,128)(2,1)S(1)}, bf16[8,48,1536]{2,1,0:T(8,128)(2,1)S(1)}, u32[]{:S(2)}, u32[]{:S(2)}) %collective-permute-start.9) | collective-permute-done | bytes 1179680 | tf_op jit(solution)/shard_map/ppermute | solution.py:562
  396.6 10.2 %collective-permute-done.10 = bf16[4,48,1536]{2,1,0:T(8,128)(2,1)S(1)} collective-permute-done((bf16[4,48,1536]{2,1,0:T(8,128)(2,1)S(1)}, bf16[4,48,1536]{2,1,0:T(8,128)(2,1)S(1)}, u32[]{:S(2)}, u32[]{:S(2)}) %collective-permute-start.10) | collective-permute-done | bytes 589856 | tf_op jit(solution)/shard_map/ppermute | solution.py:562
  407.0 8.4 %collective-permute-done.11 = bf16[2,48,1536]{2,1,0:T(8,128)(2,1)S(1)} collective-permute-done((bf16[2,48,1536]{2,1,0:T(8,128)(2,1)S(1)}, bf16[2,48,1536]{2,1,0:T(8,128)(2,1)S(1)}, u32[]{:S(2)}, u32[]{:S(2)}) %collective-permute-start.11) | collective-permute-done | bytes 294944 | tf_op jit(solution)/shard_map/ppermute | solution.py:562
  416.3 9.8 %collective-permute-done.12 = bf16[1,48,1536]{2,1,0:T(8,128)(2,1)S(1)} collective-permute-done((bf16[1,48,1536]{2,1,0:T(8,128)(2,1)S(1)}, bf16[1,48,1536]{2,1,0:T(8,128)(2,1)S(1)}, u32[]{:S(2)}, u32[]{:S(2)}) %collective-permute-start.12) | collective-permute-done | bytes 147488 | tf_op jit(solution)/shard_map/ppermute | solution.py:562
  427.1 10.2 %weight_grad_send.3 = bf16[16,48,1536]{2,1,0:T(8,128)(2,1)} custom-call(s32[2]{0:T(128)} %pad_add_fusion.1.where, bf16[768,2048]{1,0:T(8,128)(2,1)} %get-tuple-element.90.left_ref, bf16[2048,3072]{1,0:T(8,128)(2,1)} %get-tuple-element.91.right_ref), custom_call_target="tpu_custom_call" | custom-call | flops 4831838208 | bytes 14000000 | tf_op jit(solution)/shard_map/weight_grad_send/pallas_call | solution.py:483
  437.3 10.9 %weight_grad_keep.3 = f32[16,48,1536]{2,1,0:T(8,128)} custom-call(s32[2]{0:T(128)} %pad_add_fusion.1.where, bf16[768,2048]{1,0:T(8,128)(2,1)} %get-tuple-element.90.left_ref, bf16[2048,3072]{1,0:T(8,128)(2,1)} %get-tuple-element.91.right_ref), custom_call_target="tpu_custom_call" | custom-call | flops 4831838208 | bytes 14000000 | tf_op jit(solution)/shard_map/weight_grad_keep/pallas_call | solution.py:483
  448.3 3.1 fusion
  451.3 1.2 collective-permute-start.19
  452.6 19.3 %collective-permute-done.19 = bf16[8,48,1536]{2,1,0:T(8,128)(2,1)S(1)} collective-permute-done((bf16[8,48,1536]{2,1,0:T(8,128)(2,1)S(1)}, bf16[8,48,1536]{2,1,0:T(8,128)(2,1)S(1)}, u32[]{:S(2)}, u32[]{:S(2)}) %collective-permute-start.19) | collective-permute-done | bytes 1179680 | tf_op jit(solution)/shard_map/ppermute | solution.py:562
  472.2 1.4 collective-permute-start.20
  473.6 10.0 %collective-permute-done.20 = bf16[4,48,1536]{2,1,0:T(8,128)(2,1)S(1)} collective-permute-done((bf16[4,48,1536]{2,1,0:T(8,128)(2,1)S(1)}, bf16[4,48,1536]{2,1,0:T(8,128)(2,1)S(1)}, u32[]{:S(2)}, u32[]{:S(2)}) %collective-permute-start.20) | collective-permute-done | bytes 589856 | tf_op jit(solution)/shard_map/ppermute | solution.py:562
  483.8 16.9 %collective-permute-done.21 = bf16[2,48,1536]{2,1,0:T(8,128)(2,1)S(1)} collective-permute-done((bf16[2,48,1536]{2,1,0:T(8,128)(2,1)S(1)}, bf16[2,48,1536]{2,1,0:T(8,128)(2,1)S(1)}, u32[]{:S(2)}, u32[]{:S(2)}) %collective-permute-start.21) | collective-permute-done | bytes 294944 | tf_op jit(solution)/shard_map/ppermute | solution.py:562
  500.8 7.1 %collective-permute-done.22 = bf16[1,48,1536]{2,1,0:T(8,128)(2,1)S(1)} collective-permute-done((bf16[1,48,1536]{2,1,0:T(8,128)(2,1)S(1)}, bf16[1,48,1536]{2,1,0:T(8,128)(2,1)S(1)}, u32[]{:S(2)}, u32[]{:S(2)}) %collective-permute-start.22) | collective-permute-done | bytes 147488 | tf_op jit(solution)/shard_map/ppermute | solution.py:562
  508.7 10.2 %weight_grad_send.2 = bf16[16,48,1536]{2,1,0:T(8,128)(2,1)} custom-call(s32[2]{0:T(128)} %pad_add_fusion.1.where, bf16[768,2048]{1,0:T(8,128)(2,1)} %get-tuple-element.88.left_ref, bf16[2048,3072]{1,0:T(8,128)(2,1)} %get-tuple-element.89.right_ref), custom_call_target="tpu_custom_call" | custom-call | flops 4831838208 | bytes 14000000 | tf_op jit(solution)/shard_map/weight_grad_send/pallas_call | solution.py:483
  518.9 10.9 %weight_grad_keep.2 = f32[16,48,1536]{2,1,0:T(8,128)} custom-call(s32[2]{0:T(128)} %pad_add_fusion.1.where, bf16[768,2048]{1,0:T(8,128)(2,1)} %get-tuple-element.88.left_ref, bf16[2048,3072]{1,0:T(8,128)(2,1)} %get-tuple-element.89.right_ref), custom_call_target="tpu_custom_call" | custom-call | flops 4831838208 | bytes 14000000 | tf_op jit(solution)/shard_map/weight_grad_keep/pallas_call | solution.py:483
  529.9 3.1 fusion.1
  533.6 17.9 %collective-permute-done.14 = bf16[8,48,1536]{2,1,0:T(8,128)(2,1)S(1)} collective-permute-done((bf16[8,48,1536]{2,1,0:T(8,128)(2,1)S(1)}, bf16[8,48,1536]{2,1,0:T(8,128)(2,1)S(1)}, u32[]{:S(2)}, u32[]{:S(2)}) %collective-permute-start.14) | collective-permute-done | bytes 1179680 | tf_op jit(solution)/shard_map/ppermute | solution.py:562
  551.9 1.5 collective-permute-start.15
  553.5 15.8 %collective-permute-done.15 = bf16[4,48,1536]{2,1,0:T(8,128)(2,1)S(1)} collective-permute-done((bf16[4,48,1536]{2,1,0:T(8,128)(2,1)S(1)}, bf16[4,48,1536]{2,1,0:T(8,128)(2,1)S(1)}, u32[]{:S(2)}, u32[]{:S(2)}) %collective-permute-start.15) | collective-permute-done | bytes 589856 | tf_op jit(solution)/shard_map/ppermute | solution.py:562
  569.4 1.5 collective-permute-start.16
  570.9 9.6 %collective-permute-done.16 = bf16[2,48,1536]{2,1,0:T(8,128)(2,1)S(1)} collective-permute-done((bf16[2,48,1536]{2,1,0:T(8,128)(2,1)S(1)}, bf16[2,48,1536]{2,1,0:T(8,128)(2,1)S(1)}, u32[]{:S(2)}, u32[]{:S(2)}) %collective-permute-start.16) | collective-permute-done | bytes 294944 | tf_op jit(solution)/shard_map/ppermute | solution.py:562
  580.6 1.3 collective-permute-start.17
  581.9 7.8 %collective-permute-done.17 = bf16[1,48,1536]{2,1,0:T(8,128)(2,1)S(1)} collective-permute-done((bf16[1,48,1536]{2,1,0:T(8,128)(2,1)S(1)}, bf16[1,48,1536]{2,1,0:T(8,128)(2,1)S(1)}, u32[]{:S(2)}, u32[]{:S(2)}) %collective-permute-start.17) | collective-permute-done | bytes 147488 | tf_op jit(solution)/shard_map/ppermute | solution.py:562
  590.4 1.3 constant_dynamic-slice_fusion
  593.1 2.3 collective-permute-done.2
  595.4 2.0 broadcast_select_fusion.1
  597.5 1.9 pad_maximum_fusion
  599.4 3.7 unpack_small.1
  603.1 1.2 slice.242
  604.3 1.3 slice.243
  605.6 1.9 copy.63
  608.2 1.4 slice_reduce_fusion
  609.6 1.5 fusion.26
  611.2 7.6 %spread.4 = f32[768,2304]{1,0:T(8,128)} custom-call(bf16[16,1,2,48,1536]{4,3,2,1,0:T(8,128)(2,1)} %bitcast.64), custom_call_target="tpu_custom_call" | custom-call | bytes 10616832 | tf_op jit(solution)/shard_map/spread/pallas_call | solution.py:600
  618.7 3.4 spread.5
  622.1 10.2 %spread.7 = f32[3072,768]{1,0:T(8,128)} custom-call(bf16[16,1,2,48,1536]{4,3,2,1,0:T(8,128)(2,1)} %bitcast.66), custom_call_target="tpu_custom_call" | custom-call | bytes 14155776 | tf_op jit(solution)/shard_map/spread/pallas_call | solution.py:600
  632.4 20.4 %all-gather.11.cloned.1.call-done = bf16[32,48,1536]{2,1,0:T(8,128)(2,1)} async-done(((bf16[1,48,1536]{2,1,0:T(8,128)(2,1)}), bf16[32,48,1536]{2,1,0:T(8,128)(2,1)}) %all-gather.11.cloned.1.call-update) | async-done | bytes 4718608 | tf_op jit(solution)/shard_map/all_gather | solution.py:576
  652.8 9.5 %spread.6 = f32[768,3072]{1,0:T(8,128)} custom-call(bf16[16,1,2,48,1536]{4,3,2,1,0:T(8,128)(2,1)} %bitcast.67), custom_call_target="tpu_custom_call" | custom-call | bytes 14155776 | tf_op jit(solution)/shard_map/spread/pallas_call | solution.py:600
  (101 shorter events, 24.4 us)
Async XLA Ops:
  7.2 5.3 copy-start
  7.2 61.0 %all-gather.15.cloned.1.call-start = ((), (), s32[]{:S(2)}) async-start(), calls=%async_computation.4 | async-start | bytes 1081344 | tf_op jit(solution)/shard_map/all_gather | solution.py:739
  8.0 8.7 %collective-permute-start = (s32[2,512]{1,0:T(2,128)S(1)}, s32[2,512]{1,0:T(2,128)S(1)}, u32[]{:S(2)}, u32[]{:S(2)}) collective-permute-start(s32[2,512]{1,0:T(2,128)S(1)} %constant_dynamic-slice_fusion.2), channel_id=1, source_target_pairs={{0,1},{1,0},{2,3},{3,2},{4,5},{5,4},{6,7},{7,6},{8,9},{9,8},{10,11... | collective-permute-start | bytes 12296 | tf_op jit(solution)/shard_map/ppermute | solution.py:551
  9.4 11.5 %collective-permute-start.1 = (bf16[2,512,128]{2,1,0:T(8,128)(2,1)S(1)}, bf16[2,512,128]{2,1,0:T(8,128)(2,1)S(1)}, u32[]{:S(2)}, u32[]{:S(2)}) collective-permute-start(bf16[2,512,128]{2,1,0:T(8,128)(2,1)S(1)} %constant_dynamic-slice_fusion.1), channel_id=1, source_target_pairs={{0,1},{1,0},{2,3},{3,2},{4,5},{5,4},{6,7},{7,6},{8,9},{9,8},{10,11... | collective-permute-start | bytes 786440 | tf_op jit(solution)/shard_map/ppermute | solution.py:551
  11.6 587.8 %all-gather.7.cloned.1.call-start = ((), (), s32[]{:S(2)}) async-start(), calls=%async_computation | async-start | bytes 2433024 | tf_op jit(solution)/shard_map/all_gather | solution.py:576
  17.8 3.0 copy-start.4
  302.0 7.6 %copy-start.6 = (f32[1,768]{1,0:T(1,128)S(1)}, f32[1,768]{1,0:T(1,128)}, u32[]{:S(2)}) copy-start(f32[1,768]{1,0:T(1,128)} %get-tuple-element.75) | copy-start | bytes 9220
  302.1 7.6 %copy-start.7 = (f32[1,768]{1,0:T(1,128)S(1)}, f32[1,768]{1,0:T(1,128)}, u32[]{:S(2)}) copy-start(f32[1,768]{1,0:T(1,128)} %get-tuple-element.74) | copy-start | bytes 9220
  317.8 3.8 collective-permute-start.3
  324.9 25.6 %collective-permute-start.4 = (bf16[8,416,128]{2,1,0:T(8,128)(2,1)}, bf16[8,416,128]{2,1,0:T(8,128)(2,1)}, u32[]{:S(2)}, u32[]{:S(2)}) collective-permute-start(bf16[8,416,128]{2,1,0:T(8,128)(2,1)} %get-tuple-element.155), channel_id=1, source_target_pairs={{0,2},{1,5},{2,0},{3,7},{4,6},{5,1},{6,4},{7,3},{8,10},{9,13},{10,... | collective-permute-start | bytes 2555912 | tf_op jit(solution)/shard_map/ppermute | solution.py:562
  350.3 24.8 %collective-permute-start.8 = (bf16[16,48,1536]{2,1,0:T(8,128)(2,1)}, bf16[16,48,1536]{2,1,0:T(8,128)(2,1)S(1)}, u32[]{:S(2)}, u32[]{:S(2)}) collective-permute-start(bf16[16,48,1536]{2,1,0:T(8,128)(2,1)} %get-tuple-element.87), channel_id=1, source_target_pairs={{0,1},{1,0},{2,3},{3,2},{4,5},{5,4},{6,7},{7,6},{8,9},{9,8},{10,11... | collective-permute-start | bytes 7077896 | tf_op jit(solution)/shard_map/ppermute | solution.py:551
  351.8 8.2 %collective-permute-start.5 = (bf16[4,416,128]{2,1,0:T(8,128)(2,1)S(1)}, bf16[4,416,128]{2,1,0:T(8,128)(2,1)S(1)}, u32[]{:S(2)}, u32[]{:S(2)}) collective-permute-start(bf16[4,416,128]{2,1,0:T(8,128)(2,1)S(1)} %get-tuple-element.165), channel_id=1, source_target_pairs={{0,4},{1,3},{2,6},{3,1},{4,0},{5,7},{6,2},{7,5},{8,12},{9,11},{10,... | collective-permute-start | bytes 1277960 | tf_op jit(solution)/shard_map/ppermute | solution.py:562
  360.1 6.7 collective-permute-start.6
  366.8 6.8 %collective-permute-start.7 = (bf16[1,416,128]{2,1,0:T(8,128)(2,1)S(1)}, bf16[1,416,128]{2,1,0:T(8,128)(2,1)S(1)}, u32[]{:S(2)}, u32[]{:S(2)}) collective-permute-start(bf16[1,416,128]{2,1,0:T(8,128)(2,1)S(1)} %fusion.22), channel_id=1, source_target_pairs={{0,16},{1,17},{2,18},{3,19},{4,20},{5,21},{6,22},{7,23},{8,24},{9,... | collective-permute-start | bytes 319496 | tf_op jit(solution)/shard_map/ppermute | solution.py:562
  373.7 0.7 copy-start.3
  375.0 236.2 %all-gather.9.cloned.1.call-start = ((), (), s32[]{:S(2)}) async-start(), calls=%async_computation.1 | async-start | bytes 4866048 | tf_op jit(solution)/shard_map/all_gather | solution.py:576
  378.2 17.2 %collective-permute-start.9 = (bf16[8,48,1536]{2,1,0:T(8,128)(2,1)S(1)}, bf16[8,48,1536]{2,1,0:T(8,128)(2,1)S(1)}, u32[]{:S(2)}, u32[]{:S(2)}) collective-permute-start(bf16[8,48,1536]{2,1,0:T(8,128)(2,1)S(1)} %get-tuple-element.153), channel_id=1, source_target_pairs={{0,2},{1,5},{2,0},{3,7},{4,6},{5,1},{6,4},{7,3},{8,10},{9,13},{10,... | collective-permute-start | bytes 3538952 | tf_op jit(solution)/shard_map/ppermute | solution.py:562
  395.7 11.0 %collective-permute-start.10 = (bf16[4,48,1536]{2,1,0:T(8,128)(2,1)S(1)}, bf16[4,48,1536]{2,1,0:T(8,128)(2,1)S(1)}, u32[]{:S(2)}, u32[]{:S(2)}) collective-permute-start(bf16[4,48,1536]{2,1,0:T(8,128)(2,1)S(1)} %get-tuple-element.163), channel_id=1, source_target_pairs={{0,4},{1,3},{2,6},{3,1},{4,0},{5,7},{6,2},{7,5},{8,12},{9,11},{10,... | collective-permute-start | bytes 1769480 | tf_op jit(solution)/shard_map/ppermute | solution.py:562
  406.9 8.5 %collective-permute-start.11 = (bf16[2,48,1536]{2,1,0:T(8,128)(2,1)S(1)}, bf16[2,48,1536]{2,1,0:T(8,128)(2,1)S(1)}, u32[]{:S(2)}, u32[]{:S(2)}) collective-permute-start(bf16[2,48,1536]{2,1,0:T(8,128)(2,1)S(1)} %get-tuple-element.171), channel_id=1, source_target_pairs={{0,8},{1,9},{2,10},{3,11},{4,12},{5,13},{6,14},{7,15},{8,0},{9,1},... | collective-permute-start | bytes 884744 | tf_op jit(solution)/shard_map/ppermute | solution.py:562
  415.4 10.7 %collective-permute-start.12 = (bf16[1,48,1536]{2,1,0:T(8,128)(2,1)S(1)}, bf16[1,48,1536]{2,1,0:T(8,128)(2,1)S(1)}, u32[]{:S(2)}, u32[]{:S(2)}) collective-permute-start(bf16[1,48,1536]{2,1,0:T(8,128)(2,1)S(1)} %fusion.19), channel_id=1, source_target_pairs={{0,16},{1,17},{2,18},{3,19},{4,20},{5,21},{6,22},{7,23},{8,24},{9,... | collective-permute-start | bytes 442376 | tf_op jit(solution)/shard_map/ppermute | solution.py:562
  426.9 195.3 %all-gather.13.cloned.1.call-start = ((), (), s32[]{:S(2)}) async-start(), calls=%async_computation.3 | async-start | bytes 4866048 | tf_op jit(solution)/shard_map/all_gather | solution.py:576
  437.3 10.9 %collective-permute-start.18 = (bf16[16,48,1536]{2,1,0:T(8,128)(2,1)}, bf16[16,48,1536]{2,1,0:T(8,128)(2,1)S(1)}, u32[]{:S(2)}, u32[]{:S(2)}) collective-permute-start(bf16[16,48,1536]{2,1,0:T(8,128)(2,1)} %weight_grad_send.3), channel_id=1, source_target_pairs={{0,1},{1,0},{2,3},{3,2},{4,5},{5,4},{6,7},{7,6},{8,9},{9,8},{10,11... | collective-permute-start | bytes 7077896 | tf_op jit(solution)/shard_map/ppermute | solution.py:551
  451.3 20.5 %collective-permute-start.19 = (bf16[8,48,1536]{2,1,0:T(8,128)(2,1)S(1)}, bf16[8,48,1536]{2,1,0:T(8,128)(2,1)S(1)}, u32[]{:S(2)}, u32[]{:S(2)}) collective-permute-start(bf16[8,48,1536]{2,1,0:T(8,128)(2,1)S(1)} %get-tuple-element.149), channel_id=1, source_target_pairs={{0,2},{1,5},{2,0},{3,7},{4,6},{5,1},{6,4},{7,3},{8,10},{9,13},{10,... | collective-permute-start | bytes 3538952 | tf_op jit(solution)/shard_map/ppermute | solution.py:562
  472.2 11.4 %collective-permute-start.20 = (bf16[4,48,1536]{2,1,0:T(8,128)(2,1)S(1)}, bf16[4,48,1536]{2,1,0:T(8,128)(2,1)S(1)}, u32[]{:S(2)}, u32[]{:S(2)}) collective-permute-start(bf16[4,48,1536]{2,1,0:T(8,128)(2,1)S(1)} %get-tuple-element.159), channel_id=1, source_target_pairs={{0,4},{1,3},{2,6},{3,1},{4,0},{5,7},{6,2},{7,5},{8,12},{9,11},{10,... | collective-permute-start | bytes 1769480 | tf_op jit(solution)/shard_map/ppermute | solution.py:562
  483.7 17.0 %collective-permute-start.21 = (bf16[2,48,1536]{2,1,0:T(8,128)(2,1)S(1)}, bf16[2,48,1536]{2,1,0:T(8,128)(2,1)S(1)}, u32[]{:S(2)}, u32[]{:S(2)}) collective-permute-start(bf16[2,48,1536]{2,1,0:T(8,128)(2,1)S(1)} %get-tuple-element.167), channel_id=1, source_target_pairs={{0,8},{1,9},{2,10},{3,11},{4,12},{5,13},{6,14},{7,15},{8,0},{9,1},... | collective-permute-start | bytes 884744 | tf_op jit(solution)/shard_map/ppermute | solution.py:562
  500.7 7.2 %collective-permute-start.22 = (bf16[1,48,1536]{2,1,0:T(8,128)(2,1)S(1)}, bf16[1,48,1536]{2,1,0:T(8,128)(2,1)S(1)}, u32[]{:S(2)}, u32[]{:S(2)}) collective-permute-start(bf16[1,48,1536]{2,1,0:T(8,128)(2,1)S(1)} %fusion.13), channel_id=1, source_target_pairs={{0,16},{1,17},{2,18},{3,19},{4,20},{5,21},{6,22},{7,23},{8,24},{9,... | collective-permute-start | bytes 442376 | tf_op jit(solution)/shard_map/ppermute | solution.py:562
  508.7 144.1 %all-gather.11.cloned.1.call-start = ((), (), s32[]{:S(2)}) async-start(), calls=%async_computation.2 | async-start | bytes 4866048 | tf_op jit(solution)/shard_map/all_gather | solution.py:576
  518.9 11.0 %collective-permute-start.13 = (bf16[16,48,1536]{2,1,0:T(8,128)(2,1)}, bf16[16,48,1536]{2,1,0:T(8,128)(2,1)S(1)}, u32[]{:S(2)}, u32[]{:S(2)}) collective-permute-start(bf16[16,48,1536]{2,1,0:T(8,128)(2,1)} %weight_grad_send.2), channel_id=1, source_target_pairs={{0,1},{1,0},{2,3},{3,2},{4,5},{5,4},{6,7},{7,6},{8,9},{9,8},{10,11... | collective-permute-start | bytes 7077896 | tf_op jit(solution)/shard_map/ppermute | solution.py:551
  532.9 18.6 %collective-permute-start.14 = (bf16[8,48,1536]{2,1,0:T(8,128)(2,1)S(1)}, bf16[8,48,1536]{2,1,0:T(8,128)(2,1)S(1)}, u32[]{:S(2)}, u32[]{:S(2)}) collective-permute-start(bf16[8,48,1536]{2,1,0:T(8,128)(2,1)S(1)} %get-tuple-element.151), channel_id=1, source_target_pairs={{0,2},{1,5},{2,0},{3,7},{4,6},{5,1},{6,4},{7,3},{8,10},{9,13},{10,... | collective-permute-start | bytes 3538952 | tf_op jit(solution)/shard_map/ppermute | solution.py:562
  551.9 38.5 %copy-start.2 = (bf16[2048,768]{1,0:T(8,128)(2,1)S(1)}, bf16[2048,768]{1,0:T(8,128)(2,1)}, u32[]{:S(2)}) copy-start(bf16[2048,768]{1,0:T(8,128)(2,1)} %get-tuple-element.57) | copy-start | bytes 9437188
  551.9 17.3 %collective-permute-start.15 = (bf16[4,48,1536]{2,1,0:T(8,128)(2,1)S(1)}, bf16[4,48,1536]{2,1,0:T(8,128)(2,1)S(1)}, u32[]{:S(2)}, u32[]{:S(2)}) collective-permute-start(bf16[4,48,1536]{2,1,0:T(8,128)(2,1)S(1)} %get-tuple-element.161), channel_id=1, source_target_pairs={{0,4},{1,3},{2,6},{3,1},{4,0},{5,7},{6,2},{7,5},{8,12},{9,11},{10,... | collective-permute-start | bytes 1769480 | tf_op jit(solution)/shard_map/ppermute | solution.py:562
  569.4 22.3 %copy-start.5 = (bf16[120,128]{1,0:T(8,128)(2,1)S(1)}, bf16[120,128]{1,0:T(8,128)(2,1)}, u32[]{:S(2)}) copy-start(bf16[120,128]{1,0:T(8,128)(2,1)} %param.17) | copy-start | bytes 92164
  569.4 11.1 %collective-permute-start.16 = (bf16[2,48,1536]{2,1,0:T(8,128)(2,1)S(1)}, bf16[2,48,1536]{2,1,0:T(8,128)(2,1)S(1)}, u32[]{:S(2)}, u32[]{:S(2)}) collective-permute-start(bf16[2,48,1536]{2,1,0:T(8,128)(2,1)S(1)} %get-tuple-element.169), channel_id=1, source_target_pairs={{0,8},{1,9},{2,10},{3,11},{4,12},{5,13},{6,14},{7,15},{8,0},{9,1},... | collective-permute-start | bytes 884744 | tf_op jit(solution)/shard_map/ppermute | solution.py:562
  580.6 9.1 %collective-permute-start.17 = (bf16[1,48,1536]{2,1,0:T(8,128)(2,1)S(1)}, bf16[1,48,1536]{2,1,0:T(8,128)(2,1)S(1)}, u32[]{:S(2)}, u32[]{:S(2)}) collective-permute-start(bf16[1,48,1536]{2,1,0:T(8,128)(2,1)S(1)} %fusion.16), channel_id=1, source_target_pairs={{0,16},{1,17},{2,18},{3,19},{4,20},{5,21},{6,22},{7,23},{8,24},{9,... | collective-permute-start | bytes 442376 | tf_op jit(solution)/shard_map/ppermute | solution.py:562
  591.7 3.8 collective-permute-start.2
  652.8 9.5 %copy-start.1 = (f32[8,768]{1,0:T(8,128)S(1)}, f32[8,768]{1,0:T(8,128)}, u32[]{:S(2)}) copy-start(f32[8,768]{1,0:T(8,128)} %param.19) | copy-start | bytes 73732
Sparse Core Ops, SparseCore 0:
  11.8 56.3 all-gather.14
  375.1 56.5 all-gather.6
  435.3 66.2 all-gather.8
  508.8 68.9 all-gather.12
  590.5 62.1 all-gather.10

commit v2 on v1

v2 whole, which is shorter than its diff:
```python
import functools
import math

import jax
import jax.numpy as jnp
from jax import lax
from jax.experimental import pallas as pl
from jax.experimental.pallas import tpu as pltpu
from jax.sharding import PartitionSpec as P

HEAD = 64
BF = jnp.bfloat16
F32 = jnp.float32
NN = (((1,), (0,)), ((), ()))
NT = (((1,), (1,)), ((), ()))
TN = (((0,), (0,)), ((), ()))
VMEM_BYTES = 60 * 2**20
GELU_A = math.sqrt(2 / math.pi)
GELU_B = 0.044715


def dot(left, right, dims=NN):
    return lax.dot_general(left, right, dims, preferred_element_type=F32)


def params(limit=VMEM_BYTES):
    return pltpu.CompilerParams(vmem_limit_bytes=limit)


def cost(micros):
    return pl.CostEstimate(flops=int(micros * 1.2e9), bytes_accessed=0, transcendentals=0)


def whole(shape):
    return pl.BlockSpec(shape, lambda *_: (0,) * len(shape), pipeline_mode=pl.Buffered(1))


def smem():
    return pl.BlockSpec(memory_space=pltpu.SMEM)


def normalise(hidden):
    centre = hidden - jnp.mean(hidden, axis=-1, keepdims=True)
    inv = lax.rsqrt(jnp.mean(centre * centre, axis=-1, keepdims=True) + 1e-05)
    return centre * inv, inv


def norm_back(hidden, gain, grad):
    unit, inv = normalise(hidden)
    scaled = grad * gain
    part = inv * (
        scaled
        - jnp.mean(scaled, axis=-1, keepdims=True)
        - unit * jnp.mean(scaled * unit, axis=-1, keepdims=True)
    )
    return part, jnp.sum(grad * unit, axis=0, keepdims=True)


ORDER = []


def launch(kernel, inputs, in_specs, out_specs, out_shape, grid, name, estimate, prefetch=(), aliases=None, scratch=(), limit=VMEM_BYTES, chained=True):
    count = len(prefetch) + len(inputs)
    outs, waits = len(out_shape), len(ORDER)

    def body(*refs):
        at = count + waits
        refs[at + outs][...] = jnp.zeros((8, 128), F32)
        kernel(*refs[:count], *refs[at : at + outs], *refs[at + outs + 1 :])

    token = pl.BlockSpec((8, 128), lambda *_: (0, 0))
    *results, last = pl.pallas_call(
        body,
        grid_spec=pltpu.PrefetchScalarGridSpec(
            num_scalar_prefetch=len(prefetch),
            grid=grid,
            in_specs=list(in_specs) + [whole((8, 128))] * waits,
            out_specs=list(out_specs) + [token],
            scratch_shapes=list(scratch),
        ),
        out_shape=list(out_shape) + [jax.ShapeDtypeStruct((8, 128), F32)],
        input_output_aliases={len(prefetch) + k: v for k, v in (aliases or {}).items()},
        compiler_params=params(limit),
        cost_estimate=estimate,
        name=name,
    )(*prefetch, *inputs, *ORDER)
    if chained:
        ORDER[:] = [last]
    return results


def anywhere(count):
    return [pl.BlockSpec(memory_space=pl.ANY)] * count


def ignoring(kernel, inputs, extra):
    return lambda *refs: kernel(*refs[:inputs], *refs[inputs + extra :])


def accumulate(ref, first, value):
    @pl.when(first)
    def _():
        ref[...] = value

    @pl.when(jnp.logical_not(first))
    def _():
        ref[...] += value


def embed_kernel(
    buckets, ids_ref, own_ref, other_ref, noise_ref, win_ref, time_ref, pos_ref, gain_ref, wqkv_ref,
    word_ref, noisy_ref, stream_ref, left_ref, packed_ref, scal_ref, table_ref,
    *, tiles, table_span, seqs, step,
):
    index = pl.program_id(0)
    seq = index // tiles
    chunks, span, width = own_ref.shape
    bucket_count = time_ref.shape[0]

    @pl.when(index == 0)
    def _():
        real = lax.broadcasted_iota(jnp.int32, (span, 1), 0) < table_span
        norms = jnp.zeros((span, 1), F32)
        counts = jnp.zeros((1, width), F32)
        for half, ref in enumerate((own_ref, other_ref)):
            for chunk in range(chunks):
                block = ref[chunk].astype(F32)
                norms += jnp.where(
                    real, jnp.sqrt(jnp.sum(block * block, axis=1, keepdims=True) + 1e-06), 0.0
                )
                counts += block[table_span : table_span + 1, :]
                at = (half * chunks + chunk) * span
                table_ref[:, at : at + span] = block.T.astype(BF)
        mean_norm = jnp.sum(norms, axis=0, keepdims=True) / (2 * chunks * table_span)
        lane = lax.broadcasted_iota(jnp.int32, (1, width), 1)
        scal_ref[...] = jnp.zeros_like(scal_ref)
        for each in range(seqs):
            bucket = buckets[each]
            signal, spread = jnp.float32(0.0), jnp.float32(0.0)
            for kind in range(bucket_count):
                angle = math.pi / 2 * (kind + 1.0) / (bucket_count + 1)
                signal = jnp.where(bucket == kind, math.cos(angle), signal)
                spread = jnp.where(bucket == kind, math.sin(angle), spread)
            count = jnp.sum(jnp.where(lane == bucket, counts, 0.0), axis=1, keepdims=True)
            row = jnp.where(lane == 0, signal, jnp.where(lane == 1, spread, 0.0))
            row = jnp.where(lane == 2, 2.0 / count, row)
            row = jnp.where(lane == 3, math.sqrt(width) / mean_norm, row)
            scal_ref[each : each + 1, :] = jnp.where(lane == 4, mean_norm, row)

    ids = ids_ref[...]
    word = jnp.zeros((width, ids.shape[1]), F32)
    for start in range(0, 2 * chunks * span, step):
        row = lax.broadcasted_iota(jnp.int32, (step, ids.shape[1]), 0) + start
        one = jnp.where(row == ids, 1.0, 0.0).astype(BF)
        word += dot(table_ref[:, start : start + step], one)
    word = word.T
    word_ref[...] = word.astype(BF)
    scal = scal_ref[pl.ds(seq, 1), :]
    clean = word * scal[:, 3:4]
    noisy = (scal[:, 0:1] * clean + scal[:, 1:2] * noise_ref[...].astype(F32)).astype(BF)
    noisy_ref[...] = noisy
    stream = dot(noisy, win_ref[...]) + time_ref[pl.ds(buckets[seq], 1), :] + pos_ref[...]
    stream_ref[...] = stream
    attn = (normalise(stream)[0] * gain_ref[...]).astype(BF)
    left_ref[0] = attn
    packed_ref[...] = dot(attn, wqkv_ref[...]).astype(BF)


def embed(buckets, ids, own, other, noise, w_in, time_table, pos_table, gain, w_qkv, table_span, tm=256):
    tokens, width = noise.shape
    length, model = pos_table.shape
    seqs, tiles = tokens // length, length // tm
    wide = w_qkv.shape[1]
    rows = 2 * own.shape[0] * own.shape[1]
    row = lambda cols: pl.BlockSpec((tm, cols), lambda i: (i, 0))
    return launch(
        functools.partial(
            embed_kernel, tiles=tiles, table_span=table_span, seqs=seqs, step=min(rows, 1024)
        ),
        [buckets, ids, own, other, noise, w_in, time_table, pos_table, gain, w_qkv],
        [
            smem(), pl.BlockSpec((1, tm), lambda i: (0, i)), whole(own.shape), whole(other.shape),
            row(width), whole(w_in.shape), whole(time_table.shape),
            pl.BlockSpec((tm, model), lambda i: (i % tiles, 0)), whole(gain.shape), whole(w_qkv.shape),
        ],
        [
            row(width), row(width), row(model), pl.BlockSpec((1, tm, model), lambda i: (0, i, 0)),
            row(wide), pl.BlockSpec((8, width), lambda i: (0, 0)),
        ],
        [
            jax.ShapeDtypeStruct((tokens, width), BF),
            jax.ShapeDtypeStruct((tokens, width), BF),
            jax.ShapeDtypeStruct((tokens, model), F32),
            jax.ShapeDtypeStruct((2, tokens, model), BF),
            jax.ShapeDtypeStruct((tokens, wide), BF),
            jax.ShapeDtypeStruct((8, width), F32),
        ],
        (tokens // tm,),
        "embed",
        cost(tokens / 80),
        scratch=[pltpu.VMEM((width, rows), BF)],
    )


def attend_kernel(q_ref, k_ref, v_ref, mixed_ref, probs_ref, inv_ref, *, tq):
    length = q_ref.shape[0]
    lane = lax.broadcasted_iota(jnp.int32, (1, 2 * HEAD), 1)
    keys = k_ref[...]
    values = jnp.concatenate([v_ref[...], jnp.ones_like(v_ref[...])], axis=1)
    scale = math.log2(math.e) * HEAD**-0.5
    for start in range(0, length, tq):
        rows = slice(start, start + tq)
        query = q_ref[rows, :]
        parts = []
        for head in range(2):
            own = jnp.where(lane // HEAD == head, query, jnp.zeros_like(query))
            scores = dot(own, keys, NT)
            peak = jnp.max(scores, axis=1, keepdims=True)
            raised = jnp.exp2(scores * scale - peak * scale).astype(BF)
            probs_ref[head, rows, :] = raised
            sums = dot(raised, values)
            inv = 1.0 / sums[:, 2 * HEAD :]
            parts.append((sums[:, : 2 * HEAD] * inv, inv))
        low = lane < HEAD
        mixed_ref[0, rows, :] = jnp.where(low, parts[0][0], parts[1][0]).astype(BF)
        inv_ref[rows, :] = jnp.where(low, parts[0][1], parts[1][1])


def attend(packed, length, lefts, tq=256):
    tokens = packed.shape[0]
    seqs, pairs = tokens // length, packed.shape[1] // (6 * HEAD)
    spec = lambda part: pl.BlockSpec((length, 2 * HEAD), lambda s, j: (s, part * pairs + j))
    return launch(
        ignoring(functools.partial(attend_kernel, tq=tq), 3, 1),
        [packed, packed, packed, lefts],
        [spec(0), spec(1), spec(2)] + anywhere(1),
        [
            pl.BlockSpec((1, length, 2 * HEAD), lambda s, j: (1, s, j)),
            pl.BlockSpec((2, length, length), lambda s, j: (s * pairs + j, 0, 0)), spec(0),
        ],
        [
            jax.ShapeDtypeStruct(lefts.shape, BF),
            jax.ShapeDtypeStruct((seqs * pairs * 2, length, length), BF),
            jax.ShapeDtypeStruct((tokens, pairs * 2 * HEAD), F32),
        ],
        (seqs, pairs),
        "attend",
        cost(3.5 * seqs * pairs),
        aliases={3: 0},
    )


def attend_back_kernel(
    q_ref, k_ref, v_ref, grad_ref, mixed_ref, inv_ref, probs_ref, out_ref, *, tq
):
    length = q_ref.shape[0]
    lane = lax.broadcasted_iota(jnp.int32, (1, 2 * HEAD), 1)
    keys, values = k_ref[...], v_ref[...]
    scale = HEAD**-0.5
    held = [None] * (length // tq)
    key_parts, value_parts = [], []
    for head in range(2):
        mask = lane // HEAD == head
        grad_k, grad_v = None, None
        cut = slice(head * HEAD, (head + 1) * HEAD)
        for tile in range(length // tq):
            rows = slice(tile * tq, (tile + 1) * tq)
            grad = grad_ref[rows, :]
            inv = inv_ref[rows, :]
            wide = grad.astype(F32)
            inner = jnp.sum(
                jnp.where(mask, wide * mixed_ref[0, rows, :].astype(F32), 0.0), axis=1, keepdims=True
            )
            grad_probs = dot(jnp.where(mask, grad, jnp.zeros_like(grad)), values, NT)
            raised = probs_ref[head, rows, :]
            grad_scores = (raised.astype(F32) * (grad_probs - inner)).astype(BF)
            grad_q = dot(grad_scores, keys) * (inv * scale)
            if head == 0:
                held[tile] = grad_q
            else:
                out_ref[0, rows, :] = jnp.where(lane < HEAD, held[tile], grad_q).astype(BF)
            query = (q_ref[rows, :].astype(F32) * (inv * scale)).T[cut, :].astype(BF)
            outer = (wide * inv).T[cut, :].astype(BF)
            part_k, part_v = dot(query, grad_scores), dot(outer, raised)
            grad_k = part_k if grad_k is None else grad_k + part_k
            grad_v = part_v if grad_v is None else grad_v + part_v
        key_parts.append(grad_k)
        value_parts.append(grad_v)
    out_ref[1] = jnp.concatenate(key_parts, axis=0).T.astype(BF)
    out_ref[2] = jnp.concatenate(value_parts, axis=0).T.astype(BF)


def attend_back(packed, grad_mixed, lefts, inv, probs, length, first, count, held, tq=256):
    pairs = packed.shape[1] // (6 * HEAD)
    at = lambda i: ((first + i) // pairs, (first + i) % pairs)
    spec = lambda part: pl.BlockSpec(
        (length, 2 * HEAD), lambda i: (at(i)[0], part * pairs + at(i)[1])
    )
    return launch(
        ignoring(functools.partial(attend_back_kernel, tq=tq), 7, 1),
        [packed, packed, packed, grad_mixed, lefts, inv, probs, held],
        [
            spec(0), spec(1), spec(2), spec(0),
            pl.BlockSpec((1, length, 2 * HEAD), lambda i: (1, *at(i))), spec(0),
            pl.BlockSpec((2, length, length), lambda i: (first + i, 0, 0)),
        ]
        + anywhere(1),
        [pl.BlockSpec((3, length, 2 * HEAD), lambda i: (0, *at(i)))],
        [jax.ShapeDtypeStruct(held.shape, BF)],
        (count,),
        "attend_back",
        cost(4.5 * count),
        aliases={7: 0},
    )[0]


def forward_kernel(
    scal_ref, mixed_ref, stream_ref, word_ref, wout_ref, gain_ref, wup_ref, wdown_ref, whead_ref,
    mid_ref, mlp_ref, act_ref, slope_ref, out_ref, gpred_ref, branch_ref, ghead_ref,
    *, tiles, step,
):
    index = pl.program_id(0)
    seq = index // tiles
    mid = stream_ref[...] + dot(mixed_ref[0], wout_ref[...])
    mid_ref[...] = mid
    mlp = (normalise(mid)[0] * gain_ref[...]).astype(BF)
    mlp_ref[...] = mlp
    total = mid
    for start in range(0, wup_ref.shape[1], step):
        cols = slice(start, start + step)
        up = dot(mlp, wup_ref[:, cols])
        inner = (2.0 * GELU_A * GELU_B) * (up * up) + 2.0 * GELU_A
        share = 0.5 + 0.5 * jnp.tanh(up * (0.5 * inner))
        full = up * share
        act = full.astype(BF)
        act_ref[:, cols] = act
        slope = share + full * (1.0 - share) * (3.0 * inner - 4.0 * GELU_A)
        slope_ref[:, cols] = slope.astype(BF)
        total = total + dot(act, wdown_ref[cols, :])
    low = total.astype(BF)
    out_ref[...] = low
    scal = scal_ref[pl.ds(seq, 1), :]
    clean = word_ref[...].astype(F32) * scal[:, 3:4]
    gpred = (dot(low, whead_ref[...]) - clean) * scal[:, 2:3]
    gpred_ref[...] = gpred
    gpred_low = gpred.astype(BF)
    branch_ref[...] = dot(gpred_low, whead_ref[...], NT).astype(BF)
    accumulate(ghead_ref, index == 0, dot(gpred.T.astype(BF), low))


def forward(scal, lefts, stream, word, w_out, gain, w_up, w_down, w_head, length, tm=256, step=768):
    tokens, model = stream.shape
    inner, width = w_up.shape[1], w_head.shape[1]
    row = lambda cols: pl.BlockSpec((tm, cols), lambda i: (i, 0))
    shape = lambda cols, kind: jax.ShapeDtypeStruct((tokens, cols), kind)
    return launch(
        functools.partial(forward_kernel, tiles=length // tm, step=step),
        [scal, lefts, stream, word, w_out, gain, w_up, w_down, w_head],
        [
            whole(scal.shape), pl.BlockSpec((1, tm, model), lambda i: (1, i, 0)), row(model), row(width),
            whole(w_out.shape), whole(gain.shape), whole(w_up.shape), whole(w_down.shape),
            whole(w_head.shape),
        ],
        [
            row(model), row(model), row(inner), row(inner), row(model), row(width), row(model),
            pl.BlockSpec((width, model), lambda i: (0, 0)),
        ],
        [
            shape(model, F32), shape(model, BF), shape(inner, BF), shape(inner, BF),
            shape(model, BF), shape(width, F32), shape(model, BF),
            jax.ShapeDtypeStruct((width, model), F32),
        ],
        (tokens // tm,),
        "feed_forward",
        cost(tokens / 45),
    )


def back_kernel(
    mid_ref, slope_ref, gpred_ref, branch_ref, wout_ref, gain_ref, wup_ref, wdown_ref, whead_ref,
    upin_ref, gmid_ref, gattn_ref, gmixed_ref, ggain_ref, *, step,
):
    index = pl.program_id(0)
    branch = branch_ref[...]
    grad = None
    for start in range(0, wup_ref.shape[1], step):
        cols = slice(start, start + step)
        upin = (dot(branch, wdown_ref[cols, :], NT) * slope_ref[:, cols].astype(F32)).astype(BF)
        upin_ref[:, cols] = upin
        part = dot(upin, wup_ref[:, cols], NT)
        grad = part if grad is None else grad + part
    part, gain_part = norm_back(mid_ref[...], gain_ref[...], grad)
    accumulate(ggain_ref, index == 0, gain_part)
    gmid = dot(gpred_ref[...].astype(BF), whead_ref[...], NT) + part
    gmid_ref[...] = gmid
    low = gmid.astype(BF)
    gattn_ref[0] = low
    gmixed_ref[...] = dot(low, wout_ref[...], NT).astype(BF)


def back(mid, slope, gpred, branch, w_out, gain, w_up, w_down, w_head, tm=256, step=768):
    tokens, model = mid.shape
    inner, width = w_up.shape[1], w_head.shape[1]
    row = lambda cols: pl.BlockSpec((tm, cols), lambda i: (i, 0))
    shape = lambda cols, kind: jax.ShapeDtypeStruct((tokens, cols), kind)
    return launch(
        functools.partial(back_kernel, step=step),
        [mid, slope, gpred, branch, w_out, gain, w_up, w_down, w_head],
        [
            row(model), row(inner), row(width), row(model), whole(w_out.shape), whole(gain.shape),
            whole(w_up.shape), whole(w_down.shape), whole(w_head.shape),
        ],
        [
            row(inner), row(model), pl.BlockSpec((1, tm, model), lambda i: (3, i, 0)), row(model),
            pl.BlockSpec((1, model), lambda i: (0, 0)),
        ],
        [
            shape(inner, BF), shape(model, F32), jax.ShapeDtypeStruct((4, tokens, model), BF),
            shape(model, BF), jax.ShapeDtypeStruct((1, model), F32),
        ],
        (tokens // tm,),
        "feed_forward_back",
        cost(tokens / 55),
    )


def input_back_kernel(
    scal_ref, gmid_ref, dq_ref, dk_ref, dv_ref, stream_ref, noisy_ref, word_ref, gpred_ref, gain_ref,
    wqkv_ref, win_ref, gpos_ref, gtime_ref, ggain_ref, gwin_ref, grows_ref, gscale_ref,
):
    tile, seq = pl.program_id(0), pl.program_id(1)
    first = jnp.logical_and(tile == 0, seq == 0)
    model = win_ref.shape[1]
    grad = (
        dot(dq_ref[0], wqkv_ref[:, :model], NT)
        + dot(dk_ref[0], wqkv_ref[:, model : 2 * model], NT)
        + dot(dv_ref[0], wqkv_ref[:, 2 * model :], NT)
    )
    part, gain_part = norm_back(stream_ref[...], gain_ref[...], grad)
    accumulate(ggain_ref, first, gain_part)
    gin = gmid_ref[...] + part
    accumulate(gpos_ref, seq == 0, gin)
    sums = jnp.sum(gin, axis=0, keepdims=True)
    @pl.when(tile == 0)
    def _():
        gtime_ref[pl.ds(seq, 1), :] = sums

    @pl.when(tile > 0)
    def _():
        gtime_ref[pl.ds(seq, 1), :] += sums

    low = gin.astype(BF)
    accumulate(gwin_ref, first, dot(noisy_ref[...].astype(F32).T.astype(BF), low))
    scal = scal_ref[pl.ds(seq, 1), :]
    gclean = scal[:, 0:1] * dot(low, win_ref[...], NT) - gpred_ref[...]
    grows_ref[...] = (gclean * scal[:, 3:4]).astype(BF)
    accumulate(
        gscale_ref, first, jnp.sum(word_ref[...].astype(F32) * gclean, axis=0, keepdims=True)
    )


def input_back(scal, gmid, grads, stream, noisy, word, gpred, gain, w_qkv, w_in, length, tm=256):
    tokens, model = gmid.shape
    width = w_in.shape[0]
    seqs, tiles = tokens // length, length // tm
    row = lambda cols: pl.BlockSpec((tm, cols), lambda i, s: (s * tiles + i, 0))
    plane = lambda part: pl.BlockSpec((1, tm, model), lambda i, s: (part, s * tiles + i, 0))
    fixed = lambda rows, cols: pl.BlockSpec((rows, cols), lambda i, s: (0, 0))
    return launch(
        input_back_kernel,
        [scal, gmid, grads, grads, grads, stream, noisy, word, gpred, gain, w_qkv, w_in],
        [
            whole(scal.shape), row(model), plane(0), plane(1), plane(2), row(model), row(width),
            row(width), row(width), whole(gain.shape), whole(w_qkv.shape), whole(w_in.shape),
        ],
        [
            pl.BlockSpec((tm, model), lambda i, s: (i, 0)), fixed(seqs, model), fixed(1, model),
            fixed(width, model), row(width), fixed(1, width),
        ],
        [
            jax.ShapeDtypeStruct((length, model), F32),
            jax.ShapeDtypeStruct((seqs, model), F32),
            jax.ShapeDtypeStruct((1, model), F32),
            jax.ShapeDtypeStruct((width, model), F32),
            jax.ShapeDtypeStruct((tokens, width), BF),
            jax.ShapeDtypeStruct((1, width), F32),
        ],
        (tiles, seqs),
        "input_back",
        cost(tokens / 90),
    )


def bit_orders(batch):
    bits = list(range(batch.bit_length() - 1))
    return bits, bits[1:3] + bits[:1] + bits[3:]


def place(owner, me, order):
    apart = jnp.bitwise_xor(owner, me)
    spot = 0
    for bit in order:
        spot = spot * 2 + jnp.bitwise_and(lax.shift_right_logical(apart, bit), 1)
    return spot


def chunk_shape(batch, rows, cols):
    row_blocks = min(batch, 16 if batch <= 16 else 32)
    return row_blocks, rows // row_blocks, cols * row_blocks // batch


def outer_kernel(where, left_ref, right_ref, *outs, orders, row_blocks, tw, steps):
    me, core = where[0], where[1]
    acc = dot(left_ref[0], right_ref[0], TN)
    if len(outs) == 1:
        rows = outs[0].shape[2]
        for row in range(row_blocks):
            outs[0][row, 0] = acc[row * rows : (row + 1) * rows, :]
        return
    chunks, rows, cols = outs[0].shape
    col_blocks = chunks // row_blocks
    tile, per = pl.program_id(0), cols // tw
    half, step = tile // steps, tile % steps
    block = step // per if col_blocks > 1 else 0
    cut = pl.ds(pl.multiple_of((step % per) * tw, 128), tw) if col_blocks > 1 else slice(None)

    def write(ref):
        for row in range(row_blocks):
            owner = row * col_blocks + block
            spot = jnp.where(half == 0, place(owner, me, orders[0]), place(owner, me, orders[1]))
            ref[spot, :, cut] = acc[row * rows : (row + 1) * rows, :].astype(ref.dtype)

    @pl.when(core == half)
    def _():
        write(outs[0])

    @pl.when(core != half)
    def _():
        write(outs[1])


def outer(where, lefts, rights, batch, tw=768, by_device=False):
    _, tokens, rows = lefts.shape
    planes, _, width = rights.shape
    cols = planes * width
    row_blocks, chunk_rows, chunk_cols = chunk_shape(batch, rows, cols // 2)
    col_blocks = batch // row_blocks
    tw = next(size for size in (tw, 384, 256, 128) if chunk_cols % size == 0 and width % size == 0)
    per, steps, inside = width // tw, cols // 2 // tw, chunk_cols // tw
    left = lambda i, w: (jnp.where(i // per == planes - 1, lefts.shape[0] - 1, 0), 0, 0)
    if by_device:
        shapes = [jax.ShapeDtypeStruct((row_blocks, col_blocks * 2, chunk_rows, chunk_cols), F32)]
        at = lambda i, w: (0, (i % steps) // inside * 2 + i // steps, 0, i % inside)
        specs = [pl.BlockSpec((row_blocks, 1, chunk_rows, tw), at)]
    else:
        shape = (batch, chunk_rows, chunk_cols)
        shapes = [jax.ShapeDtypeStruct(shape, BF)] * 2
        early = lambda i: jnp.minimum(i, steps - 1)
        late = lambda i: jnp.maximum(i - steps, 0)
        specs = [
            pl.BlockSpec(
                (batch, chunk_rows, tw), lambda i, w: (0, 0, jnp.where(w[1] == 0, early(i), late(i)))
            ),
            pl.BlockSpec(
                (batch, chunk_rows, tw), lambda i, w: (0, 0, jnp.where(w[1] == 0, late(i), early(i)))
            ),
        ]
        if col_blocks > 1:
            specs = [whole(shape)] * 2
    return launch(
        functools.partial(
            outer_kernel, orders=bit_orders(batch), row_blocks=row_blocks, tw=tw, steps=steps
        ),
        [lefts, rights],
        [
            pl.BlockSpec((1, tokens, rows), left),
            pl.BlockSpec((1, tokens, tw), lambda i, w: (i // per, 0, i % per)),
        ],
        specs,
        shapes,
        (cols // tw,),
        "weight_grad",
        cost(tokens / 120),
        prefetch=[where],
    )


def swap(array):
    return lax.ppermute(array, "seq", [(0, 1), (1, 0)])


def hop(array, step):
    batch = lax.axis_size("batch")
    orders = bit_orders(batch)
    pairs = [
        (2 * me + core, 2 * (me ^ (1 << orders[core][step])) + core)
        for me in range(batch)
        for core in range(2)
    ]
    return lax.ppermute(array, ("batch", "seq"), pairs)


def fold_kernel(keep_ref, got_ref, *outs):
    count = keep_ref.shape[0] // 2
    if not count:
        outs[0][...] = (keep_ref[0] + got_ref[0].astype(F32)).astype(outs[0].dtype)
        return
    outs[0][...] = (keep_ref[count:] + got_ref[count:].astype(F32)).astype(BF)
    outs[1][...] = keep_ref[:count] + got_ref[:count].astype(F32)


def fold(keep, got, last=BF, micros=0.4, chained=True):
    count, tail = keep.shape[0] // 2, keep.shape[1:]
    if count:
        shapes = [jax.ShapeDtypeStruct((count, *tail), BF), jax.ShapeDtypeStruct((count, *tail), F32)]
    else:
        shapes = [jax.ShapeDtypeStruct(tail, last)]
    out = launch(
        fold_kernel, [keep, got], [whole(keep.shape), whole(got.shape)],
        [whole(shape.shape) for shape in shapes], shapes, (1,), "fold", cost(micros),
        limit=8 * 2**20 + 12 * keep.size, chained=chained,
    )
    return out if count else out[0]


def rounded_kernel(in_ref, out_ref):
    out_ref[...] = in_ref[...].astype(BF)


def rounded(chunk):
    return launch(
        rounded_kernel, [chunk], [whole(chunk.shape)], [whole(chunk.shape)],
        [jax.ShapeDtypeStruct(chunk.shape, BF)], (1,), "rounded", cost(0.4), limit=8 * 2**20, chained=False,
    )[0]


def join_kernel(held_ref, got_ref, out_ref):
    count = held_ref.shape[0]
    out_ref[:count] = held_ref[...]
    out_ref[count:] = got_ref[...]


def join(held, got):
    shape = (2 * held.shape[0], *held.shape[1:])
    return launch(
        join_kernel, [held, got], [whole(held.shape)] * 2, [whole(shape)],
        [jax.ShapeDtypeStruct(shape, held.dtype)], (1,), "join", cost(0.4),
        limit=8 * 2**20 + 8 * held.size,
    )[0]


class Sum:
    def __init__(self, keep, send):
        self.keep, self.got, self.step = keep, swap(send), -1
        self.steps = lax.axis_size("batch").bit_length() - 1
        self.chunk = None

    def fold(self, last=BF, micros=0.4):
        if self.chunk is not None:
            return
        out = fold(self.keep, self.got, last, micros)
        self.step += 1
        if self.step == self.steps:
            self.chunk = out
        else:
            self.keep = out[1]
            self.got = hop(out[0], self.step)

    def rest(self):
        while self.step < self.steps - 1:
            self.fold()
        return fold(self.keep, self.got, chained=False)

    def finish(self, last=BF):
        while self.chunk is None:
            self.fold(last)
        return self.chunk


class Gather:
    def __init__(self, chunk, batch):
        self.held, self.other = chunk[None], None
        self.steps = list(reversed(range(batch.bit_length() - 1)))
        self.got = hop(self.held, self.steps[0])

    def join(self, plain=False):
        if self.other is not None:
            return
        if plain:
            self.held = jnp.concatenate([self.held, self.got], axis=0)
        else:
            self.held = join(self.held, self.got)
        self.steps.pop(0)
        if self.steps:
            self.got = hop(self.held, self.steps[0])
        else:
            self.other = swap(self.held)

    def finish(self, plain=False):
        while self.other is None:
            self.join(plain)
        return self.held, self.other


def share(chunk):
    return lax.all_gather(chunk, ("batch", "seq"), axis=0)


def mend_kernel(where, own_ref, other_ref, out_ref, *, seqs):
    ours = pl.program_id(0) // seqs == where[1]

    @pl.when(ours)
    def _():
        out_ref[...] = own_ref[...]

    @pl.when(jnp.logical_not(ours))
    def _():
        out_ref[...] = other_ref[...]


def mend(where, own, other):
    seqs, half_len, model = other.shape
    block = (1, half_len, model)
    return launch(
        functools.partial(mend_kernel, seqs=seqs),
        [own, other],
        [
            pl.BlockSpec(block, lambda i, w: (i % seqs, w[1], 0)),
            pl.BlockSpec(block, lambda i, w: (i % seqs, 0, 0)),
        ],
        [pl.BlockSpec(block, lambda i, w: (i, 0, 0))],
        [jax.ShapeDtypeStruct((2 * seqs, half_len, model), BF)],
        (2 * seqs,),
        "mend",
        cost(6),
        prefetch=[where],
    )[0]


def spread_kernel(in_ref, out_ref, *, flip):
    row_blocks, _, _, rows, cols = in_ref.shape
    block = in_ref[...].reshape(row_blocks * rows, cols).astype(F32)
    out_ref[...] = block.T if flip else block


def spread(gathered, batch, rows, cols, flip=False):
    row_blocks, chunk_rows, chunk_cols = chunk_shape(batch, rows, cols // 2)
    view = gathered.reshape(row_blocks, batch // row_blocks, 2, chunk_rows, chunk_cols)
    tw = next(size for size in (512, 384, 256, 128) if chunk_cols % size == 0)
    per, half = chunk_cols // tw, cols // 2 // tw
    return launch(
        functools.partial(spread_kernel, flip=flip),
        [view],
        [
            pl.BlockSpec(
                (row_blocks, 1, 1, chunk_rows, tw),
                lambda i: (0, (i % half) // per, i // half, 0, i % per),
            )
        ],
        [
            pl.BlockSpec((tw, rows), lambda i: (i, 0))
            if flip
            else pl.BlockSpec((rows, tw), lambda i: (0, i))
        ],
        [jax.ShapeDtypeStruct((cols, rows) if flip else (rows, cols), F32)],
        (cols // tw,),
        "spread",
        cost(8),
    )[0]


def spread_near_kernel(
    where, own_ref, other_ref, first_ref, second_ref, *, steps, orders, row_blocks, split
):
    me, core = where[0], where[1]
    chunks, rows, tw = own_ref.shape
    col_blocks = chunks // row_blocks
    step = pl.program_id(0)
    block = (step % steps) * col_blocks // steps if col_blocks > 1 else 0
    tile = jnp.where(step < steps, core, 1 - core) * steps + step % steps

    def write(ref, half, out_ref):
        for row in range(row_blocks):
            owner = row * col_blocks + block
            spot = jnp.where(half == 0, place(owner, me, orders[0]), place(owner, me, orders[1]))
            out_ref[row * rows : (row + 1) * rows, :] = ref[spot].astype(F32)

    for ours in (True, False):
        for out_ref, wanted in ((first_ref, tile < split), (second_ref, tile >= split)):

            @pl.when(jnp.logical_and((step < steps) == ours, wanted))
            def _():
                if ours:
                    write(own_ref, core, out_ref)
                else:
                    write(other_ref, 1 - core, out_ref)


def spread_near(where, own, other, rows, widths):
    batch, chunk_rows, chunk_cols = own.shape
    row_blocks = rows // chunk_rows
    tw = next(size for size in (768, 512, 384, 256, 128) if chunk_cols % size == 0)
    steps, per = sum(widths) // 2 // tw, chunk_cols // tw
    split, rest = widths[0] // tw, widths[1] // tw
    tile = lambda i, w: jnp.where(i < steps, w[1], 1 - w[1]) * steps + i % steps
    second = lambda i, w: jnp.where(
        tile(i, w) >= split, tile(i, w) - split, jnp.where(i < steps, 0, rest - 1)
    )
    return launch(
        functools.partial(
            spread_near_kernel, steps=steps, orders=bit_orders(batch), row_blocks=row_blocks, split=split
        ),
        [own, other],
        [
            pl.BlockSpec(
                (batch, chunk_rows, tw), lambda i, w: (0, 0, jnp.minimum(i, steps - 1) % per)
            ),
            pl.BlockSpec(
                (batch, chunk_rows, tw), lambda i, w: (0, 0, jnp.maximum(i - steps, 0) % per)
            ),
        ],
        [
            pl.BlockSpec((rows, tw), lambda i, w: (0, jnp.minimum(tile(i, w), split - 1))),
            pl.BlockSpec((rows, tw), lambda i, w: (0, second(i, w))),
        ],
        [jax.ShapeDtypeStruct((rows, width), F32) for width in widths],
        (2 * steps,),
        "spread_near",
        cost(8),
        prefetch=[where],
    )


def small_plan(rows, devices):
    each = -(-sum(rows) // devices // 16) * 16
    plan = [[] for _ in range(devices)]
    start = 0
    for source, count in enumerate(rows):
        done = 0
        while done < count:
            chunk, at = divmod(start + done, each)
            size = min(count - done, each - at)
            plan[chunk].append((source, done, at, size))
            done += size
        start += count
    return each, plan


def pack_kernel(
    where, buckets, gpos_ref, gwin_ref, ghead_ref, gtime_ref, ggain_a_ref, ggain_m_ref, gscale_ref,
    ids_ref, grows_ref, keep_ref, send_ref, extra_ref, *, each, plan, orders, buckets_in, span,
):
    me, core = where[0], where[1]
    batch = keep_ref.shape[0]
    panels = gpos_ref.shape[1] // 128
    extra_ref[...] = jnp.zeros_like(extra_ref)
    for seq in range(gtime_ref.shape[0]):
        extra_ref[pl.ds(buckets[seq], 1), :] += gtime_ref[seq : seq + 1, :]
    extra_ref[buckets_in : buckets_in + 1, :] = ggain_a_ref[...]
    extra_ref[buckets_in + 1 : buckets_in + 2, :] = ggain_m_ref[...]
    extra_ref[buckets_in + 2 : buckets_in + 3, :128] = gscale_ref[...]
    sources = (gpos_ref, gwin_ref, ghead_ref, extra_ref)
    for chunk, pieces in enumerate(plan):
        half, owner = divmod(chunk, batch)
        spot = place(owner, me, orders[half])

        def write(ref):
            for panel in range(panels):
                base = panel * each
                filled = 0
                for source, first, at, size in pieces:
                    ref[spot, base + at : base + at + size, :] = sources[source][
                        first : first + size, panel * 128 : (panel + 1) * 128
                    ].astype(ref.dtype)
                    filled = at + size
                if filled < each:
                    ref[spot, base + filled : base + each, :] = jnp.zeros(
                        (each - filled, 128), ref.dtype
                    )

        @pl.when(core == half)
        def _():
            write(keep_ref)

        @pl.when(core != half)
        def _():
            write(send_ref)


    grows = grows_ref[...]
    per = min(4, batch)
    below = slice(panels * each, None)

    def gather_rows(index, _):
        start = index * per * 2 * span
        row = lax.broadcasted_iota(jnp.int32, (per * 2 * span, ids_ref.shape[1]), 0) + start
        one = jnp.where(row == ids_ref[...], 1.0, 0.0).astype(BF)
        sums = dot(one, grows)
        for owner in range(per):
            for half in range(2):
                part = sums[(owner * 2 + half) * span : (owner * 2 + half + 1) * span, :]
                spot = place(index * per + owner, me, orders[half])

                @pl.when(core == half)
                def _():
                    keep_ref[spot, below, :] = part

                @pl.when(core != half)
                def _():
                    send_ref[spot, below, :] = part.astype(BF)

        return 0

    lax.fori_loop(0, batch // per, gather_rows, 0)


def small_rows(length, width, bucket_count):
    return [length, width, width, -(-(bucket_count + 3) // 16) * 16]


def pack(
    where, buckets, gpos, gwin, ghead, gtime, ggain_a, ggain_m, gscale, ids, grows, batch, span,
    bucket_count,
):
    model, width = gpos.shape[1], gwin.shape[0]
    rows = small_rows(gpos.shape[0], width, bucket_count)
    each, plan = small_plan(rows, 2 * batch)
    shape = (batch, each * (model // 128) + span, 128)
    arrays = [gpos, gwin, ghead, gtime, ggain_a, ggain_m, gscale, ids, grows]
    return launch(
        functools.partial(
            pack_kernel, each=each, plan=plan, orders=bit_orders(batch), buckets_in=bucket_count,
            span=span,
        ),
        arrays,
        [whole(array.shape) for array in arrays],
        [whole(shape)] * 2,
        [jax.ShapeDtypeStruct(shape, F32), jax.ShapeDtypeStruct(shape, BF)],
        (1,),
        "pack_small",
        cost(12),
        prefetch=[where, buckets],
        scratch=[pltpu.VMEM((rows[3], model), F32)],
    )


def unpack_kernel(
    where, own_ref, other_ref, mine_ref, table_ref, scal_ref,
    pos_ref, win_ref, head_ref, time_ref, gain_a_ref, gain_m_ref, gtable_ref, turned_ref, extra_ref,
    *, each, plan, orders, vocab,
):
    me, core = where[0], where[1]
    batch = own_ref.shape[0]
    panels = pos_ref.shape[1] // 128
    outs = (pos_ref, win_ref, turned_ref, extra_ref)
    for chunk, pieces in enumerate(plan):
        half, owner = divmod(chunk, batch)
        spot = place(owner, me, orders[half])

        def read(ref):
            for panel in range(panels):
                for source, first, at, size in pieces:
                    base = panel * each + at
                    outs[source][first : first + size, panel * 128 : (panel + 1) * 128] = ref[
                        spot, base : base + size, :
                    ].astype(F32)

        if pieces:

            @pl.when(core == half)
            def _():
                read(own_ref)

            @pl.when(core != half)
            def _():
                read(other_ref)

    head_ref[...] = turned_ref[...].T
    count, width = time_ref.shape[0], table_ref.shape[1]
    time_ref[...] = extra_ref[:count, :]
    gain_a_ref[...] = extra_ref[count, :]
    gain_m_ref[...] = extra_ref[count + 1, :]
    scale = jnp.sum(extra_ref[count + 2 : count + 3, :128], axis=1, keepdims=True)
    mean_norm = scal_ref[0:1, 4:5]
    grad_mean = -math.sqrt(width) / (mean_norm * mean_norm) * scale
    table = table_ref[...].astype(F32)
    norms = jnp.sqrt(jnp.sum(table * table, axis=1, keepdims=True) + 1e-06)
    gtable_ref[...] = mine_ref[: table.shape[0], :] + grad_mean / vocab * table / norms


def unpack(where, own, other, mine, table, scal, length, model, bucket_count, vocab):
    batch = own.shape[0]
    width = table.shape[1]
    rows = small_rows(length, width, bucket_count)
    each, plan = small_plan(rows, 2 * batch)
    shapes = [
        (length, model), (width, model), (model, width), (bucket_count, model), (model,), (model,),
        table.shape,
    ]
    arrays = [own, other, mine, table, scal]
    return launch(
        functools.partial(unpack_kernel, each=each, plan=plan, orders=bit_orders(batch), vocab=vocab),
        arrays,
        [whole(array.shape) for array in arrays],
        [whole(shape) for shape in shapes],
        [jax.ShapeDtypeStruct(shape, F32) for shape in shapes],
        (1,),
        "unpack_small",
        cost(5),
        prefetch=[where],
        scratch=[pltpu.VMEM((width, model), F32), pltpu.VMEM((rows[3], model), F32)],
    )


def local(
    word_ids, buckets, noise, table, w_in, time_table, pos_table, gain_attn, w_qkv, w_out,
    gain_mlp, w_up, w_down, w_head,
):
    ORDER.clear()
    seq_rows, half_len = word_ids.shape
    table_span, embed_width = table.shape
    model = w_qkv.shape[0]
    bucket_count = time_table.shape[0]
    batch, cores = lax.axis_size("batch"), lax.axis_size("seq")
    devices = batch * cores
    vocab = table_span * devices
    length = half_len * cores
    seqs = seq_rows // cores
    tokens = seqs * length
    me = lax.axis_index("batch").astype(jnp.int32)
    core = lax.axis_index("seq").astype(jnp.int32)
    where = jnp.stack([me, core])

    def regroup(array):
        own = lax.dynamic_slice_in_dim(array, core * seqs, seqs, 0)
        other = swap(lax.dynamic_slice_in_dim(array, (1 - core) * seqs, seqs, 0))
        return jnp.concatenate(
            [jnp.where(core == 0, own, other), jnp.where(core == 0, other, own)], axis=1
        )

    bucket_hot = (buckets[:, None] == jnp.arange(bucket_count, dtype=jnp.int32)[None, :]).astype(F32)
    span = -(-(table_span + 1) // 16) * 16
    behind = jnp.pad(
        jnp.sum(bucket_hot, axis=0).astype(BF)[None, :],
        ((0, span - table_span - 1), (0, embed_width - bucket_count)),
    )
    own_table, other_table = Gather(jnp.concatenate([table, behind], axis=0), batch).finish(True)
    word_list = regroup(word_ids)
    device = lax.div(word_list, table_span)
    row_in = word_list - device * table_span
    owner, its_core = lax.div(device, cores), lax.rem(device, cores)
    orders = bit_orders(batch)
    spot = jnp.where(its_core == 0, place(owner, me, orders[0]), place(owner, me, orders[1]))
    spot = jnp.where(its_core == core, spot, spot + batch)
    ids = (spot * span + row_in).reshape(1, tokens)
    home = (device * span + row_in).reshape(1, tokens)
    noise_rows = regroup(noise).reshape(tokens, embed_width)
    own_buckets = lax.dynamic_slice_in_dim(buckets, core * seqs, seqs, 0)

    gain_a, gain_m = gain_attn.reshape(1, model), gain_mlp.reshape(1, model)
    word, noisy, stream, lefts, packed, scal = embed(
        own_buckets, ids, own_table, other_table, noise_rows, w_in, time_table, pos_table, gain_a,
        w_qkv, table_span,
    )
    lefts, probs, inv = attend(packed, length, lefts)
    mid, mlp, act, slope, low, gpred, branch, ghead = forward(
        scal, lefts, stream, word, w_out, gain_m, w_up, w_down, w_head, length
    )
    pairs = tokens // length * (packed.shape[1] // (6 * HEAD))
    inner = w_up.shape[1]

    def attend_part(first, last, grads):
        return attend_back(packed, gmixed, lefts, inv, probs, length, first, last - first, grads)

    (down,) = outer(where, branch[None], act[None], batch, 512, by_device=True)
    down_sum = lax.psum_scatter(
        down.reshape(devices, *down.shape[2:]), ("batch", "seq"), scatter_dimension=0, tiled=False
    )
    upin, gmid, grads, gmixed, ggain_m = back(
        mid, slope, gpred, branch, w_out, gain_m, w_up, w_down, w_head
    )
    up = Sum(*outer(where, mlp[None], upin[None], batch, 512))
    grads = attend_part(0, pairs // 2, grads)
    up.fold()
    grads = attend_part(pairs // 2, pairs, grads)
    up.fold()
    attn = Sum(*outer(where, lefts, grads, batch))
    down_all = share(rounded(down_sum))
    up.fold()
    gpos, gtime, ggain_a, gwin, grows, gscale = input_back(
        scal, gmid, grads, stream, noisy, word, gpred, gain_a, w_qkv, w_in, length
    )
    up.fold()
    attn.fold()
    small = Sum(
        *pack(
            where, own_buckets, gpos, gwin, ghead, gtime, ggain_a, ggain_m, gscale, home, grows, batch,
            span, bucket_count,
        )
    )
    up_all = share(up.rest())
    attn.fold(micros=25)
    small.fold(F32)
    low = low.reshape(seqs, length, model)
    output = mend(
        where, low, swap(lax.dynamic_slice_in_dim(low, (1 - core) * half_len, half_len, 1))
    )
    grad_down = spread(down_all, batch, model, inner, True)
    attn.fold()
    small.fold(F32)
    attn.fold()
    small.fold(F32)
    attn_all = Gather(attn.finish(), batch)
    small.fold(F32)
    mine = small.finish(F32)
    cut = mine.shape[0] - span
    small_all = Gather(mine[:cut].astype(BF), batch)
    attn_all.join()
    small_all.join()
    attn_all.join()
    small_all.join()
    attn_all.join()
    small_all.join()
    grad_up = spread(up_all, batch, model, inner)
    small_all.join()
    attn_own, attn_other = attn_all.finish()
    small_own, small_other = small_all.finish()
    grad_qkv, grad_out = spread_near(where, attn_own, attn_other, model, (3 * model, model))
    pos_sum, win_sum, head_sum, time_sum, gain_a_sum, gain_m_sum, grad_table = unpack(
        where, small_own, small_other, mine[cut:], table, scal, length, model, bucket_count, vocab
    )
    return (
        output,
        grad_table,
        win_sum,
        time_sum,
        pos_sum,
        gain_a_sum,
        grad_qkv,
        grad_out,
        gain_m_sum,
        grad_up,
        grad_down,
        head_sum,
        scal[0, 4],
    )


def solution(mesh):
    rows = P(("batch", "seq"), None)
    in_specs = (P("batch", "seq"), P("batch"), P("batch", "seq", None), rows) + (P(),) * 10
    out_specs = (P("batch", "seq", None), rows) + (P(),) * 11
    return jax.shard_map(local, mesh=mesh, in_specs=in_specs, out_specs=out_specs, check_vma=False)
```

time: 675 us -> 539 us (0.80)
  the two profiles are of different devices: /device:TPU:0 before, /device:TPU:19 now
where the time goes in v2:
time: 539 us; the launch traced here: 529 us
  Pallas kernels  337 us (63%)
  waiting for transfers between devices  95.8 us (18%)
  starting transfers between devices  43.3 us (8%)
  local copies, waits for them, and re-layouts  31.5 us (6%)
  between operations  14.6 us (3%)
  other arithmetic  6.74 us (1%)
    pallas_call x40, Pallas kernels, launch(): pl.pallas_call(body, grid_spec=pltpu.PrefetchScalarGridSpec(num_scalar_pr...  337 us
    ppermute x24, waiting for transfers between devices, hop(): return lax.ppermute(array, ('batch', 'seq'), pairs)  91.9 us
    ppermute x24, starting transfers between devices, hop(): return lax.ppermute(array, ('batch', 'seq'), pairs)  28.9 us
    unnamed x76, local copies, waits for them, and re-layouts  22.4 us
    ppermute x9, starting transfers between devices, swap(): return lax.ppermute(array, 'seq', [(0, 1), (1, 0)])  14.3 us
  transfers between devices with their start and end apart: 36, of which 17 were waited for; matrix products, arithmetic and copies ran while one was open for 3% of the time, Pallas kernels for 39%

profile of v2, /device:TPU:19, one launch (start us, length us, event | category | flops | bytes accessed | tf_op | source)
XLA Modules:
  0.0 528.8 jit_solution(7708497611320135658)
XLA Ops:
  12.8 1.2 dynamic_slice.18.refs_0_.refs_1_
  14.1 1.3 reshape.205.refs_8_.refs_9_
  15.4 1.3 reshape.206.refs_5_
  17.5 3.4 collective-permute-done.2
  20.9 1.4 collective-permute-start.3
  22.9 1.9 collective-permute-done.3
  24.8 1.3 collective-permute-start.4
  26.1 4.2 collective-permute-done.4
  30.4 3.2 collective-permute-start.5
  36.9 25.5 %embed.1 = (bf16[2048,128]{1,0:T(8,128)(2,1)}, bf16[2048,128]{1,0:T(8,128)(2,1)}, f32[2048,768]{1,0:T(8,128)}, bf16[2,2048,768]{2,1,0:T(8,128)(2,1)}, bf16[2048,...) custom-call(s32[2]{0:T(128)} %dynamic_slice.18.refs_0_.refs_1_, s32[1,2048]{1,0:T(1,128)} %multiply_add_fusion.1.refs_1_, ...), custom_call_target="tpu_custom_call" | custom-call | flops 30720000000 | tf_op jit(solution)/shard_map/embed/pallas_call | solution.py:72
  62.3 41.5 %attend.1 = (bf16[2,2048,768]{2,1,0:T(8,128)(2,1)}, bf16[24,1024,1024]{2,1,0:T(8,128)(2,1)}, f32[2048,768]{1,0:T(8,128)}, f32[8,128]{1,0:T(8,128)}) custom-call(bf16[2048,2304]{1,0:T(8,128)(2,1)} %get-tuple-element.136.refs_0_.refs_1_.refs_2_, bf16[2048,2304]{1,0:T(8,128)(2,1)} %get-tuple-element.136.refs_0_.refs_1_.refs_2_, ...), custom_call_target="tpu_custom_call", output_to_operand_aliasing={{0}: (3, {})} | custom-call | flops 50400002048 | tf_op jit(solution)/shard_map/attend/pallas_call | solution.py:72
  103.8 43.7 %feed_forward.1 = (f32[2048,768]{1,0:T(8,128)}, bf16[2048,768]{1,0:T(8,128)(2,1)}, bf16[2048,3072]{1,0:T(8,128)(2,1)}, bf16[2048,3072]{1,0:T(8,128)(2,1)}, bf16[...) custom-call(f32[8,128]{1,0:T(8,128)} %get-tuple-element.135.refs_0_., ...), custom_call_target="tpu_custom_call" | custom-call | flops 54613331968 | tf_op jit(solution)/shard_map/feed_forward/pallas_call | solution.py:72
  147.5 16.3 %weight_grad.3 = (f32[16,2,48,1536]{3,2,1,0:T(8,128)}, f32[8,128]{1,0:T(8,128)}) custom-call(s32[2]{0:T(128)} %pad_add_fusion.refs_0_, bf16[1,2048,768]{2,1,0:T(8,128)(2,1)} %bitcast.43, bf16[1,2048,3072]{2,1,0:T(8,128)(2,1)} %bitcast.41, f32[8,128]{1,0:T(8,128)} %get-tuple-element.149.refs_3_), custom_call_target="tpu_custom_call" | custom-call | flops 20480000000 | tf_op jit(solution)/shard_map/weight_grad/pallas_call | solution.py:72
  163.9 37.8 %feed_forward_back.1 = (bf16[2048,3072]{1,0:T(8,128)(2,1)}, f32[2048,768]{1,0:T(8,128)}, bf16[4,2048,768]{2,1,0:T(8,128)(2,1)}, bf16[2048,768]{1,0:T(8,128)(2,1)}, f32[1,768]{1,0:T(1,128)}, /*index=5*/f32[8,128]{1,0:T(8,128)}) custom-call(f32[2048,768]{1,0:T(8,128)} %get-tuple-element.144.refs_0_, bf16[2048,3072]{1,0:T(8,128)(2,1)} %get-tuple-element.145.refs_1_, ...), custom_call_target="tpu_custom_call" | custom-call | flops 44683636736 | tf_op jit(solution)/shard_map/feed_forward_back/pallas_call | solution.py:72
  201.7 17.0 %weight_grad.4 = (bf16[16,48,1536]{2,1,0:T(8,128)(2,1)}, bf16[16,48,1536]{2,1,0:T(8,128)(2,1)}, f32[8,128]{1,0:T(8,128)}) custom-call(s32[2]{0:T(128)} %pad_add_fusion.refs_0_, bf16[1,2048,768]{2,1,0:T(8,128)(2,1)} %bitcast.42, bf16[1,2048,3072]{2,1,0:T(8,128)(2,1)} %bitcast.40, f32[8,128]{1,0:T(8,128)} %get-tuple-element.158.refs_3_), custom_call_target="tpu_custom_call" | custom-call | flops 20480000000 | tf_op jit(solution)/shard_map/weight_grad/pallas_call | solution.py:72
  218.6 28.3 %attend_back.2 = (bf16[4,2048,768]{2,1,0:T(8,128)(2,1)}, f32[8,128]{1,0:T(8,128)}) custom-call(bf16[2048,2304]{1,0:T(8,128)(2,1)} %get-tuple-element.136.refs_0_.refs_1_.refs_2_, bf16[2048,2304]{1,0:T(8,128)(2,1)} %get-tuple-element.136.refs_0_.refs_1_.refs_2_, ...), custom_call_target="tpu_custom_call", output_to_operand_aliasing={{0}: (7, {})} | custom-call | flops 32399998976 | tf_op jit(solution)/shard_map/attend_back/pallas_call | solution.py:72
  247.0 1.4 copy-done.3
  248.4 1.7 copy-done.2
  250.0 1.7 copy-done.4
  252.4 1.4 fold.15
  254.5 1.3 collective-permute-start.9
  255.8 28.6 %attend_back.3 = (bf16[4,2048,768]{2,1,0:T(8,128)(2,1)}, f32[8,128]{1,0:T(8,128)}) custom-call(bf16[2048,2304]{1,0:T(8,128)(2,1)} %get-tuple-element.136.refs_0_.refs_1_.refs_2_, bf16[2048,2304]{1,0:T(8,128)(2,1)} %get-tuple-element.136.refs_0_.refs_1_.refs_2_, ...), custom_call_target="tpu_custom_call", output_to_operand_aliasing={{0}: (7, {})} | custom-call | flops 32399998976 | tf_op jit(solution)/shard_map/attend_back/pallas_call | solution.py:72
  286.9 16.7 %weight_grad.5 = (bf16[16,48,1536]{2,1,0:T(8,128)(2,1)}, bf16[16,48,1536]{2,1,0:T(8,128)(2,1)}, f32[8,128]{1,0:T(8,128)}) custom-call(s32[2]{0:T(128)} %pad_add_fusion.refs_0_, bf16[2,2048,768]{2,1,0:T(8,128)(2,1)} %get-tuple-element.139.refs_1_.refs_4_, bf16[4,2048,768]{2,1,0:T(8,128)(2,1)} %get-tuple-element.165.refs_2_.refs_3_.refs_4_, f32[8,128]{1,0:T(8,128)} %copy-done.17), custom_call_target="tpu_custom_call" | custom-call | flops 20480000000 | tf_op jit(solution)/shard_map/weight_grad/pallas_call | solution.py:72
  306.0 1.3 collective-permute-start.10
  308.5 6.6 %collective-permute-done.10.refs_1_ = bf16[4,48,1536]{2,1,0:T(8,128)(2,1)S(1)} collective-permute-done((bf16[4,48,1536]{2,1,0:T(8,128)(2,1)S(1)}, bf16[4,48,1536]{2,1,0:T(8,128)(2,1)S(1)}, u32[]{:S(2)}, u32[]{:S(2)}) %collective-permute-start.10) | collective-permute-done | bytes 589856 | tf_op jit(solution)/shard_map/ppermute | solution.py:600
  316.5 23.6 %input_back.1 = (f32[1024,768]{1,0:T(8,128)}, f32[2,768]{1,0:T(2,128)}, f32[1,768]{1,0:T(1,128)}, f32[128,768]{1,0:T(8,128)}, bf16[2048,128]{1,0:T(8,128)(2,1)}, /*index=5*/f32[1,128]{1,0:T(1,128)}, f32[8,128]{1,0:T(8,128)}) custom-call(f32[8,128]{1,0:T(8,128)} %get-tuple-element.135.refs_0_.refs_5_, f32[2048,768]{1,0:T(8,128)} %get-tuple-element.151.refs_1_, ...), custom_call_target="tpu_custom_call" | custom-call | flops 27306665984 | tf_op jit(solution)/shard_map/input_back/pallas_call | solution.py:72
  342.2 2.7 collective-permute-start.29
  345.0 2.2 fold.19
  347.1 1.4 copy-done.7
  349.1 11.7 %pack_small.1 = (f32[16,416,128]{2,1,0:T(8,128)}, bf16[16,416,128]{2,1,0:T(8,128)(2,1)}, f32[8,128]{1,0:T(8,128)}) custom-call(s32[2]{0:T(128)} %pad_add_fusion.refs_0_, s32[2]{0:T(128)} %dynamic_slice.18.refs_0_.refs_1_, f32[1024,768]{1,0:T(8,128)} %get-tuple-element.175.refs_2_, f32[128,768]{1,0:T(8,128)} %get-tuple-element.176.refs_3_, ...), custom_call_target="tpu_custom_call" | custom-call | flops 14400000000 | tf_op jit(solution)/shard_map/pack_small/pallas_call | solution.py:72
  361.7 1.6 fold.29
  363.7 1.6 constant_dynamic-slice_fusion
  365.4 3.3 collective-permute-start.7
  369.0 9.9 %collective-permute-done.14.refs_1_ = bf16[8,48,1536]{2,1,0:T(8,128)(2,1)} collective-permute-done((bf16[8,48,1536]{2,1,0:T(8,128)(2,1)S(1)}, bf16[8,48,1536]{2,1,0:T(8,128)(2,1)}, u32[]{:S(2)}, u32[]{:S(2)}) %collective-permute-start.14) | collective-permute-done | bytes 1179680 | tf_op jit(solution)/shard_map/ppermute | solution.py:600
  378.9 2.4 fold.20
  381.3 1.3 collective-permute-start.16
  384.9 5.6 %mend.1 = (bf16[4,512,768]{2,1,0:T(8,128)(2,1)}, f32[8,128]{1,0:T(8,128)}) custom-call(s32[2]{0:T(128)} %pad_add_fusion.refs_0_, bf16[2,1024,768]{2,1,0:T(8,128)(2,1)} %bitcast.32, bf16[2,512,768]{2,1,0:T(8,128)(2,1)} %copy-done.34, f32[8,128]{1,0:T(8,128)} %copy-done.16), custom_call_target="tpu_custom_call" | custom-call | flops 7200000000 | tf_op jit(solution)/shard_map/mend/pallas_call | solution.py:72
  390.5 7.5 %spread.2 = (f32[3072,768]{1,0:T(8,128)}, f32[8,128]{1,0:T(8,128)}) custom-call(bf16[16,1,2,48,1536]{4,3,2,1,0:T(8,128)(2,1)} %bitcast.39, f32[8,128]{1,0:T(8,128)} %get-tuple-element.204.refs_1_), custom_call_target="tpu_custom_call" | custom-call | flops 9600000000 | tf_op jit(solution)/shard_map/spread/pallas_call | solution.py:72
  398.0 1.3 copy-done.19
  400.0 1.2 fold.22
  401.1 1.3 collective-permute-done.15.refs_1_
  402.8 1.9 collective-permute-start.18
  404.7 6.3 %collective-permute-done.18.refs_1_ = bf16[2,48,1536]{2,1,0:T(8,128)(2,1)S(1)} collective-permute-done((bf16[2,48,1536]{2,1,0:T(8,128)(2,1)S(1)}, bf16[2,48,1536]{2,1,0:T(8,128)(2,1)S(1)}, u32[]{:S(2)}, u32[]{:S(2)}) %collective-permute-start.18) | collective-permute-done | bytes 294944 | tf_op jit(solution)/shard_map/ppermute | solution.py:600
  411.1 7.0 %collective-permute-done.17.refs_1_ = bf16[4,416,128]{2,1,0:T(8,128)(2,1)S(1)} collective-permute-done((bf16[4,416,128]{2,1,0:T(8,128)(2,1)S(1)}, bf16[4,416,128]{2,1,0:T(8,128)(2,1)S(1)}, u32[]{:S(2)}, u32[]{:S(2)}) %collective-permute-start.17) | collective-permute-done | bytes 426016 | tf_op jit(solution)/shard_map/ppermute | solution.py:600
  419.0 8.8 %collective-permute-done.20.refs_1_ = bf16[1,48,1536]{2,1,0:T(8,128)(2,1)S(1)} collective-permute-done((bf16[1,48,1536]{2,1,0:T(8,128)(2,1)S(1)}, bf16[1,48,1536]{2,1,0:T(8,128)(2,1)S(1)}, u32[]{:S(2)}, u32[]{:S(2)}) %collective-permute-start.20) | collective-permute-done | bytes 147488 | tf_op jit(solution)/shard_map/ppermute | solution.py:600
  428.9 1.4 collective-permute-start.23
  430.3 7.0 %collective-permute-done.21.refs_1_ = bf16[1,416,128]{2,1,0:T(8,128)(2,1)S(1)} collective-permute-done((bf16[1,416,128]{2,1,0:T(8,128)(2,1)S(1)}, bf16[1,416,128]{2,1,0:T(8,128)(2,1)S(1)}, u32[]{:S(2)}, u32[]{:S(2)}) %collective-permute-start.21) | collective-permute-done | bytes 106528 | tf_op jit(solution)/shard_map/ppermute | solution.py:600
  437.3 6.6 %collective-permute-done.23.refs_1_ = bf16[1,48,1536]{2,1,0:T(8,128)(2,1)S(1)} collective-permute-done((bf16[1,48,1536]{2,1,0:T(8,128)(2,1)S(1)}, bf16[1,48,1536]{2,1,0:T(8,128)(2,1)S(1)}, u32[]{:S(2)}, u32[]{:S(2)}) %collective-permute-start.23) | collective-permute-done | bytes 147488 | tf_op jit(solution)/shard_map/ppermute | solution.py:600
  443.9 6.1 %collective-permute-start.25 = (bf16[2,48,1536]{2,1,0:T(8,128)(2,1)S(1)}, bf16[2,48,1536]{2,1,0:T(8,128)(2,1)S(1)}, u32[]{:S(2)}, u32[]{:S(2)}) collective-permute-start(bf16[2,48,1536]{2,1,0:T(8,128)(2,1)S(1)} %get-tuple-element.227.refs_0_), channel_id=1, source_target_pairs={{0,8},{1,3},{2,10},{3,1},{4,12},{5,7},{6,14},{7,5},{8,0},{9,11},{1... | collective-permute-start | bytes 884744 | tf_op jit(solution)/shard_map/ppermute | solution.py:600
  450.0 3.2 collective-permute-start.22
  453.2 1.8 collective-permute-done.22.refs_1_
  455.1 1.9 collective-permute-start.27
  457.8 3.5 collective-permute-done.24.refs_1_
  461.5 3.4 collective-permute-done.27.refs_1_
  465.5 4.2 collective-permute-done.26.refs_1_
  471.1 7.0 %spread.3 = (f32[768,3072]{1,0:T(8,128)}, f32[8,128]{1,0:T(8,128)}) custom-call(bf16[16,1,2,48,1536]{4,3,2,1,0:T(8,128)(2,1)} %bitcast.38, f32[8,128]{1,0:T(8,128)} %copy-done.28), custom_call_target="tpu_custom_call" | custom-call | flops 9600000000 | tf_op jit(solution)/shard_map/spread/pallas_call | solution.py:72
  478.1 15.8 %collective-permute-done.28.refs_1_ = bf16[8,288,128]{2,1,0:T(8,128)(2,1)} collective-permute-done((bf16[8,288,128]{2,1,0:T(8,128)(2,1)S(1)}, bf16[8,288,128]{2,1,0:T(8,128)(2,1)}, u32[]{:S(2)}, u32[]{:S(2)}) %collective-permute-start.28) | collective-permute-done | bytes 589856 | tf_op jit(solution)/shard_map/ppermute | solution.py:600
  494.5 2.1 join.14
  496.9 5.3 %collective-permute-start.32 = (bf16[16,48,1536]{2,1,0:T(8,128)(2,1)S(1)}, bf16[16,48,1536]{2,1,0:T(8,128)(2,1)S(1)}, u32[]{:S(2)}, u32[]{:S(2)}) collective-permute-start(bf16[16,48,1536]{2,1,0:T(8,128)(2,1)S(1)} %get-tuple-element.243.refs_1_), channel_id=1, source_target_pairs={{0,1},{1,0},{2,3},{3,2},{4,5},{5,4},{6,7},{7,6},{8,9},{9,8},{10,11... | collective-permute-start | bytes 7077896 | tf_op jit(solution)/shard_map/ppermute | solution.py:589
  502.3 1.3 slice.12
  504.2 3.9 collective-permute-done.32.refs_2_
  508.1 1.4 copy-done.32
  509.5 7.5 %spread_near.1 = (f32[768,2304]{1,0:T(8,128)}, f32[768,768]{1,0:T(8,128)}, f32[8,128]{1,0:T(8,128)}) custom-call(s32[2]{0:T(128)} %pad_add_fusion.refs_0_, bf16[16,48,1536]{2,1,0:T(8,128)(2,1)} %copy-done.9, bf16[16,48,1536]{2,1,0:T(8,128)(2,1)} %copy-done.32, f32[8,128]{1,0:T(8,128)} %copy-done.13), custom_call_target="tpu_custom_call" | custom-call | flops 9600000000 | tf_op jit(solution)/shard_map/spread_near/pallas_call | solution.py:72
  516.9 4.9 unpack_small.1
  (150 shorter events, 33.3 us)
Async XLA Ops:
  7.2 296.4 %reduce-scatter.2.cloned.1.call-start = ((), (), s32[]{:S(2)}) async-start(), calls=%async_computation.1 | async-start | bytes 9732096 | tf_op jit(solution)/shard_map/reduce_scatter | solution.py:1076
  7.9 8.7 %collective-permute-start = (s32[2,512]{1,0:T(2,128)S(1)}, s32[2,512]{1,0:T(2,128)S(1)}, u32[]{:S(2)}, u32[]{:S(2)}) collective-permute-start(s32[2,512]{1,0:T(2,128)S(1)} %constant_dynamic-slice_fusion.2), channel_id=1, source_target_pairs={{0,1},{1,0},{2,3},{3,2},{4,5},{5,4},{6,7},{7,6},{8,9},{9,8},{10,11... | collective-permute-start | bytes 12296 | tf_op jit(solution)/shard_map/ppermute | solution.py:589
  10.1 7.2 %collective-permute-start.1 = (bf16[1,128,128]{2,1,0:T(8,128)(2,1)S(1)}, bf16[1,128,128]{2,1,0:T(8,128)(2,1)S(1)}, u32[]{:S(2)}, u32[]{:S(2)}) collective-permute-start(bf16[1,128,128]{2,1,0:T(8,128)(2,1)S(1)} %fusion.3), channel_id=1, source_target_pairs={{0,16},{1,17},{2,18},{3,19},{4,20},{5,21},{6,22},{7,23},{8,24},{9,... | collective-permute-start | bytes 98312 | tf_op jit(solution)/shard_map/ppermute | solution.py:600
  11.1 23.1 %collective-permute-start.6 = (bf16[2,512,128]{2,1,0:T(8,128)(2,1)S(1)}, bf16[2,512,128]{2,1,0:T(8,128)(2,1)S(1)}, u32[]{:S(2)}, u32[]{:S(2)}) collective-permute-start(bf16[2,512,128]{2,1,0:T(8,128)(2,1)S(1)} %constant_dynamic-slice_fusion.1), channel_id=1, source_target_pairs={{0,1},{1,0},{2,3},{3,2},{4,5},{5,4},{6,7},{7,6},{8,9},{9,8},{10,11... | collective-permute-start | bytes 786440 | tf_op jit(solution)/shard_map/ppermute | solution.py:589
  17.4 3.5 collective-permute-start.2
  20.9 3.9 collective-permute-start.3
  24.8 5.6 %collective-permute-start.4 = (bf16[8,128,128]{2,1,0:T(8,128)(2,1)S(1)}, bf16[8,128,128]{2,1,0:T(8,128)(2,1)S(1)}, u32[]{:S(2)}, u32[]{:S(2)}) collective-permute-start(bf16[8,128,128]{2,1,0:T(8,128)(2,1)S(1)} %pad_maximum_fusion.1), channel_id=1, source_target_pairs={{0,2},{1,5},{2,0},{3,7},{4,6},{5,1},{6,4},{7,3},{8,10},{9,13},{10,... | collective-permute-start | bytes 786440 | tf_op jit(solution)/shard_map/ppermute | solution.py:600
  30.4 5.7 %copy-start.31 = (bf16[16,128,128]{2,1,0:T(8,128)(2,1)}, bf16[16,128,128]{2,1,0:T(8,128)(2,1)S(1)}, u32[]{:S(2)}) copy-start(bf16[16,128,128]{2,1,0:T(8,128)(2,1)S(1)} %constant_dynamic-update-slice_fusion.refs_2_) | copy-start | bytes 1572868
  30.4 5.7 %collective-permute-start.5 = (bf16[16,128,128]{2,1,0:T(8,128)(2,1)S(1)}, bf16[16,128,128]{2,1,0:T(8,128)(2,1)S(1)}, u32[]{:S(2)}, u32[]{:S(2)}) collective-permute-start(bf16[16,128,128]{2,1,0:T(8,128)(2,1)S(1)} %constant_dynamic-update-slice_fusion.refs_2_), channel_id=1, source_target_pairs={{0,1},{1,0},{2,3},{3,2},{4,5},{5,4},{6,7},{7,6},{8,9},{9,8},{10,11... | collective-permute-start | bytes 1572872 | tf_op jit(solution)/shard_map/ppermute | solution.py:589
  36.1 0.8 copy-start.35
  163.8 226.6 %all-gather.5.cloned.1.call-start = ((), (), s32[]{:S(2)}) async-start(), calls=%async_computation.2 | async-start | bytes 4866048 | tf_op jit(solution)/shard_map/all_gather | solution.py:706
  218.6 28.3 %collective-permute-start.8 = (bf16[16,48,1536]{2,1,0:T(8,128)(2,1)}, bf16[16,48,1536]{2,1,0:T(8,128)(2,1)S(1)}, u32[]{:S(2)}, u32[]{:S(2)}) collective-permute-start(bf16[16,48,1536]{2,1,0:T(8,128)(2,1)} %get-tuple-element.162), channel_id=1, source_target_pairs={{0,1},{1,0},{2,3},{3,2},{4,5},{5,4},{6,7},{7,6},{8,9},{9,8},{10,11... | collective-permute-start | bytes 7077896 | tf_op jit(solution)/shard_map/ppermute | solution.py:589
  247.0 1.4 copy-start.3
  248.4 1.7 copy-start.2
  250.0 1.7 copy-start.4
  251.8 0.7 copy-start.6
  254.5 29.9 %collective-permute-start.9 = (bf16[8,48,1536]{2,1,0:T(8,128)(2,1)}, bf16[8,48,1536]{2,1,0:T(8,128)(2,1)S(1)}, u32[]{:S(2)}, u32[]{:S(2)}) collective-permute-start(bf16[8,48,1536]{2,1,0:T(8,128)(2,1)} %get-tuple-element.168), channel_id=1, source_target_pairs={{0,2},{1,5},{2,0},{3,7},{4,6},{5,1},{6,4},{7,3},{8,10},{9,13},{10,... | collective-permute-start | bytes 3538952 | tf_op jit(solution)/shard_map/ppermute | solution.py:600
  284.4 0.7 copy-start.5
  285.3 1.0 copy-start.10
  286.9 28.2 %copy-start.11 = (f32[4,48,1536]{2,1,0:T(8,128)S(1)}, f32[4,48,1536]{2,1,0:T(8,128)}, u32[]{:S(2)}) copy-start(f32[4,48,1536]{2,1,0:T(8,128)} %copy-done.10) | copy-start | bytes 3538948
  303.6 1.0 copy-start.12
  306.0 165.1 %all-gather.7.cloned.1.call-start = ((), (), s32[]{:S(2)}) async-start(), calls=%async_computation.3 | async-start | bytes 4866048 | tf_op jit(solution)/shard_map/all_gather | solution.py:706
  306.0 9.1 %collective-permute-start.10 = (bf16[4,48,1536]{2,1,0:T(8,128)(2,1)S(1)}, bf16[4,48,1536]{2,1,0:T(8,128)(2,1)S(1)}, u32[]{:S(2)}, u32[]{:S(2)}) collective-permute-start(bf16[4,48,1536]{2,1,0:T(8,128)(2,1)S(1)} %get-tuple-element.171), channel_id=1, source_target_pairs={{0,4},{1,9},{2,6},{3,11},{4,0},{5,13},{6,2},{7,15},{8,12},{9,1},{1... | collective-permute-start | bytes 1769480 | tf_op jit(solution)/shard_map/ppermute | solution.py:600
  307.4 37.6 %collective-permute-start.11 = (bf16[16,48,1536]{2,1,0:T(8,128)(2,1)}, bf16[16,48,1536]{2,1,0:T(8,128)(2,1)}, u32[]{:S(2)}, u32[]{:S(2)}) collective-permute-start(bf16[16,48,1536]{2,1,0:T(8,128)(2,1)} %get-tuple-element.184), channel_id=1, source_target_pairs={{0,1},{1,0},{2,3},{3,2},{4,5},{5,4},{6,7},{7,6},{8,9},{9,8},{10,11... | collective-permute-start | bytes 7077896 | tf_op jit(solution)/shard_map/ppermute | solution.py:589
  315.1 0.7 copy-start.21
  315.9 24.2 %collective-permute-start.12 = (bf16[2,48,1536]{2,1,0:T(8,128)(2,1)S(1)}, bf16[2,48,1536]{2,1,0:T(8,128)(2,1)S(1)}, u32[]{:S(2)}, u32[]{:S(2)}) collective-permute-start(bf16[2,48,1536]{2,1,0:T(8,128)(2,1)S(1)} %get-tuple-element.186), channel_id=1, source_target_pairs={{0,8},{1,3},{2,10},{3,1},{4,12},{5,7},{6,14},{7,5},{8,0},{9,11},{1... | collective-permute-start | bytes 884744 | tf_op jit(solution)/shard_map/ppermute | solution.py:600
  316.5 28.5 %copy-start.1 = (bf16[16,48,1536]{2,1,0:T(8,128)(2,1)S(1)}, bf16[16,48,1536]{2,1,0:T(8,128)(2,1)}, u32[]{:S(2)}) copy-start(bf16[16,48,1536]{2,1,0:T(8,128)(2,1)} %get-tuple-element.183.refs_0_) | copy-start | bytes 7077892
  340.1 0.7 copy-start.27
  341.5 0.7 copy-start.24
  342.2 18.6 %collective-permute-start.29 = (bf16[1,48,1536]{2,1,0:T(8,128)(2,1)}, bf16[1,48,1536]{2,1,0:T(8,128)(2,1)}, u32[]{:S(2)}, u32[]{:S(2)}) collective-permute-start(bf16[1,48,1536]{2,1,0:T(8,128)(2,1)} %get-tuple-element.236), channel_id=1, source_target_pairs={{0,16},{1,17},{2,18},{3,19},{4,20},{5,21},{6,22},{7,23},{8,24},{9,... | collective-permute-start | bytes 442376 | tf_op jit(solution)/shard_map/ppermute | solution.py:600
  347.1 1.4 copy-start.7
  349.1 11.8 %copy-start.25 = (f32[1,48,1536]{2,1,0:T(8,128)S(1)}, f32[1,48,1536]{2,1,0:T(8,128)}, u32[]{:S(2)}) copy-start(f32[1,48,1536]{2,1,0:T(8,128)} %copy-done.24) | copy-start | bytes 884740
  360.9 18.0 %copy-start.8 = (f32[8,48,1536]{2,1,0:T(8,128)S(1)}, f32[8,48,1536]{2,1,0:T(8,128)}, u32[]{:S(2)}) copy-start(f32[8,48,1536]{2,1,0:T(8,128)} %copy-done.7) | copy-start | bytes 7077892
  360.9 0.8 copy-start.29
  361.7 17.2 %copy-start.30 = (f32[8,128]{1,0:T(8,128)S(1)}, f32[8,128]{1,0:T(8,128)}, u32[]{:S(2)}) copy-start(f32[8,128]{1,0:T(8,128)} %get-tuple-element.194.refs_2_) | copy-start | bytes 12292
  363.4 15.5 %collective-permute-start.14 = (bf16[8,48,1536]{2,1,0:T(8,128)(2,1)S(1)}, bf16[8,48,1536]{2,1,0:T(8,128)(2,1)}, u32[]{:S(2)}, u32[]{:S(2)}) collective-permute-start(bf16[8,48,1536]{2,1,0:T(8,128)(2,1)S(1)} %get-tuple-element.193), channel_id=1, source_target_pairs={{0,2},{1,5},{2,0},{3,7},{4,6},{5,1},{6,4},{7,3},{8,10},{9,13},{10,... | collective-permute-start | bytes 3538952 | tf_op jit(solution)/shard_map/ppermute | solution.py:600
  363.7 5.0 copy-start.33
  365.4 18.4 %collective-permute-start.7 = (bf16[2,512,768]{2,1,0:T(8,128)(2,1)S(1)}, bf16[2,512,768]{2,1,0:T(8,128)(2,1)S(1)}, u32[]{:S(2)}, u32[]{:S(2)}) collective-permute-start(bf16[2,512,768]{2,1,0:T(8,128)(2,1)S(1)} %constant_dynamic-slice_fusion), channel_id=1, source_target_pairs={{0,1},{1,0},{2,3},{3,2},{4,5},{5,4},{6,7},{7,6},{8,9},{9,8},{10,11... | collective-permute-start | bytes 4718600 | tf_op jit(solution)/shard_map/ppermute | solution.py:589
  368.7 13.9 %collective-permute-start.13 = (bf16[16,416,128]{2,1,0:T(8,128)(2,1)S(1)}, bf16[16,416,128]{2,1,0:T(8,128)(2,1)S(1)}, u32[]{:S(2)}, u32[]{:S(2)}) collective-permute-start(bf16[16,416,128]{2,1,0:T(8,128)(2,1)S(1)} %copy-done.33), channel_id=1, source_target_pairs={{0,1},{1,0},{2,3},{3,2},{4,5},{5,4},{6,7},{7,6},{8,9},{9,8},{10,11... | collective-permute-start | bytes 5111816 | tf_op jit(solution)/shard_map/ppermute | solution.py:589
  378.9 3.7 copy-start
  381.3 2.4 copy-start.18
  381.3 16.7 %collective-permute-start.16 = (bf16[4,48,1536]{2,1,0:T(8,128)(2,1)}, bf16[4,48,1536]{2,1,0:T(8,128)(2,1)}, u32[]{:S(2)}, u32[]{:S(2)}) collective-permute-start(bf16[4,48,1536]{2,1,0:T(8,128)(2,1)} %get-tuple-element.201), channel_id=1, source_target_pairs={{0,4},{1,9},{2,6},{3,11},{4,0},{5,13},{6,2},{7,15},{8,12},{9,1},{1... | collective-permute-start | bytes 1769480 | tf_op jit(solution)/shard_map/ppermute | solution.py:600
  383.6 18.9 %collective-permute-start.15 = (bf16[8,416,128]{2,1,0:T(8,128)(2,1)S(1)}, bf16[8,416,128]{2,1,0:T(8,128)(2,1)S(1)}, u32[]{:S(2)}, u32[]{:S(2)}) collective-permute-start(bf16[8,416,128]{2,1,0:T(8,128)(2,1)S(1)} %get-tuple-element.199), channel_id=1, source_target_pairs={{0,2},{1,5},{2,0},{3,7},{4,6},{5,1},{6,4},{7,3},{8,10},{9,13},{10,... | collective-permute-start | bytes 2555912 | tf_op jit(solution)/shard_map/ppermute | solution.py:600
  383.7 1.1 copy-start.34
  398.0 1.3 copy-start.19
  402.6 15.5 %collective-permute-start.17 = (bf16[4,416,128]{2,1,0:T(8,128)(2,1)S(1)}, bf16[4,416,128]{2,1,0:T(8,128)(2,1)S(1)}, u32[]{:S(2)}, u32[]{:S(2)}) collective-permute-start(bf16[4,416,128]{2,1,0:T(8,128)(2,1)S(1)} %get-tuple-element.208), channel_id=1, source_target_pairs={{0,4},{1,9},{2,6},{3,11},{4,0},{5,13},{6,2},{7,15},{8,12},{9,1},{1... | collective-permute-start | bytes 1277960 | tf_op jit(solution)/shard_map/ppermute | solution.py:600
  402.8 8.2 %collective-permute-start.18 = (bf16[2,48,1536]{2,1,0:T(8,128)(2,1)S(1)}, bf16[2,48,1536]{2,1,0:T(8,128)(2,1)S(1)}, u32[]{:S(2)}, u32[]{:S(2)}) collective-permute-start(bf16[2,48,1536]{2,1,0:T(8,128)(2,1)S(1)} %get-tuple-element.210), channel_id=1, source_target_pairs={{0,8},{1,3},{2,10},{3,1},{4,12},{5,7},{6,14},{7,5},{8,0},{9,11},{1... | collective-permute-start | bytes 884744 | tf_op jit(solution)/shard_map/ppermute | solution.py:600
  418.2 9.6 %collective-permute-start.19 = (bf16[2,416,128]{2,1,0:T(8,128)(2,1)S(1)}, bf16[2,416,128]{2,1,0:T(8,128)(2,1)S(1)}, u32[]{:S(2)}, u32[]{:S(2)}) collective-permute-start(bf16[2,416,128]{2,1,0:T(8,128)(2,1)S(1)} %get-tuple-element.214), channel_id=1, source_target_pairs={{0,8},{1,3},{2,10},{3,1},{4,12},{5,7},{6,14},{7,5},{8,0},{9,11},{1... | collective-permute-start | bytes 638984 | tf_op jit(solution)/shard_map/ppermute | solution.py:600
  419.0 8.8 %collective-permute-start.20 = (bf16[1,48,1536]{2,1,0:T(8,128)(2,1)S(1)}, bf16[1,48,1536]{2,1,0:T(8,128)(2,1)S(1)}, u32[]{:S(2)}, u32[]{:S(2)}) collective-permute-start(bf16[1,48,1536]{2,1,0:T(8,128)(2,1)S(1)} %get-tuple-element.216), channel_id=1, source_target_pairs={{0,16},{1,17},{2,18},{3,19},{4,20},{5,21},{6,22},{7,23},{8,24},{9,... | collective-permute-start | bytes 442376 | tf_op jit(solution)/shard_map/ppermute | solution.py:600
  427.9 9.4 %collective-permute-start.21 = (bf16[1,416,128]{2,1,0:T(8,128)(2,1)S(1)}, bf16[1,416,128]{2,1,0:T(8,128)(2,1)S(1)}, u32[]{:S(2)}, u32[]{:S(2)}) collective-permute-start(bf16[1,416,128]{2,1,0:T(8,128)(2,1)S(1)} %get-tuple-element.220), channel_id=1, source_target_pairs={{0,16},{1,17},{2,18},{3,19},{4,20},{5,21},{6,22},{7,23},{8,24},{9,... | collective-permute-start | bytes 319496 | tf_op jit(solution)/shard_map/ppermute | solution.py:600
  428.9 15.0 %collective-permute-start.23 = (bf16[1,48,1536]{2,1,0:T(8,128)(2,1)S(1)}, bf16[1,48,1536]{2,1,0:T(8,128)(2,1)S(1)}, u32[]{:S(2)}, u32[]{:S(2)}) collective-permute-start(bf16[1,48,1536]{2,1,0:T(8,128)(2,1)S(1)} %bitcast.28), channel_id=1, source_target_pairs={{0,16},{1,17},{2,18},{3,19},{4,20},{5,21},{6,22},{7,23},{8,24},{9,... | collective-permute-start | bytes 442376 | tf_op jit(solution)/shard_map/ppermute | solution.py:600
  443.9 11.1 %collective-permute-start.25 = (bf16[2,48,1536]{2,1,0:T(8,128)(2,1)S(1)}, bf16[2,48,1536]{2,1,0:T(8,128)(2,1)S(1)}, u32[]{:S(2)}, u32[]{:S(2)}) collective-permute-start(bf16[2,48,1536]{2,1,0:T(8,128)(2,1)S(1)} %get-tuple-element.227.refs_0_), channel_id=1, source_target_pairs={{0,8},{1,3},{2,10},{3,1},{4,12},{5,7},{6,14},{7,5},{8,0},{9,11},{1... | collective-permute-start | bytes 884744 | tf_op jit(solution)/shard_map/ppermute | solution.py:600
  450.0 5.0 collective-permute-start.22
  455.1 9.8 %collective-permute-start.27 = (bf16[4,48,1536]{2,1,0:T(8,128)(2,1)S(1)}, bf16[4,48,1536]{2,1,0:T(8,128)(2,1)S(1)}, u32[]{:S(2)}, u32[]{:S(2)}) collective-permute-start(bf16[4,48,1536]{2,1,0:T(8,128)(2,1)S(1)} %get-tuple-element.231.refs_0_), channel_id=1, source_target_pairs={{0,4},{1,9},{2,6},{3,11},{4,0},{5,13},{6,2},{7,15},{8,12},{9,1},{1... | collective-permute-start | bytes 1769480 | tf_op jit(solution)/shard_map/ppermute | solution.py:600
  457.1 4.3 collective-permute-start.24
  461.4 8.3 %collective-permute-start.26 = (bf16[4,288,128]{2,1,0:T(8,128)(2,1)S(1)}, bf16[4,288,128]{2,1,0:T(8,128)(2,1)S(1)}, u32[]{:S(2)}, u32[]{:S(2)}) collective-permute-start(bf16[4,288,128]{2,1,0:T(8,128)(2,1)S(1)} %get-tuple-element.230.refs_0_), channel_id=1, source_target_pairs={{0,4},{1,9},{2,6},{3,11},{4,0},{5,13},{6,2},{7,15},{8,12},{9,1},{1... | collective-permute-start | bytes 884744 | tf_op jit(solution)/shard_map/ppermute | solution.py:600
  465.0 31.7 %collective-permute-start.31 = (bf16[8,48,1536]{2,1,0:T(8,128)(2,1)S(1)}, bf16[8,48,1536]{2,1,0:T(8,128)(2,1)S(1)}, u32[]{:S(2)}, u32[]{:S(2)}) collective-permute-start(bf16[8,48,1536]{2,1,0:T(8,128)(2,1)S(1)} %get-tuple-element.241.refs_0_), channel_id=1, source_target_pairs={{0,2},{1,5},{2,0},{3,7},{4,6},{5,1},{6,4},{7,3},{8,10},{9,13},{10,... | collective-permute-start | bytes 3538952 | tf_op jit(solution)/shard_map/ppermute | solution.py:600
  470.3 23.5 %collective-permute-start.28 = (bf16[8,288,128]{2,1,0:T(8,128)(2,1)S(1)}, bf16[8,288,128]{2,1,0:T(8,128)(2,1)}, u32[]{:S(2)}, u32[]{:S(2)}) collective-permute-start(bf16[8,288,128]{2,1,0:T(8,128)(2,1)S(1)} %get-tuple-element.234.refs_0_), channel_id=1, source_target_pairs={{0,2},{1,5},{2,0},{3,7},{4,6},{5,1},{6,4},{7,3},{8,10},{9,13},{10,... | collective-permute-start | bytes 1769480 | tf_op jit(solution)/shard_map/ppermute | solution.py:600
  493.9 0.7 copy-start.26
  496.9 7.3 %copy-start.9 = (bf16[16,48,1536]{2,1,0:T(8,128)(2,1)}, bf16[16,48,1536]{2,1,0:T(8,128)(2,1)S(1)}, u32[]{:S(2)}) copy-start(bf16[16,48,1536]{2,1,0:T(8,128)(2,1)S(1)} %get-tuple-element.243.refs_1_) | copy-start | bytes 7077892
  496.9 11.2 %copy-start.13 = (f32[8,128]{1,0:T(8,128)}, f32[8,128]{1,0:T(8,128)S(1)}, u32[]{:S(2)}) copy-start(f32[8,128]{1,0:T(8,128)S(1)} %get-tuple-element.244.refs_3_) | copy-start | bytes 12292
  496.9 11.2 %collective-permute-start.32 = (bf16[16,48,1536]{2,1,0:T(8,128)(2,1)S(1)}, bf16[16,48,1536]{2,1,0:T(8,128)(2,1)S(1)}, u32[]{:S(2)}, u32[]{:S(2)}) collective-permute-start(bf16[16,48,1536]{2,1,0:T(8,128)(2,1)S(1)} %get-tuple-element.243.refs_1_), channel_id=1, source_target_pairs={{0,1},{1,0},{2,3},{3,2},{4,5},{5,4},{6,7},{7,6},{8,9},{9,8},{10,11... | collective-permute-start | bytes 7077896 | tf_op jit(solution)/shard_map/ppermute | solution.py:589
  502.2 14.7 %collective-permute-start.30 = (bf16[16,288,128]{2,1,0:T(8,128)(2,1)}, bf16[16,288,128]{2,1,0:T(8,128)(2,1)}, u32[]{:S(2)}, u32[]{:S(2)}) collective-permute-start(bf16[16,288,128]{2,1,0:T(8,128)(2,1)} %get-tuple-element.240.refs_1_), channel_id=1, source_target_pairs={{0,1},{1,0},{2,3},{3,2},{4,5},{5,4},{6,7},{7,6},{8,9},{9,8},{10,11... | collective-permute-start | bytes 3538952 | tf_op jit(solution)/shard_map/ppermute | solution.py:589
  508.1 1.4 copy-start.32
  (8 other events, 4.9 us)
Sparse Core Ops, SparseCore 0:
  164.0 138.1 reduce-scatter.1
  306.1 67.2 all-gather.4
  377.3 75.1 all-gather.6

commit v3 on v2

--- a/solution.py
+++ b/solution.py
@@ -14,7 +14,7 @@
 NN = (((1,), (0,)), ((), ()))
 NT = (((1,), (1,)), ((), ()))
 TN = (((0,), (0,)), ((), ()))
-VMEM_BYTES = 60 * 2**20
+VMEM_BYTES = 50 * 2**20
 GELU_A = math.sqrt(2 / math.pi)
 GELU_B = 0.044715
 
@@ -68,13 +68,13 @@
         refs[at + outs][...] = jnp.zeros((8, 128), F32)
         kernel(*refs[:count], *refs[at : at + outs], *refs[at + outs + 1 :])
 
-    token = pl.BlockSpec((8, 128), lambda *_: (0, 0))
+    token = pl.BlockSpec((8, 128), lambda *_: (0, 0)) if grid else resident(1)[0]
     *results, last = pl.pallas_call(
         body,
         grid_spec=pltpu.PrefetchScalarGridSpec(
             num_scalar_prefetch=len(prefetch),
             grid=grid,
-            in_specs=list(in_specs) + [whole((8, 128))] * waits,
+            in_specs=list(in_specs) + anywhere(waits),
             out_specs=list(out_specs) + [token],
             scratch_shapes=list(scratch),
         ),
@@ -89,6 +89,10 @@
     return results
 
 
+def resident(count):
+    return [pl.BlockSpec(memory_space=pltpu.VMEM)] * count
+
+
 def anywhere(count):
     return [pl.BlockSpec(memory_space=pl.ANY)] * count
 
@@ -108,12 +112,13 @@
 
 
 def embed_kernel(
-    buckets, ids_ref, own_ref, other_ref, noise_ref, win_ref, time_ref, pos_ref, gain_ref, wqkv_ref,
+    where, buckets, ids_ref, own_ref, other_ref, noise_ref, win_ref, time_ref, pos_ref, gain_ref, wqkv_ref,
     word_ref, noisy_ref, stream_ref, left_ref, packed_ref, scal_ref, table_ref,
     *, tiles, table_span, seqs, step,
 ):
     index = pl.program_id(0)
     seq = index // tiles
+    first = where[1] * seqs
     chunks, span, width = own_ref.shape
     bucket_count = time_ref.shape[0]
 
@@ -135,7 +140,7 @@
         lane = lax.broadcasted_iota(jnp.int32, (1, width), 1)
         scal_ref[...] = jnp.zeros_like(scal_ref)
         for each in range(seqs):
-            bucket = buckets[each]
+            bucket = buckets[first + each]
             signal, spread = jnp.float32(0.0), jnp.float32(0.0)
             for kind in range(bucket_count):
                 angle = math.pi / 2 * (kind + 1.0) / (bucket_count + 1)
@@ -159,33 +164,34 @@
     clean = word * scal[:, 3:4]
     noisy = (scal[:, 0:1] * clean + scal[:, 1:2] * noise_ref[...].astype(F32)).astype(BF)
     noisy_ref[...] = noisy
-    stream = dot(noisy, win_ref[...]) + time_ref[pl.ds(buckets[seq], 1), :] + pos_ref[...]
+    stream = dot(noisy, win_ref[...]) + time_ref[pl.ds(buckets[first + seq], 1), :] + pos_ref[...]
     stream_ref[...] = stream
-    attn = (normalise(stream)[0] * gain_ref[...]).astype(BF)
+    attn = (normalise(stream)[0] * gain_ref[...].reshape(1, -1)).astype(BF)
     left_ref[0] = attn
     packed_ref[...] = dot(attn, wqkv_ref[...]).astype(BF)
 
 
-def embed(buckets, ids, own, other, noise, w_in, time_table, pos_table, gain, w_qkv, table_span, tm=256):
+def embed(buckets, ids, own, other, noise, w_in, time_table, pos_table, gain, w_qkv, table_span, where, tm=256):
     tokens, width = noise.shape
     length, model = pos_table.shape
     seqs, tiles = tokens // length, length // tm
     wide = w_qkv.shape[1]
     rows = 2 * own.shape[0] * own.shape[1]
-    row = lambda cols: pl.BlockSpec((tm, cols), lambda i: (i, 0))
+    row = lambda cols: pl.BlockSpec((tm, cols), lambda i, *_: (i, 0))
     return launch(
         functools.partial(
             embed_kernel, tiles=tiles, table_span=table_span, seqs=seqs, step=min(rows, 1024)
         ),
-        [buckets, ids, own, other, noise, w_in, time_table, pos_table, gain, w_qkv],
-        [
-            smem(), pl.BlockSpec((1, tm), lambda i: (0, i)), whole(own.shape), whole(other.shape),
+        [ids, own, other, noise, w_in, time_table, pos_table, gain, w_qkv],
+        [
+            pl.BlockSpec((1, tm), lambda i, *_: (0, i)), whole(own.shape), whole(other.shape),
             row(width), whole(w_in.shape), whole(time_table.shape),
-            pl.BlockSpec((tm, model), lambda i: (i % tiles, 0)), whole(gain.shape), whole(w_qkv.shape),
-        ],
-        [
-            row(width), row(width), row(model), pl.BlockSpec((1, tm, model), lambda i: (0, i, 0)),
-            row(wide), pl.BlockSpec((8, width), lambda i: (0, 0)),
+            pl.BlockSpec((tm, model), lambda i, *_: (i % tiles, 0)), whole(gain.shape),
+            whole(w_qkv.shape),
+        ],
+        [
+            row(width), row(width), row(model), pl.BlockSpec((1, tm, model), lambda i, *_: (0, i, 0)),
+            row(wide), pl.BlockSpec((8, width), lambda *_: (0, 0)),
         ],
         [
             jax.ShapeDtypeStruct((tokens, width), BF),
@@ -198,6 +204,7 @@
         (tokens // tm,),
         "embed",
         cost(tokens / 80),
+        prefetch=[where, buckets],
         scratch=[pltpu.VMEM((width, rows), BF)],
     )
 
@@ -309,21 +316,21 @@
         [jax.ShapeDtypeStruct(held.shape, BF)],
         (count,),
         "attend_back",
-        cost(4.5 * count),
+        cost(4.5 * count), limit=34 * 2**20,
         aliases={7: 0},
     )[0]
 
 
 def forward_kernel(
-    scal_ref, mixed_ref, stream_ref, word_ref, wout_ref, gain_ref, wup_ref, wdown_ref, whead_ref,
-    mid_ref, mlp_ref, act_ref, slope_ref, out_ref, gpred_ref, branch_ref, ghead_ref,
+    where, scal_ref, mixed_ref, stream_ref, word_ref, wout_ref, gain_ref, wup_ref, wdown_ref, whead_ref,
+    mid_ref, mlp_ref, act_ref, slope_ref, ours_ref, theirs_ref, gpred_ref, branch_ref, ghead_ref,
     *, tiles, step,
 ):
     index = pl.program_id(0)
     seq = index // tiles
     mid = stream_ref[...] + dot(mixed_ref[0], wout_ref[...])
     mid_ref[...] = mid
-    mlp = (normalise(mid)[0] * gain_ref[...]).astype(BF)
+    mlp = (normalise(mid)[0] * gain_ref[...].reshape(1, -1)).astype(BF)
     mlp_ref[...] = mlp
     total = mid
     for start in range(0, wup_ref.shape[1], step):
@@ -338,7 +345,16 @@
         slope_ref[:, cols] = slope.astype(BF)
         total = total + dot(act, wdown_ref[cols, :])
     low = total.astype(BF)
-    out_ref[...] = low
+    half = (index % tiles) // (tiles // 2)
+
+    @pl.when(half == where[1])
+    def _():
+        ours_ref[0] = low
+
+    @pl.when(half != where[1])
+    def _():
+        theirs_ref[0] = low
+
     scal = scal_ref[pl.ds(seq, 1), :]
     clean = word_ref[...].astype(F32) * scal[:, 3:4]
     gpred = (dot(low, whead_ref[...]) - clean) * scal[:, 2:3]
@@ -348,31 +364,37 @@
     accumulate(ghead_ref, index == 0, dot(gpred.T.astype(BF), low))
 
 
-def forward(scal, lefts, stream, word, w_out, gain, w_up, w_down, w_head, length, tm=256, step=768):
+def forward(where, scal, lefts, stream, word, w_out, gain, w_up, w_down, w_head, length, tm=256, step=768):
     tokens, model = stream.shape
     inner, width = w_up.shape[1], w_head.shape[1]
-    row = lambda cols: pl.BlockSpec((tm, cols), lambda i: (i, 0))
+    row = lambda cols: pl.BlockSpec((tm, cols), lambda i, *_: (i, 0))
     shape = lambda cols, kind: jax.ShapeDtypeStruct((tokens, cols), kind)
-    return launch(
-        functools.partial(forward_kernel, tiles=length // tm, step=step),
+    tiles = length // tm
+    turn = lambda i, core: (i // tiles, jnp.clip(i % tiles - core * (tiles // 2), 0, tiles // 2 - 1), 0)
+    halves = jax.ShapeDtypeStruct((tokens // length, length // 2, model), BF)
+    return launch(
+        functools.partial(forward_kernel, tiles=tiles, step=step),
         [scal, lefts, stream, word, w_out, gain, w_up, w_down, w_head],
         [
-            whole(scal.shape), pl.BlockSpec((1, tm, model), lambda i: (1, i, 0)), row(model), row(width),
+            whole(scal.shape), pl.BlockSpec((1, tm, model), lambda i, *_: (1, i, 0)), row(model), row(width),
             whole(w_out.shape), whole(gain.shape), whole(w_up.shape), whole(w_down.shape),
             whole(w_head.shape),
         ],
         [
-            row(model), row(model), row(inner), row(inner), row(model), row(width), row(model),
-            pl.BlockSpec((width, model), lambda i: (0, 0)),
+            row(model), row(model), row(inner), row(inner),
+            pl.BlockSpec((1, tm, model), lambda i, w: turn(i, w[1])),
+            pl.BlockSpec((1, tm, model), lambda i, w: turn(i, 1 - w[1])), row(width), row(model),
+            pl.BlockSpec((width, model), lambda *_: (0, 0)),
         ],
         [
             shape(model, F32), shape(model, BF), shape(inner, BF), shape(inner, BF),
-            shape(model, BF), shape(width, F32), shape(model, BF),
+            halves, halves, shape(width, F32), shape(model, BF),
             jax.ShapeDtypeStruct((width, model), F32),
         ],
         (tokens // tm,),
         "feed_forward",
         cost(tokens / 45),
+        prefetch=[where],
     )
 
 
@@ -389,7 +411,7 @@
         upin_ref[:, cols] = upin
         part = dot(upin, wup_ref[:, cols], NT)
         grad = part if grad is None else grad + part
-    part, gain_part = norm_back(mid_ref[...], gain_ref[...], grad)
+    part, gain_part = norm_back(mid_ref[...], gain_ref[...].reshape(1, -1), grad)
     accumulate(ggain_ref, index == 0, gain_part)
     gmid = dot(gpred_ref[...].astype(BF), whead_ref[...], NT) + part
     gmid_ref[...] = gmid
@@ -436,7 +458,7 @@
         + dot(dk_ref[0], wqkv_ref[:, model : 2 * model], NT)
         + dot(dv_ref[0], wqkv_ref[:, 2 * model :], NT)
     )
-    part, gain_part = norm_back(stream_ref[...], gain_ref[...], grad)
+    part, gain_part = norm_back(stream_ref[...], gain_ref[...].reshape(1, -1), grad)
     accumulate(ggain_ref, first, gain_part)
     gin = gmid_ref[...] + part
     accumulate(gpos_ref, seq == 0, gin)
@@ -487,7 +509,7 @@
         ],
         (tiles, seqs),
         "input_back",
-        cost(tokens / 90),
+        cost(tokens / 90), limit=34 * 2**20,
     )
 
 
@@ -616,8 +638,7 @@
     else:
         shapes = [jax.ShapeDtypeStruct(tail, last)]
     out = launch(
-        fold_kernel, [keep, got], [whole(keep.shape), whole(got.shape)],
-        [whole(shape.shape) for shape in shapes], shapes, (1,), "fold", cost(micros),
+        fold_kernel, [keep, got], resident(2), resident(len(shapes)), shapes, (), "fold", cost(micros),
         limit=8 * 2**20 + 12 * keep.size, chained=chained,
     )
     return out if count else out[0]
@@ -640,11 +661,11 @@
     out_ref[count:] = got_ref[...]
 
 
-def join(held, got):
+def join(held, got, micros):
     shape = (2 * held.shape[0], *held.shape[1:])
     return launch(
-        join_kernel, [held, got], [whole(held.shape)] * 2, [whole(shape)],
-        [jax.ShapeDtypeStruct(shape, held.dtype)], (1,), "join", cost(0.4),
+        join_kernel, [held, got], resident(2), resident(1),
+        [jax.ShapeDtypeStruct(shape, held.dtype)], (), "join", cost(micros),
         limit=8 * 2**20 + 8 * held.size,
     )[0]
 
@@ -666,11 +687,6 @@
             self.keep = out[1]
             self.got = hop(out[0], self.step)
 
-    def rest(self):
-        while self.step < self.steps - 1:
-            self.fold()
-        return fold(self.keep, self.got, chained=False)
-
     def finish(self, last=BF):
         while self.chunk is None:
             self.fold(last)
@@ -683,13 +699,13 @@
         self.steps = list(reversed(range(batch.bit_length() - 1)))
         self.got = hop(self.held, self.steps[0])
 
-    def join(self, plain=False):
+    def join(self, plain=False, micros=0.4):
         if self.other is not None:
             return
         if plain:
             self.held = jnp.concatenate([self.held, self.got], axis=0)
         else:
-            self.held = join(self.held, self.got)
+            self.held = join(self.held, self.got, micros)
         self.steps.pop(0)
         if self.steps:
             self.got = hop(self.held, self.steps[0])
@@ -725,14 +741,14 @@
         functools.partial(mend_kernel, seqs=seqs),
         [own, other],
         [
-            pl.BlockSpec(block, lambda i, w: (i % seqs, w[1], 0)),
+            pl.BlockSpec(block, lambda i, w: (i % seqs, 0, 0)),
             pl.BlockSpec(block, lambda i, w: (i % seqs, 0, 0)),
         ],
         [pl.BlockSpec(block, lambda i, w: (i, 0, 0))],
         [jax.ShapeDtypeStruct((2 * seqs, half_len, model), BF)],
         (2 * seqs,),
         "mend",
-        cost(6),
+        cost(6), limit=16 * 2**20,
         prefetch=[where],
     )[0]
 
@@ -765,13 +781,11 @@
         [jax.ShapeDtypeStruct((cols, rows) if flip else (rows, cols), F32)],
         (cols // tw,),
         "spread",
-        cost(8),
+        cost(8), limit=20 * 2**20,
     )[0]
 
 
-def spread_near_kernel(
-    where, own_ref, other_ref, first_ref, second_ref, *, steps, orders, row_blocks, split
-):
+def spread_near_kernel(where, own_ref, other_ref, *outs, steps, orders, row_blocks, splits):
     me, core = where[0], where[1]
     chunks, rows, tw = own_ref.shape
     col_blocks = chunks // row_blocks
@@ -786,9 +800,11 @@
             out_ref[row * rows : (row + 1) * rows, :] = ref[spot].astype(F32)
 
     for ours in (True, False):
-        for out_ref, wanted in ((first_ref, tile < split), (second_ref, tile >= split)):
-
-            @pl.when(jnp.logical_and((step < steps) == ours, wanted))
+        for out_ref, first, last in zip(outs, splits[:-1], splits[1:]):
+
+            @pl.when(
+                jnp.logical_and((step < steps) == ours, jnp.logical_and(tile >= first, tile < last))
+            )
             def _():
                 if ours:
                     write(own_ref, core, out_ref)
@@ -801,14 +817,21 @@
     row_blocks = rows // chunk_rows
     tw = next(size for size in (768, 512, 384, 256, 128) if chunk_cols % size == 0)
     steps, per = sum(widths) // 2 // tw, chunk_cols // tw
-    split, rest = widths[0] // tw, widths[1] // tw
+    splits = [sum(widths[:index]) // tw for index in range(len(widths) + 1)]
     tile = lambda i, w: jnp.where(i < steps, w[1], 1 - w[1]) * steps + i % steps
-    second = lambda i, w: jnp.where(
-        tile(i, w) >= split, tile(i, w) - split, jnp.where(i < steps, 0, rest - 1)
-    )
+
+    def column(first, last):
+        def pick(i, w):
+            at = tile(i, w)
+            idle = jnp.where(i < steps, 0, last - first - 1) if first else last - 1
+            return (0, jnp.where(jnp.logical_and(at >= first, at < last), at - first, idle))
+
+        return pick
+
     return launch(
         functools.partial(
-            spread_near_kernel, steps=steps, orders=bit_orders(batch), row_blocks=row_blocks, split=split
+            spread_near_kernel, steps=steps, orders=bit_orders(batch), row_blocks=row_blocks,
+            splits=splits,
         ),
         [own, other],
         [
@@ -820,13 +843,13 @@
             ),
         ],
         [
-            pl.BlockSpec((rows, tw), lambda i, w: (0, jnp.minimum(tile(i, w), split - 1))),
-            pl.BlockSpec((rows, tw), lambda i, w: (0, second(i, w))),
+            pl.BlockSpec((rows, tw), column(first, last))
+            for first, last in zip(splits[:-1], splits[1:])
         ],
         [jax.ShapeDtypeStruct((rows, width), F32) for width in widths],
         (2 * steps,),
         "spread_near",
-        cost(8),
+        cost(8), limit=24 * 2**20,
         prefetch=[where],
     )
 
@@ -855,7 +878,7 @@
     panels = gpos_ref.shape[1] // 128
     extra_ref[...] = jnp.zeros_like(extra_ref)
     for seq in range(gtime_ref.shape[0]):
-        extra_ref[pl.ds(buckets[seq], 1), :] += gtime_ref[seq : seq + 1, :]
+        extra_ref[pl.ds(buckets[core * gtime_ref.shape[0] + seq], 1), :] += gtime_ref[seq : seq + 1, :]
     extra_ref[buckets_in : buckets_in + 1, :] = ggain_a_ref[...]
     extra_ref[buckets_in + 1 : buckets_in + 2, :] = ggain_m_ref[...]
     extra_ref[buckets_in + 2 : buckets_in + 3, :128] = gscale_ref[...]
@@ -938,7 +961,7 @@
         [jax.ShapeDtypeStruct(shape, F32), jax.ShapeDtypeStruct(shape, BF)],
         (1,),
         "pack_small",
-        cost(12),
+        cost(12), limit=34 * 2**20,
         prefetch=[where, buckets],
         scratch=[pltpu.VMEM((rows[3], model), F32)],
     )
@@ -1006,7 +1029,7 @@
         [jax.ShapeDtypeStruct(shape, F32) for shape in shapes],
         (1,),
         "unpack_small",
-        cost(5),
+        cost(5), limit=24 * 2**20,
         prefetch=[where],
         scratch=[pltpu.VMEM((width, model), F32), pltpu.VMEM((rows[3], model), F32)],
     )
@@ -1055,16 +1078,14 @@
     ids = (spot * span + row_in).reshape(1, tokens)
     home = (device * span + row_in).reshape(1, tokens)
     noise_rows = regroup(noise).reshape(tokens, embed_width)
-    own_buckets = lax.dynamic_slice_in_dim(buckets, core * seqs, seqs, 0)
-
-    gain_a, gain_m = gain_attn.reshape(1, model), gain_mlp.reshape(1, model)
+
     word, noisy, stream, lefts, packed, scal = embed(
-        own_buckets, ids, own_table, other_table, noise_rows, w_in, time_table, pos_table, gain_a,
-        w_qkv, table_span,
+        buckets, ids, own_table, other_table, noise_rows, w_in, time_table, pos_table, gain_attn,
+        w_qkv, table_span, where,
     )
     lefts, probs, inv = attend(packed, length, lefts)
-    mid, mlp, act, slope, low, gpred, branch, ghead = forward(
-        scal, lefts, stream, word, w_out, gain_m, w_up, w_down, w_head, length
+    mid, mlp, act, slope, ours, theirs, gpred, branch, ghead = forward(
+        where, scal, lefts, stream, word, w_out, gain_mlp, w_up, w_down, w_head, length
     )
     pairs = tokens // length * (packed.shape[1] // (6 * HEAD))
     inner = w_up.shape[1]
@@ -1077,51 +1098,50 @@
         down.reshape(devices, *down.shape[2:]), ("batch", "seq"), scatter_dimension=0, tiled=False
     )
     upin, gmid, grads, gmixed, ggain_m = back(
-        mid, slope, gpred, branch, w_out, gain_m, w_up, w_down, w_head
-    )
+        mid, slope, gpred, branch, w_out, gain_mlp, w_up, w_down, w_head
+    )
+    sizes = [0, pairs // 3, pairs * 2 // 3, pairs]
     up = Sum(*outer(where, mlp[None], upin[None], batch, 512))
-    grads = attend_part(0, pairs // 2, grads)
-    up.fold()
-    grads = attend_part(pairs // 2, pairs, grads)
-    up.fold()
+    for part in range(3):
+        grads = attend_part(sizes[part], sizes[part + 1], grads)
+        up.fold()
     attn = Sum(*outer(where, lefts, grads, batch))
+    up.fold(micros=25)
     down_all = share(rounded(down_sum))
-    up.fold()
+    attn.fold()
+    up_all = Gather(up.finish(), batch)
     gpos, gtime, ggain_a, gwin, grows, gscale = input_back(
-        scal, gmid, grads, stream, noisy, word, gpred, gain_a, w_qkv, w_in, length
-    )
-    up.fold()
+        scal, gmid, grads, stream, noisy, word, gpred, gain_attn, w_qkv, w_in, length
+    )
     attn.fold()
+    up_all.join()
     small = Sum(
         *pack(
-            where, own_buckets, gpos, gwin, ghead, gtime, ggain_a, ggain_m, gscale, home, grows, batch,
+            where, buckets, gpos, gwin, ghead, gtime, ggain_a, ggain_m, gscale, home, grows, batch,
             span, bucket_count,
         )
     )
-    up_all = share(up.rest())
-    attn.fold(micros=25)
+    attn.fold()
+    up_all.join(micros=25)
     small.fold(F32)
-    low = low.reshape(seqs, length, model)
-    output = mend(
-        where, low, swap(lax.dynamic_slice_in_dim(low, (1 - core) * half_len, half_len, 1))
-    )
-    grad_down = spread(down_all, batch, model, inner, True)
-    attn.fold()
+    output = mend(where, ours, swap(theirs))
     small.fold(F32)
     attn.fold()
+    up_all.join()
     small.fold(F32)
     attn_all = Gather(attn.finish(), batch)
+    grad_down = spread(down_all, batch, model, inner, True)
+    attn_all.join()
     small.fold(F32)
+    up_own, up_other = up_all.finish()
     mine = small.finish(F32)
     cut = mine.shape[0] - span
     small_all = Gather(mine[:cut].astype(BF), batch)
     attn_all.join()
     small_all.join()
-    attn_all.join()
     small_all.join()
     attn_all.join()
-    small_all.join()
-    grad_up = spread(up_all, batch, model, inner)
+    (grad_up,) = spread_near(where, up_own, up_other, model, (inner,))
     small_all.join()
     attn_own, attn_other = attn_all.finish()
     small_own, small_other = small_all.finish()

time: 539 us -> 484 us (0.90)
  the two profiles are of different devices: /device:TPU:19 before, /device:TPU:0 now
where the time goes in v3:
time: 484 us; the launch traced here: 474 us
  Pallas kernels  315 us (65%)
  waiting for transfers between devices  78.8 us (16%)
  starting transfers between devices  48.1 us (10%)
  between operations  15.1 us (3%)
  local copies, waits for them, and re-layouts  14.5 us (3%)
    pallas_call x45, Pallas kernels, launch(): pl.pallas_call(body, grid_spec=pltpu.PrefetchScalarGridSpec(num_scalar_pr...  315 us
    ppermute x28, waiting for transfers between devices, hop(): return lax.ppermute(array, ('batch', 'seq'), pairs)  71.2 us
    ppermute x28, starting transfers between devices, hop(): return lax.ppermute(array, ('batch', 'seq'), pairs)  42.2 us
    unnamed x68, local copies, waits for them, and re-layouts  12.1 us
  transfers between devices with their start and end apart: 40, of which 18 were waited for; matrix products, arithmetic and copies ran while one was open for 1% of the time, Pallas kernels for 38%

profile of v3, /device:TPU:0, one launch (start us, length us, event | category | flops | bytes accessed | tf_op | source)
XLA Modules:
  0.0 474.2 jit_solution(166247148987228678)
XLA Ops:
  9.2 0.8 fusion.3
  10.0 3.7 collective-permute-start.1
  13.6 1.0 constant_dynamic-slice_fusion
  16.5 1.6 collective-permute-start.2
  18.1 2.7 collective-permute-done.2
  20.8 1.6 collective-permute-start.3
  22.4 3.4 collective-permute-done.3
  25.9 1.6 collective-permute-start.4
  27.5 4.8 %collective-permute-done.4 = bf16[8,128,128]{2,1,0:T(8,128)(2,1)S(1)} collective-permute-done((bf16[8,128,128]{2,1,0:T(8,128)(2,1)S(1)}, bf16[8,128,128]{2,1,0:T(8,128)(2,1)S(1)}, u32[]{:S(2)}, u32[]{:S(2)}) %collective-permute-start.4) | collective-permute-done | bytes 262176 | tf_op jit(solution)/shard_map/ppermute | solution.py:622
  32.6 1.7 collective-permute-done.5.refs_4_
  34.4 25.3 %embed.1 = (bf16[2048,128]{1,0:T(8,128)(2,1)S(1)}, bf16[2048,128]{1,0:T(8,128)(2,1)S(1)}, f32[2048,768]{1,0:T(8,128)}, bf16[2,2048,768]{2,1,0:T(8,128)(2,1)}, bf...) custom-call(s32[2]{0:T(128)S(1)} %pad_add_fusion.refs_0_, s32[4]{0:T(128)S(1)} %copy-done.14, ...), custom_call_target="tpu_custom_call" | custom-call | flops 30720000000 | tf_op jit(solution)/shard_map/embed/pallas_call | solution.py:72
  59.7 41.9 %attend.1 = (bf16[2,2048,768]{2,1,0:T(8,128)(2,1)}, bf16[24,1024,1024]{2,1,0:T(8,128)(2,1)}, f32[2048,768]{1,0:T(8,128)}, f32[8,128]{1,0:T(8,128)S(1)}) custom-call(bf16[2048,2304]{1,0:T(8,128)(2,1)} %get-tuple-element.148.refs_0_.refs_1_.refs_2_, bf16[2048,2304]{1,0:T(8,128)(2,1)} %get-tuple-element.148.refs_0_.refs_1_.refs_2_, ...), custom_call_target="tpu_custom_call", output_to_operand_aliasing={{0}: (3, {})} | custom-call | flops 50400002048 | tf_op jit(solution)/shard_map/attend/pallas_call | solution.py:72
  101.7 46.2 %feed_forward.1 = (f32[2048,768]{1,0:T(8,128)}, bf16[2048,768]{1,0:T(8,128)(2,1)}, bf16[2048,3072]{1,0:T(8,128)(2,1)}, bf16[2048,3072]{1,0:T(8,128)(2,1)}, bf16[...) custom-call(s32[2]{0:T(128)S(1)} %pad_add_fusion.refs_0_, ...), custom_call_target="tpu_custom_call" | custom-call | flops 54613331968 | tf_op jit(solution)/shard_map/feed_forward/pallas_call | solution.py:72
  148.7 2.3 copy-done.16
  150.9 15.3 %weight_grad.3 = (f32[16,2,48,1536]{3,2,1,0:T(8,128)}, f32[8,128]{1,0:T(8,128)S(1)}) custom-call(s32[2]{0:T(128)S(1)} %pad_add_fusion.refs_0_, bf16[1,2048,768]{2,1,0:T(8,128)(2,1)S(1)} %bitcast.35, bf16[1,2048,3072]{2,1,0:T(8,128)(2,1)} %bitcast.42, f32[8,128]{1,0:T(8,128)S(1)} %get-tuple-element.162.refs_3_), custom_call_target="tpu_custom_call" | custom-call | flops 20480000000 | tf_op jit(solution)/shard_map/weight_grad/pallas_call | solution.py:72
  166.4 37.1 %feed_forward_back.1 = (bf16[2048,3072]{1,0:T(8,128)(2,1)}, f32[2048,768]{1,0:T(8,128)}, bf16[4,2048,768]{2,1,0:T(8,128)(2,1)}, bf16[2048,768]{1,0:T(8,128)(2,1)...) custom-call(f32[2048,768]{1,0:T(8,128)} %get-tuple-element.157.refs_0_, bf16[2048,3072]{1,0:T(8,128)(2,1)} %get-tuple-element.158.refs_1_, ...), custom_call_target="tpu_custom_call" | custom-call | flops 44683636736 | tf_op jit(solution)/shard_map/feed_forward_back/pallas_call | solution.py:72
  203.5 17.1 %weight_grad.4 = (bf16[16,48,1536]{2,1,0:T(8,128)(2,1)S(1)}, bf16[16,48,1536]{2,1,0:T(8,128)(2,1)}, f32[8,128]{1,0:T(8,128)S(1)}) custom-call(s32[2]{0:T(128)S(1)} %pad_add_fusion.refs_0_, bf16[1,2048,768]{2,1,0:T(8,128)(2,1)} %bitcast.43, bf16[1,2048,3072]{2,1,0:T(8,128)(2,1)} %bitcast.41, f32[8,128]{1,0:T(8,128)S(1)} %get-tuple-element.171.refs_3_), custom_call_target="tpu_custom_call" | custom-call | flops 20480000000 | tf_op jit(solution)/shard_map/weight_grad/pallas_call | solution.py:72
  220.7 2.8 copy-done
  223.5 20.0 %attend_back.3 = (bf16[4,2048,768]{2,1,0:T(8,128)(2,1)}, f32[8,128]{1,0:T(8,128)S(1)}) custom-call(bf16[2048,2304]{1,0:T(8,128)(2,1)} %get-tuple-element.148.refs_0_.refs_1_.refs_2_, bf16[2048,2304]{1,0:T(8,128)(2,1)} %get-tuple-element.148.refs_0_.refs_1_.refs_2_, ...), custom_call_target="tpu_custom_call", output_to_operand_aliasing={{0}: (7, {})} | custom-call | flops 21600000000 | tf_op jit(solution)/shard_map/attend_back/pallas_call | solution.py:72
  244.0 1.6 collective-permute-start.9
  245.6 20.4 %attend_back.4 = (bf16[4,2048,768]{2,1,0:T(8,128)(2,1)}, f32[8,128]{1,0:T(8,128)S(1)}) custom-call(bf16[2048,2304]{1,0:T(8,128)(2,1)} %get-tuple-element.148.refs_0_.refs_1_.refs_2_, bf16[2048,2304]{1,0:T(8,128)(2,1)} %get-tuple-element.148.refs_0_.refs_1_.refs_2_, ...), custom_call_target="tpu_custom_call", output_to_operand_aliasing={{0}: (7, {})} | custom-call | flops 21600000000 | tf_op jit(solution)/shard_map/attend_back/pallas_call | solution.py:72
  266.1 1.6 collective-permute-start.10
  267.7 20.1 %attend_back.5 = (bf16[4,2048,768]{2,1,0:T(8,128)(2,1)}, f32[8,128]{1,0:T(8,128)S(1)}) custom-call(bf16[2048,2304]{1,0:T(8,128)(2,1)} %get-tuple-element.148.refs_0_.refs_1_.refs_2_, bf16[2048,2304]{1,0:T(8,128)(2,1)} %get-tuple-element.148.refs_0_.refs_1_.refs_2_, ...), custom_call_target="tpu_custom_call", output_to_operand_aliasing={{0}: (7, {})} | custom-call | flops 21600000000 | tf_op jit(solution)/shard_map/attend_back/pallas_call | solution.py:72
  287.9 1.6 collective-permute-start.11
  289.5 16.2 %weight_grad.5 = (bf16[16,48,1536]{2,1,0:T(8,128)(2,1)S(1)}, bf16[16,48,1536]{2,1,0:T(8,128)(2,1)}, f32[8,128]{1,0:T(8,128)S(1)}) custom-call(s32[2]{0:T(128)S(1)} %pad_add_fusion.refs_0_, bf16[2,2048,768]{2,1,0:T(8,128)(2,1)} %get-tuple-element.151.refs_2_.refs_4_.refs_1_, bf16[4,2048,768]{2,1,0:T(8,128)(2,1)} %get-tuple-element.183.refs_2_.refs_3_.refs_4_, ...), custom_call_target="tpu_custom_call" | custom-call | flops 20480000000 | tf_op jit(solution)/shard_map/weight_grad/pallas_call | solution.py:72
  305.8 4.5 reduce-scatter.2.cloned.1.call-done
  310.4 1.0 copy-done.6
  312.0 1.5 collective-permute-start.12
  313.6 2.5 fold.19
  316.1 3.7 collective-permute-done.12.refs_1_
  319.8 1.5 collective-permute-start.15
  321.4 2.8 copy-done.19
  324.2 21.3 %input_back.1 = (f32[1024,768]{1,0:T(8,128)S(1)}, f32[2,768]{1,0:T(2,128)S(1)}, f32[1,768]{1,0:T(1,128)S(1)}, f32[128,768]{1,0:T(8,128)S(1)}, bf16[2048,128]{1,0...) custom-call(f32[8,128]{1,0:T(8,128)S(1)} %copy-done.18, f32[2048,768]{1,0:T(8,128)S(1)} %copy-done.19, ...), custom_call_target="tpu_custom_call" | custom-call | flops 27306665984 | tf_op jit(solution)/shard_map/input_back/pallas_call | solution.py:72
  345.8 3.0 collective-permute-start.17
  348.7 1.2 collective-permute-start.18
  349.9 6.5 %pack_small.1 = (f32[16,416,128]{2,1,0:T(8,128)S(1)}, bf16[16,416,128]{2,1,0:T(8,128)(2,1)S(1)}, f32[8,128]{1,0:T(8,128)S(1)}) custom-call(s32[2]{0:T(128)S(1)} %pad_add_fusion.refs_0_, s32[4]{0:T(128)S(1)} %copy-done.15, f32[1024,768]{1,0:T(8,128)S(1)} %get-tuple-element.199.refs_2_, f32[128,768]{1,0:T(8,128)S(1)} %get-tuple-element.200.refs_3_, ...), custom_call_target="tpu_custom_call" | custom-call | flops 14400000000 | tf_op jit(solution)/shard_map/pack_small/pallas_call | solution.py:72
  356.5 2.1 collective-permute-done.18.refs_1_
  358.8 1.3 collective-permute-done.16.refs_1_
  360.5 1.0 collective-permute-start.19
  362.1 2.7 mend.1
  364.8 15.9 %collective-permute-done.19.refs_1_ = bf16[8,416,128]{2,1,0:T(8,128)(2,1)S(1)} collective-permute-done((bf16[8,416,128]{2,1,0:T(8,128)(2,1)S(1)}, bf16[8,416,128]{2,1,0:T(8,128)(2,1)S(1)}, u32[]{:S(2)}, u32[]{:S(2)}) %collective-permute-start.19) | collective-permute-done | bytes 852000 | tf_op jit(solution)/shard_map/ppermute | solution.py:622
  380.9 1.5 collective-permute-start.20
  382.5 2.5 collective-permute-start.24
  385.7 3.4 collective-permute-done.20.refs_1_
  389.2 1.2 collective-permute-done.24.refs_1_
  390.4 2.2 collective-permute-start.25
  392.6 2.9 collective-permute-start.23
  395.5 2.3 copy-done.3
  397.8 5.0 %spread.1 = (f32[3072,768]{1,0:T(8,128)}, f32[8,128]{1,0:T(8,128)S(1)}) custom-call(bf16[16,1,2,48,1536]{4,3,2,1,0:T(8,128)(2,1)S(1)} %bitcast.29, f32[8,128]{1,0:T(8,128)S(1)} %get-tuple-element.242.refs_1_), custom_call_target="tpu_custom_call" | custom-call | flops 9600000000 | tf_op jit(solution)/shard_map/spread/pallas_call | solution.py:72
  403.5 2.3 collective-permute-start.32
  405.7 4.1 collective-permute-start.29
  410.2 6.9 %collective-permute-done.26.refs_1_ = bf16[1,416,128]{2,1,0:T(8,128)(2,1)S(1)} collective-permute-done((bf16[1,416,128]{2,1,0:T(8,128)(2,1)S(1)}, bf16[1,416,128]{2,1,0:T(8,128)(2,1)S(1)}, u32[]{:S(2)}, u32[]{:S(2)}) %collective-permute-start.26) | collective-permute-done | bytes 106528 | tf_op jit(solution)/shard_map/ppermute | solution.py:622
  417.3 1.6 collective-permute-start.28
  418.9 4.5 collective-permute-done.28.refs_1_
  423.8 4.8 %collective-permute-done.30.refs_1_ = bf16[2,288,128]{2,1,0:T(8,128)(2,1)S(1)} collective-permute-done((bf16[2,288,128]{2,1,0:T(8,128)(2,1)S(1)}, bf16[2,288,128]{2,1,0:T(8,128)(2,1)S(1)}, u32[]{:S(2)}, u32[]{:S(2)}) %collective-permute-start.30) | collective-permute-done | bytes 147488 | tf_op jit(solution)/shard_map/ppermute | solution.py:622
  429.4 1.6 collective-permute-start.31
  431.0 4.8 %spread_near.2 = (f32[768,3072]{1,0:T(8,128)}, f32[8,128]{1,0:T(8,128)S(1)}) custom-call(s32[2]{0:T(128)S(1)} %pad_add_fusion.refs_0_, bf16[16,48,1536]{2,1,0:T(8,128)(2,1)S(1)} %get-tuple-element.257.refs_1_, bf16[16,48,1536]{2,1,0:T(8,128)(2,1)S(1)} %collective-permute-done.32.refs_2_, f32[8,128]{1,0:T(8,128)S(1)} %get-tuple-element.260.refs_3_), custom_call_target="tpu_custom_call" | custom-call | flops 9600000000 | tf_op jit(solution)/shard_map/spread_near/pallas_call | solution.py:72
  435.8 3.5 collective-permute-done.31.refs_1_
  439.4 5.6 %collective-permute-done.35.refs_1_ = bf16[8,48,1536]{2,1,0:T(8,128)(2,1)S(1)} collective-permute-done((bf16[8,48,1536]{2,1,0:T(8,128)(2,1)S(1)}, bf16[8,48,1536]{2,1,0:T(8,128)(2,1)S(1)}, u32[]{:S(2)}, u32[]{:S(2)}) %collective-permute-start.35) | collective-permute-done | bytes 1179680 | tf_op jit(solution)/shard_map/ppermute | solution.py:622
  445.2 2.4 collective-permute-start.37
  447.6 1.7 collective-permute-start.34
  449.3 8.1 %collective-permute-done.34.refs_1_ = bf16[8,288,128]{2,1,0:T(8,128)(2,1)S(1)} collective-permute-done((bf16[8,288,128]{2,1,0:T(8,128)(2,1)S(1)}, bf16[8,288,128]{2,1,0:T(8,128)(2,1)S(1)}, u32[]{:S(2)}, u32[]{:S(2)}) %collective-permute-start.34) | collective-permute-done | bytes 589856 | tf_op jit(solution)/shard_map/ppermute | solution.py:622
  458.2 5.6 %spread_near.3 = (f32[768,2304]{1,0:T(8,128)}, f32[768,768]{1,0:T(8,128)}, f32[8,128]{1,0:T(8,128)S(1)}) custom-call(s32[2]{0:T(128)S(1)} %pad_add_fusion.refs_0_, bf16[16,48,1536]{2,1,0:T(8,128)(2,1)S(1)} %get-tuple-element.267.refs_1_, bf16[16,48,1536]{2,1,0:T(8,128)(2,1)S(1)} %collective-permute-done.37.refs_2_, f32[8,128]{1,0:T(8,128)S(1)} %get-tuple-element.268.refs_3_), custom_call_target="tpu_custom_call" | custom-call | flops 9600000000 | tf_op jit(solution)/shard_map/spread_near/pallas_call | solution.py:72
  463.8 3.1 unpack_small.1
  (151 shorter events, 12.7 us)
Async XLA Ops:
  7.2 25.4 %copy-start.29 = (bf16[4,512,128]{2,1,0:T(8,128)(2,1)S(1)}, bf16[4,512,128]{2,1,0:T(8,128)(2,1)}, u32[]{:S(2)}) copy-start(bf16[4,512,128]{2,1,0:T(8,128)(2,1)} %param.16) | copy-start | bytes 1572868
  7.2 303.2 %reduce-scatter.2.cloned.1.call-start = ((), (), s32[]{:S(2)}) async-start(), calls=%async_computation.1 | async-start | bytes 9732096 | tf_op jit(solution)/shard_map/reduce_scatter | solution.py:1097
  8.0 7.7 %collective-permute-start = (s32[2,512]{1,0:T(2,128)S(1)}, s32[2,512]{1,0:T(2,128)S(1)}, u32[]{:S(2)}, u32[]{:S(2)}) collective-permute-start(s32[2,512]{1,0:T(2,128)S(1)} %constant_dynamic-slice_fusion.1), channel_id=1, source_target_pairs={{0,1},{1,0},{2,3},{3,2},{4,5},{5,4},{6,7},{7,6},{8,9},{9,8},{10,11... | collective-permute-start | bytes 12296 | tf_op jit(solution)/shard_map/ppermute | solution.py:611
  9.9 24.4 %copy-start.8 = (bf16[128,768]{1,0:T(8,128)(2,1)S(1)}, bf16[128,768]{1,0:T(8,128)(2,1)}, u32[]{:S(2)}) copy-start(bf16[128,768]{1,0:T(8,128)(2,1)} %refs_11_.1) | copy-start | bytes 589828
  9.9 24.4 %copy-start.10 = (f32[8,768]{1,0:T(8,128)S(1)}, f32[8,768]{1,0:T(8,128)}, u32[]{:S(2)}) copy-start(f32[8,768]{1,0:T(8,128)} %refs_7_.3) | copy-start | bytes 73732
  10.0 24.4 %copy-start.12 = (f32[768]{0:T(1024)S(1)}, f32[768]{0:T(1024)}, u32[]{:S(2)}) copy-start(f32[768]{0:T(1024)} %refs_9_.5) | copy-start | bytes 9220
  10.0 24.4 %copy-start.14 = (s32[4]{0:T(128)S(1)}, s32[4]{0:T(128)}, u32[]{:S(2)}) copy-start(s32[4]{0:T(128)} %refs_1_.3) | copy-start | bytes 52
  10.0 6.5 %collective-permute-start.1 = (bf16[1,128,128]{2,1,0:T(8,128)(2,1)S(1)}, bf16[1,128,128]{2,1,0:T(8,128)(2,1)S(1)}, u32[]{:S(2)}, u32[]{:S(2)}) collective-permute-start(bf16[1,128,128]{2,1,0:T(8,128)(2,1)S(1)} %fusion.3), channel_id=1, source_target_pairs={{0,16},{1,17},{2,18},{3,19},{4,20},{5,21},{6,22},{7,23},{8,24},{9,... | collective-permute-start | bytes 98312 | tf_op jit(solution)/shard_map/ppermute | solution.py:622
  14.6 17.9 %collective-permute-start.6 = (bf16[2,512,128]{2,1,0:T(8,128)(2,1)S(1)}, bf16[2,512,128]{2,1,0:T(8,128)(2,1)S(1)}, u32[]{:S(2)}, u32[]{:S(2)}) collective-permute-start(bf16[2,512,128]{2,1,0:T(8,128)(2,1)S(1)} %constant_dynamic-slice_fusion), channel_id=1, source_target_pairs={{0,1},{1,0},{2,3},{3,2},{4,5},{5,4},{6,7},{7,6},{8,9},{9,8},{10,11... | collective-permute-start | bytes 786440 | tf_op jit(solution)/shard_map/ppermute | solution.py:611
  16.5 4.3 collective-permute-start.2
  20.8 5.0 %collective-permute-start.3 = (bf16[4,128,128]{2,1,0:T(8,128)(2,1)S(1)}, bf16[4,128,128]{2,1,0:T(8,128)(2,1)S(1)}, u32[]{:S(2)}, u32[]{:S(2)}) collective-permute-start(bf16[4,128,128]{2,1,0:T(8,128)(2,1)S(1)} %pad_maximum_fusion.2), channel_id=1, source_target_pairs={{0,4},{1,9},{2,6},{3,11},{4,0},{5,13},{6,2},{7,15},{8,12},{9,1},{1... | collective-permute-start | bytes 393224 | tf_op jit(solution)/shard_map/ppermute | solution.py:622
  25.9 6.4 %collective-permute-start.4 = (bf16[8,128,128]{2,1,0:T(8,128)(2,1)S(1)}, bf16[8,128,128]{2,1,0:T(8,128)(2,1)S(1)}, u32[]{:S(2)}, u32[]{:S(2)}) collective-permute-start(bf16[8,128,128]{2,1,0:T(8,128)(2,1)S(1)} %pad_maximum_fusion.1), channel_id=1, source_target_pairs={{0,2},{1,5},{2,0},{3,7},{4,6},{5,1},{6,4},{7,3},{8,10},{9,13},{10,... | collective-permute-start | bytes 786440 | tf_op jit(solution)/shard_map/ppermute | solution.py:622
  32.4 2.0 collective-permute-start.5
  59.7 42.0 %copy-start.25 = (bf16[2048,128]{1,0:T(8,128)(2,1)}, bf16[2048,128]{1,0:T(8,128)(2,1)S(1)}, u32[]{:S(2)}) copy-start(bf16[2048,128]{1,0:T(8,128)(2,1)S(1)} %get-tuple-element.184.refs_6_) | copy-start | bytes 1572868
  59.7 42.0 %copy-start.17 = (f32[8,128]{1,0:T(8,128)}, f32[8,128]{1,0:T(8,128)S(1)}, u32[]{:S(2)}) copy-start(f32[8,128]{1,0:T(8,128)S(1)} %get-tuple-element.147.refs_1_.refs_0_.refs_5_) | copy-start | bytes 12292
  59.7 42.0 %copy-start.23 = (bf16[2048,128]{1,0:T(8,128)(2,1)}, bf16[2048,128]{1,0:T(8,128)(2,1)S(1)}, u32[]{:S(2)}) copy-start(bf16[2048,128]{1,0:T(8,128)(2,1)S(1)} %get-tuple-element.153.refs_4_.refs_7_) | copy-start | bytes 1572868
  59.7 42.0 %copy-start.5 = (bf16[768,768]{1,0:T(8,128)(2,1)S(1)}, bf16[768,768]{1,0:T(8,128)(2,1)}, u32[]{:S(2)}) copy-start(bf16[768,768]{1,0:T(8,128)(2,1)} %refs_4_.2) | copy-start | bytes 3538948
  59.7 42.0 %copy-start.7 = (bf16[768,128]{1,0:T(8,128)(2,1)S(1)}, bf16[768,128]{1,0:T(8,128)(2,1)}, u32[]{:S(2)}) copy-start(bf16[768,128]{1,0:T(8,128)(2,1)} %refs_8_.5) | copy-start | bytes 589828
  59.7 42.0 %copy-start.11 = (f32[768]{0:T(1024)S(1)}, f32[768]{0:T(1024)}, u32[]{:S(2)}) copy-start(f32[768]{0:T(1024)} %refs_5_.3) | copy-start | bytes 9220
  148.7 17.7 %copy-start.21 = (f32[2048,128]{1,0:T(8,128)}, f32[2048,128]{1,0:T(8,128)S(1)}, u32[]{:S(2)}) copy-start(f32[2048,128]{1,0:T(8,128)S(1)} %get-tuple-element.159.refs_2_.refs_8_) | copy-start | bytes 3145732
  166.3 229.2 %all-gather.3.cloned.1.call-start = ((), (), s32[]{:S(2)}) async-start(), calls=%async_computation.2 | async-start | bytes 4866048 | tf_op jit(solution)/shard_map/all_gather | solution.py:722
  203.5 17.2 %slice-start = ((s8[6291456]{0:T(1024)(128)(4,1)}), s8[4194304]{0:T(1024)(128)(4,1)S(1)}, s32[]{:S(2)}) async-start(s8[6291456]{0:T(1024)(128)(4,1)} %bitcast.26), calls=%async_computation.3 | async-start | bytes 8388608
  203.5 17.2 %slice-start.1 = ((s8[6291456]{0:T(1024)(128)(4,1)}), s8[2097152]{0:T(1024)(128)(4,1)S(1)}, s32[]{:S(2)}) async-start(s8[6291456]{0:T(1024)(128)(4,1)} %bitcast.26), calls=%async_computation.4 | async-start | bytes 4194304
  203.5 17.2 %copy-start.1 = (bf16[2048,768]{1,0:T(8,128)(2,1)S(1)}, bf16[2048,768]{1,0:T(8,128)(2,1)}, u32[]{:S(2)}) copy-start(bf16[2048,768]{1,0:T(8,128)(2,1)} %get-tuple-element.165.refs_3_) | copy-start | bytes 9437188
  220.6 22.9 %collective-permute-start.8 = (bf16[16,48,1536]{2,1,0:T(8,128)(2,1)}, bf16[16,48,1536]{2,1,0:T(8,128)(2,1)S(1)}, u32[]{:S(2)}, u32[]{:S(2)}) collective-permute-start(bf16[16,48,1536]{2,1,0:T(8,128)(2,1)} %get-tuple-element.175), channel_id=1, source_target_pairs={{0,1},{1,0},{2,3},{3,2},{4,5},{5,4},{6,7},{7,6},{8,9},{9,8},{10,11... | collective-permute-start | bytes 7077896 | tf_op jit(solution)/shard_map/ppermute | solution.py:611
  244.0 21.9 %collective-permute-start.9 = (bf16[8,48,1536]{2,1,0:T(8,128)(2,1)S(1)}, bf16[8,48,1536]{2,1,0:T(8,128)(2,1)S(1)}, u32[]{:S(2)}, u32[]{:S(2)}) collective-permute-start(bf16[8,48,1536]{2,1,0:T(8,128)(2,1)S(1)} %get-tuple-element.180), channel_id=1, source_target_pairs={{0,2},{1,5},{2,0},{3,7},{4,6},{5,1},{6,4},{7,3},{8,10},{9,13},{10,... | collective-permute-start | bytes 3538952 | tf_op jit(solution)/shard_map/ppermute | solution.py:622
  266.1 21.7 %collective-permute-start.10 = (bf16[4,48,1536]{2,1,0:T(8,128)(2,1)S(1)}, bf16[4,48,1536]{2,1,0:T(8,128)(2,1)S(1)}, u32[]{:S(2)}, u32[]{:S(2)}) collective-permute-start(bf16[4,48,1536]{2,1,0:T(8,128)(2,1)S(1)} %get-tuple-element.186), channel_id=1, source_target_pairs={{0,4},{1,9},{2,6},{3,11},{4,0},{5,13},{6,2},{7,15},{8,12},{9,1},{1... | collective-permute-start | bytes 1769480 | tf_op jit(solution)/shard_map/ppermute | solution.py:622
  287.9 17.8 %collective-permute-start.11 = (bf16[2,48,1536]{2,1,0:T(8,128)(2,1)S(1)}, bf16[2,48,1536]{2,1,0:T(8,128)(2,1)S(1)}, u32[]{:S(2)}, u32[]{:S(2)}) collective-permute-start(bf16[2,48,1536]{2,1,0:T(8,128)(2,1)S(1)} %get-tuple-element.189), channel_id=1, source_target_pairs={{0,8},{1,3},{2,10},{3,1},{4,12},{5,7},{6,14},{7,5},{8,0},{9,11},{1... | collective-permute-start | bytes 884744 | tf_op jit(solution)/shard_map/ppermute | solution.py:622
  305.8 7.7 %collective-permute-start.13 = (bf16[16,48,1536]{2,1,0:T(8,128)(2,1)}, bf16[16,48,1536]{2,1,0:T(8,128)(2,1)}, u32[]{:S(2)}, u32[]{:S(2)}) collective-permute-start(bf16[16,48,1536]{2,1,0:T(8,128)(2,1)} %get-tuple-element.195), channel_id=1, source_target_pairs={{0,1},{1,0},{2,3},{3,2},{4,5},{5,4},{6,7},{7,6},{8,9},{9,8},{10,11... | collective-permute-start | bytes 7077896 | tf_op jit(solution)/shard_map/ppermute | solution.py:611
  312.0 7.7 %collective-permute-start.12 = (bf16[1,48,1536]{2,1,0:T(8,128)(2,1)S(1)}, bf16[1,48,1536]{2,1,0:T(8,128)(2,1)S(1)}, u32[]{:S(2)}, u32[]{:S(2)}) collective-permute-start(bf16[1,48,1536]{2,1,0:T(8,128)(2,1)S(1)} %get-tuple-element.193), channel_id=1, source_target_pairs={{0,16},{1,17},{2,18},{3,19},{4,20},{5,21},{6,22},{7,23},{8,24},{9,... | collective-permute-start | bytes 442376 | tf_op jit(solution)/shard_map/ppermute | solution.py:622
  313.5 48.6 %collective-permute-start.7 = (bf16[2,512,768]{2,1,0:T(8,128)(2,1)}, bf16[2,512,768]{2,1,0:T(8,128)(2,1)S(1)}, u32[]{:S(2)}, u32[]{:S(2)}) collective-permute-start(bf16[2,512,768]{2,1,0:T(8,128)(2,1)} %get-tuple-element.156), channel_id=1, source_target_pairs={{0,1},{1,0},{2,3},{3,2},{4,5},{5,4},{6,7},{7,6},{8,9},{9,8},{10,11... | collective-permute-start | bytes 4718600 | tf_op jit(solution)/shard_map/ppermute | solution.py:611
  313.5 7.9 %copy-start.4 = (bf16[768,2304]{1,0:T(8,128)(2,1)S(1)}, bf16[768,2304]{1,0:T(8,128)(2,1)}, u32[]{:S(2)}) copy-start(bf16[768,2304]{1,0:T(8,128)(2,1)} %refs_10_.3) | copy-start | bytes 10616836
  313.5 7.9 %copy-start.9 = (bf16[128,768]{1,0:T(8,128)(2,1)S(1)}, bf16[128,768]{1,0:T(8,128)(2,1)}, u32[]{:S(2)}) copy-start(bf16[128,768]{1,0:T(8,128)(2,1)} %refs_11_.1) | copy-start | bytes 589828
  313.5 7.9 %copy-start.13 = (f32[768]{0:T(1024)S(1)}, f32[768]{0:T(1024)}, u32[]{:S(2)}) copy-start(f32[768]{0:T(1024)} %refs_9_.5) | copy-start | bytes 9220
  313.5 7.9 %copy-start.18 = (f32[8,128]{1,0:T(8,128)S(1)}, f32[8,128]{1,0:T(8,128)}, u32[]{:S(2)}) copy-start(f32[8,128]{1,0:T(8,128)} %copy-done.17) | copy-start | bytes 12292
  313.5 7.9 %copy-start.22 = (f32[2048,128]{1,0:T(8,128)S(1)}, f32[2048,128]{1,0:T(8,128)}, u32[]{:S(2)}) copy-start(f32[2048,128]{1,0:T(8,128)} %copy-done.21) | copy-start | bytes 3145732
  313.5 7.9 %copy-start.24 = (bf16[2048,128]{1,0:T(8,128)(2,1)S(1)}, bf16[2048,128]{1,0:T(8,128)(2,1)}, u32[]{:S(2)}) copy-start(bf16[2048,128]{1,0:T(8,128)(2,1)} %copy-done.23) | copy-start | bytes 1572868
  313.5 7.9 %copy-start.26 = (bf16[2048,128]{1,0:T(8,128)(2,1)S(1)}, bf16[2048,128]{1,0:T(8,128)(2,1)}, u32[]{:S(2)}) copy-start(bf16[2048,128]{1,0:T(8,128)(2,1)} %copy-done.25) | copy-start | bytes 1572868
  319.8 26.0 %collective-permute-start.14 = (bf16[1,48,1536]{2,1,0:T(8,128)(2,1)S(1)}, bf16[1,48,1536]{2,1,0:T(8,128)(2,1)S(1)}, u32[]{:S(2)}, u32[]{:S(2)}) collective-permute-start(bf16[1,48,1536]{2,1,0:T(8,128)(2,1)S(1)} %bitcast.31), channel_id=1, source_target_pairs={{0,16},{1,17},{2,18},{3,19},{4,20},{5,21},{6,22},{7,23},{8,24},{9,... | collective-permute-start | bytes 442376 | tf_op jit(solution)/shard_map/ppermute | solution.py:622
  319.8 25.7 %collective-permute-start.15 = (bf16[8,48,1536]{2,1,0:T(8,128)(2,1)S(1)}, bf16[8,48,1536]{2,1,0:T(8,128)(2,1)S(1)}, u32[]{:S(2)}, u32[]{:S(2)}) collective-permute-start(bf16[8,48,1536]{2,1,0:T(8,128)(2,1)S(1)} %get-tuple-element.209), channel_id=1, source_target_pairs={{0,2},{1,5},{2,0},{3,7},{4,6},{5,1},{6,4},{7,3},{8,10},{9,13},{10,... | collective-permute-start | bytes 3538952 | tf_op jit(solution)/shard_map/ppermute | solution.py:622
  345.5 4.4 copy-start.15
  345.8 13.0 %collective-permute-start.17 = (bf16[2,48,1536]{2,1,0:T(8,128)(2,1)S(1)}, bf16[2,48,1536]{2,1,0:T(8,128)(2,1)S(1)}, u32[]{:S(2)}, u32[]{:S(2)}) collective-permute-start(bf16[2,48,1536]{2,1,0:T(8,128)(2,1)S(1)} %get-tuple-element.215.refs_0_), channel_id=1, source_target_pairs={{0,8},{1,3},{2,10},{3,1},{4,12},{5,7},{6,14},{7,5},{8,0},{9,11},{1... | collective-permute-start | bytes 884744 | tf_op jit(solution)/shard_map/ppermute | solution.py:622
  348.7 9.9 %collective-permute-start.18 = (bf16[4,48,1536]{2,1,0:T(8,128)(2,1)S(1)}, bf16[4,48,1536]{2,1,0:T(8,128)(2,1)S(1)}, u32[]{:S(2)}, u32[]{:S(2)}) collective-permute-start(bf16[4,48,1536]{2,1,0:T(8,128)(2,1)S(1)} %get-tuple-element.217), channel_id=1, source_target_pairs={{0,4},{1,9},{2,6},{3,11},{4,0},{5,13},{6,2},{7,15},{8,12},{9,1},{1... | collective-permute-start | bytes 1769480 | tf_op jit(solution)/shard_map/ppermute | solution.py:622
  356.4 3.7 collective-permute-start.16
  360.5 20.3 %collective-permute-start.19 = (bf16[8,416,128]{2,1,0:T(8,128)(2,1)S(1)}, bf16[8,416,128]{2,1,0:T(8,128)(2,1)S(1)}, u32[]{:S(2)}, u32[]{:S(2)}) collective-permute-start(bf16[8,416,128]{2,1,0:T(8,128)(2,1)S(1)} %get-tuple-element.224), channel_id=1, source_target_pairs={{0,2},{1,5},{2,0},{3,7},{4,6},{5,1},{6,4},{7,3},{8,10},{9,13},{10,... | collective-permute-start | bytes 2555912 | tf_op jit(solution)/shard_map/ppermute | solution.py:622
  361.4 21.0 %collective-permute-start.22 = (bf16[2,48,1536]{2,1,0:T(8,128)(2,1)S(1)}, bf16[2,48,1536]{2,1,0:T(8,128)(2,1)S(1)}, u32[]{:S(2)}, u32[]{:S(2)}) collective-permute-start(bf16[2,48,1536]{2,1,0:T(8,128)(2,1)S(1)} %get-tuple-element.230), channel_id=1, source_target_pairs={{0,8},{1,3},{2,10},{3,1},{4,12},{5,7},{6,14},{7,5},{8,0},{9,11},{1... | collective-permute-start | bytes 884744 | tf_op jit(solution)/shard_map/ppermute | solution.py:622
  361.5 23.4 %collective-permute-start.21 = (bf16[4,48,1536]{2,1,0:T(8,128)(2,1)S(1)}, bf16[4,48,1536]{2,1,0:T(8,128)(2,1)S(1)}, u32[]{:S(2)}, u32[]{:S(2)}) collective-permute-start(bf16[4,48,1536]{2,1,0:T(8,128)(2,1)S(1)} %get-tuple-element.228.refs_0_), channel_id=1, source_target_pairs={{0,4},{1,9},{2,6},{3,11},{4,0},{5,13},{6,2},{7,15},{8,12},{9,1},{1... | collective-permute-start | bytes 1769480 | tf_op jit(solution)/shard_map/ppermute | solution.py:622
  380.9 8.2 %collective-permute-start.20 = (bf16[4,416,128]{2,1,0:T(8,128)(2,1)S(1)}, bf16[4,416,128]{2,1,0:T(8,128)(2,1)S(1)}, u32[]{:S(2)}, u32[]{:S(2)}) collective-permute-start(bf16[4,416,128]{2,1,0:T(8,128)(2,1)S(1)} %get-tuple-element.227), channel_id=1, source_target_pairs={{0,4},{1,9},{2,6},{3,11},{4,0},{5,13},{6,2},{7,15},{8,12},{9,1},{1... | collective-permute-start | bytes 1277960 | tf_op jit(solution)/shard_map/ppermute | solution.py:622
  382.5 7.9 %collective-permute-start.24 = (bf16[1,48,1536]{2,1,0:T(8,128)(2,1)S(1)}, bf16[1,48,1536]{2,1,0:T(8,128)(2,1)S(1)}, u32[]{:S(2)}, u32[]{:S(2)}) collective-permute-start(bf16[1,48,1536]{2,1,0:T(8,128)(2,1)S(1)} %get-tuple-element.237), channel_id=1, source_target_pairs={{0,16},{1,17},{2,18},{3,19},{4,20},{5,21},{6,22},{7,23},{8,24},{9,... | collective-permute-start | bytes 442376 | tf_op jit(solution)/shard_map/ppermute | solution.py:622
  385.0 18.3 %collective-permute-start.27 = (bf16[8,48,1536]{2,1,0:T(8,128)(2,1)S(1)}, bf16[8,48,1536]{2,1,0:T(8,128)(2,1)S(1)}, u32[]{:S(2)}, u32[]{:S(2)}) collective-permute-start(bf16[8,48,1536]{2,1,0:T(8,128)(2,1)S(1)} %get-tuple-element.247.refs_0_), channel_id=1, source_target_pairs={{0,2},{1,5},{2,0},{3,7},{4,6},{5,1},{6,4},{7,3},{8,10},{9,13},{10,... | collective-permute-start | bytes 3538952 | tf_op jit(solution)/shard_map/ppermute | solution.py:622
  390.4 12.4 %collective-permute-start.25 = (bf16[1,48,1536]{2,1,0:T(8,128)(2,1)S(1)}, bf16[1,48,1536]{2,1,0:T(8,128)(2,1)S(1)}, u32[]{:S(2)}, u32[]{:S(2)}) collective-permute-start(bf16[1,48,1536]{2,1,0:T(8,128)(2,1)S(1)} %bitcast.33), channel_id=1, source_target_pairs={{0,16},{1,17},{2,18},{3,19},{4,20},{5,21},{6,22},{7,23},{8,24},{9,... | collective-permute-start | bytes 442376 | tf_op jit(solution)/shard_map/ppermute | solution.py:622
  392.6 10.2 %collective-permute-start.23 = (bf16[2,416,128]{2,1,0:T(8,128)(2,1)S(1)}, bf16[2,416,128]{2,1,0:T(8,128)(2,1)S(1)}, u32[]{:S(2)}, u32[]{:S(2)}) collective-permute-start(bf16[2,416,128]{2,1,0:T(8,128)(2,1)S(1)} %get-tuple-element.235), channel_id=1, source_target_pairs={{0,8},{1,3},{2,10},{3,1},{4,12},{5,7},{6,14},{7,5},{8,0},{9,11},{1... | collective-permute-start | bytes 638984 | tf_op jit(solution)/shard_map/ppermute | solution.py:622
  403.5 27.5 %collective-permute-start.32 = (bf16[16,48,1536]{2,1,0:T(8,128)(2,1)S(1)}, bf16[16,48,1536]{2,1,0:T(8,128)(2,1)S(1)}, u32[]{:S(2)}, u32[]{:S(2)}) collective-permute-start(bf16[16,48,1536]{2,1,0:T(8,128)(2,1)S(1)} %get-tuple-element.257.refs_1_), channel_id=1, source_target_pairs={{0,1},{1,0},{2,3},{3,2},{4,5},{5,4},{6,7},{7,6},{8,9},{9,8},{10,11... | collective-permute-start | bytes 7077896 | tf_op jit(solution)/shard_map/ppermute | solution.py:611
  405.7 11.4 %collective-permute-start.29 = (bf16[2,48,1536]{2,1,0:T(8,128)(2,1)S(1)}, bf16[2,48,1536]{2,1,0:T(8,128)(2,1)S(1)}, u32[]{:S(2)}, u32[]{:S(2)}) collective-permute-start(bf16[2,48,1536]{2,1,0:T(8,128)(2,1)S(1)} %get-tuple-element.251.refs_0_), channel_id=1, source_target_pairs={{0,8},{1,3},{2,10},{3,1},{4,12},{5,7},{6,14},{7,5},{8,0},{9,11},{1... | collective-permute-start | bytes 884744 | tf_op jit(solution)/shard_map/ppermute | solution.py:622
  409.9 7.3 %collective-permute-start.26 = (bf16[1,416,128]{2,1,0:T(8,128)(2,1)S(1)}, bf16[1,416,128]{2,1,0:T(8,128)(2,1)S(1)}, u32[]{:S(2)}, u32[]{:S(2)}) collective-permute-start(bf16[1,416,128]{2,1,0:T(8,128)(2,1)S(1)} %get-tuple-element.246), channel_id=1, source_target_pairs={{0,16},{1,17},{2,18},{3,19},{4,20},{5,21},{6,22},{7,23},{8,24},{9,... | collective-permute-start | bytes 319496 | tf_op jit(solution)/shard_map/ppermute | solution.py:622
  417.2 11.4 %collective-permute-start.33 = (bf16[4,48,1536]{2,1,0:T(8,128)(2,1)S(1)}, bf16[4,48,1536]{2,1,0:T(8,128)(2,1)S(1)}, u32[]{:S(2)}, u32[]{:S(2)}) collective-permute-start(bf16[4,48,1536]{2,1,0:T(8,128)(2,1)S(1)} %get-tuple-element.258.refs_0_), channel_id=1, source_target_pairs={{0,4},{1,9},{2,6},{3,11},{4,0},{5,13},{6,2},{7,15},{8,12},{9,1},{1... | collective-permute-start | bytes 1769480 | tf_op jit(solution)/shard_map/ppermute | solution.py:622
  417.3 6.1 %collective-permute-start.28 = (bf16[1,288,128]{2,1,0:T(8,128)(2,1)S(1)}, bf16[1,288,128]{2,1,0:T(8,128)(2,1)S(1)}, u32[]{:S(2)}, u32[]{:S(2)}) collective-permute-start(bf16[1,288,128]{2,1,0:T(8,128)(2,1)S(1)} %fusion.refs_0_), channel_id=1, source_target_pairs={{0,16},{1,17},{2,18},{3,19},{4,20},{5,21},{6,22},{7,23},{8,24},{9,... | collective-permute-start | bytes 221192 | tf_op jit(solution)/shard_map/ppermute | solution.py:622
  423.4 5.2 %collective-permute-start.30 = (bf16[2,288,128]{2,1,0:T(8,128)(2,1)S(1)}, bf16[2,288,128]{2,1,0:T(8,128)(2,1)S(1)}, u32[]{:S(2)}, u32[]{:S(2)}) collective-permute-start(bf16[2,288,128]{2,1,0:T(8,128)(2,1)S(1)} %get-tuple-element.254.refs_0_), channel_id=1, source_target_pairs={{0,8},{1,3},{2,10},{3,1},{4,12},{5,7},{6,14},{7,5},{8,0},{9,11},{1... | collective-permute-start | bytes 442376 | tf_op jit(solution)/shard_map/ppermute | solution.py:622
  428.7 16.3 %collective-permute-start.35 = (bf16[8,48,1536]{2,1,0:T(8,128)(2,1)S(1)}, bf16[8,48,1536]{2,1,0:T(8,128)(2,1)S(1)}, u32[]{:S(2)}, u32[]{:S(2)}) collective-permute-start(bf16[8,48,1536]{2,1,0:T(8,128)(2,1)S(1)} %get-tuple-element.263.refs_0_), channel_id=1, source_target_pairs={{0,2},{1,5},{2,0},{3,7},{4,6},{5,1},{6,4},{7,3},{8,10},{9,13},{10,... | collective-permute-start | bytes 3538952 | tf_op jit(solution)/shard_map/ppermute | solution.py:622
  429.4 9.9 %collective-permute-start.31 = (bf16[4,288,128]{2,1,0:T(8,128)(2,1)S(1)}, bf16[4,288,128]{2,1,0:T(8,128)(2,1)S(1)}, u32[]{:S(2)}, u32[]{:S(2)}) collective-permute-start(bf16[4,288,128]{2,1,0:T(8,128)(2,1)S(1)} %get-tuple-element.256.refs_0_), channel_id=1, source_target_pairs={{0,4},{1,9},{2,6},{3,11},{4,0},{5,13},{6,2},{7,15},{8,12},{9,1},{1... | collective-permute-start | bytes 884744 | tf_op jit(solution)/shard_map/ppermute | solution.py:622
  445.2 13.0 %collective-permute-start.37 = (bf16[16,48,1536]{2,1,0:T(8,128)(2,1)S(1)}, bf16[16,48,1536]{2,1,0:T(8,128)(2,1)S(1)}, u32[]{:S(2)}, u32[]{:S(2)}) collective-permute-start(bf16[16,48,1536]{2,1,0:T(8,128)(2,1)S(1)} %get-tuple-element.267.refs_1_), channel_id=1, source_target_pairs={{0,1},{1,0},{2,3},{3,2},{4,5},{5,4},{6,7},{7,6},{8,9},{9,8},{10,11... | collective-permute-start | bytes 7077896 | tf_op jit(solution)/shard_map/ppermute | solution.py:611
  447.6 9.9 %collective-permute-start.34 = (bf16[8,288,128]{2,1,0:T(8,128)(2,1)S(1)}, bf16[8,288,128]{2,1,0:T(8,128)(2,1)S(1)}, u32[]{:S(2)}, u32[]{:S(2)}) collective-permute-start(bf16[8,288,128]{2,1,0:T(8,128)(2,1)S(1)} %get-tuple-element.262.refs_0_), channel_id=1, source_target_pairs={{0,2},{1,5},{2,0},{3,7},{4,6},{5,1},{6,4},{7,3},{8,10},{9,13},{10,... | collective-permute-start | bytes 1769480 | tf_op jit(solution)/shard_map/ppermute | solution.py:622
  457.5 6.3 %collective-permute-start.36 = (bf16[16,288,128]{2,1,0:T(8,128)(2,1)S(1)}, bf16[16,288,128]{2,1,0:T(8,128)(2,1)S(1)}, u32[]{:S(2)}, u32[]{:S(2)}) collective-permute-start(bf16[16,288,128]{2,1,0:T(8,128)(2,1)S(1)} %get-tuple-element.266.refs_1_), channel_id=1, source_target_pairs={{0,1},{1,0},{2,3},{3,2},{4,5},{5,4},{6,7},{7,6},{8,9},{9,8},{10,11... | collective-permute-start | bytes 3538952 | tf_op jit(solution)/shard_map/ppermute | solution.py:611
  458.2 5.6 %copy-start.2 = (bf16[120,128]{1,0:T(8,128)(2,1)S(1)}, bf16[120,128]{1,0:T(8,128)(2,1)}, u32[]{:S(2)}) copy-start(bf16[120,128]{1,0:T(8,128)(2,1)} %refs_4_.3) | copy-start | bytes 92164
  (8 other events, 18.4 us)
Sparse Core Ops, SparseCore 0:
  166.4 143.8 reduce-scatter.1
  314.2 69.3 all-gather.2

commit v4 on v3

--- a/solution.py
+++ b/solution.py
@@ -509,7 +509,7 @@
         ],
         (tiles, seqs),
         "input_back",
-        cost(tokens / 90), limit=34 * 2**20,
+        cost(tokens / 90), limit=60 * 2**20,
     )
 
 
@@ -644,15 +644,9 @@
     return out if count else out[0]
 
 
-def rounded_kernel(in_ref, out_ref):
-    out_ref[...] = in_ref[...].astype(BF)
-
-
-def rounded(chunk):
-    return launch(
-        rounded_kernel, [chunk], [whole(chunk.shape)], [whole(chunk.shape)],
-        [jax.ShapeDtypeStruct(chunk.shape, BF)], (1,), "rounded", cost(0.4), limit=8 * 2**20, chained=False,
-    )[0]
+def both_kernel(keep_ref, got_ref, other_ref, out_ref):
+    out_ref[0] = other_ref[...].astype(BF)
+    out_ref[1] = (keep_ref[0] + got_ref[0].astype(F32)).astype(BF)
 
 
 def join_kernel(held_ref, got_ref, out_ref):
@@ -686,6 +680,16 @@
         else:
             self.keep = out[1]
             self.got = hop(out[0], self.step)
+
+    def finish_with(self, other):
+        while self.step < self.steps - 1:
+            self.fold()
+        shape = jax.ShapeDtypeStruct((2, *other.shape), BF)
+        return launch(
+            both_kernel, [self.keep, self.got, other],
+            [whole(self.keep.shape), whole(self.got.shape), whole(other.shape)], [whole(shape.shape)],
+            [shape], (1,), "both", cost(0.4), limit=60 * 2**20,
+        )[0]
 
     def finish(self, last=BF):
         while self.chunk is None:
@@ -718,10 +722,6 @@
         return self.held, self.other
 
 
-def share(chunk):
-    return lax.all_gather(chunk, ("batch", "seq"), axis=0)
-
-
 def mend_kernel(where, own_ref, other_ref, out_ref, *, seqs):
     ours = pl.program_id(0) // seqs == where[1]
 
@@ -753,41 +753,10 @@
     )[0]
 
 
-def spread_kernel(in_ref, out_ref, *, flip):
-    row_blocks, _, _, rows, cols = in_ref.shape
-    block = in_ref[...].reshape(row_blocks * rows, cols).astype(F32)
-    out_ref[...] = block.T if flip else block
-
-
-def spread(gathered, batch, rows, cols, flip=False):
-    row_blocks, chunk_rows, chunk_cols = chunk_shape(batch, rows, cols // 2)
-    view = gathered.reshape(row_blocks, batch // row_blocks, 2, chunk_rows, chunk_cols)
-    tw = next(size for size in (512, 384, 256, 128) if chunk_cols % size == 0)
-    per, half = chunk_cols // tw, cols // 2 // tw
-    return launch(
-        functools.partial(spread_kernel, flip=flip),
-        [view],
-        [
-            pl.BlockSpec(
-                (row_blocks, 1, 1, chunk_rows, tw),
-                lambda i: (0, (i % half) // per, i // half, 0, i % per),
-            )
-        ],
-        [
-            pl.BlockSpec((tw, rows), lambda i: (i, 0))
-            if flip
-            else pl.BlockSpec((rows, tw), lambda i: (0, i))
-        ],
-        [jax.ShapeDtypeStruct((cols, rows) if flip else (rows, cols), F32)],
-        (cols // tw,),
-        "spread",
-        cost(8), limit=20 * 2**20,
-    )[0]
-
-
-def spread_near_kernel(where, own_ref, other_ref, *outs, steps, orders, row_blocks, splits):
+def spread_near_kernel(where, own_ref, other_ref, *outs, steps, orders, row_blocks, splits, flip):
     me, core = where[0], where[1]
-    chunks, rows, tw = own_ref.shape
+    *outs, whole_ref = outs
+    chunks, _, rows, tw = own_ref.shape
     col_blocks = chunks // row_blocks
     step = pl.program_id(0)
     block = (step % steps) * col_blocks // steps if col_blocks > 1 else 0
@@ -797,7 +766,10 @@
         for row in range(row_blocks):
             owner = row * col_blocks + block
             spot = jnp.where(half == 0, place(owner, me, orders[0]), place(owner, me, orders[1]))
-            out_ref[row * rows : (row + 1) * rows, :] = ref[spot].astype(F32)
+            target = whole_ref if flip else out_ref
+            target[row * rows : (row + 1) * rows, :] = ref[spot, 0].astype(F32)
+        if flip:
+            out_ref[...] = whole_ref[...].T
 
     for ours in (True, False):
         for out_ref, first, last in zip(outs, splits[:-1], splits[1:]):
@@ -812,8 +784,8 @@
                     write(other_ref, 1 - core, out_ref)
 
 
-def spread_near(where, own, other, rows, widths):
-    batch, chunk_rows, chunk_cols = own.shape
+def spread_near(where, own, other, which, rows, widths, flip=False):
+    batch, _, chunk_rows, chunk_cols = own.shape
     row_blocks = rows // chunk_rows
     tw = next(size for size in (768, 512, 384, 256, 128) if chunk_cols % size == 0)
     steps, per = sum(widths) // 2 // tw, chunk_cols // tw
@@ -824,33 +796,37 @@
         def pick(i, w):
             at = tile(i, w)
             idle = jnp.where(i < steps, 0, last - first - 1) if first else last - 1
-            return (0, jnp.where(jnp.logical_and(at >= first, at < last), at - first, idle))
+            block = jnp.where(jnp.logical_and(at >= first, at < last), at - first, idle)
+            return (block, 0) if flip else (0, block)
 
         return pick
 
     return launch(
         functools.partial(
             spread_near_kernel, steps=steps, orders=bit_orders(batch), row_blocks=row_blocks,
-            splits=splits,
+            splits=splits, flip=flip,
         ),
         [own, other],
         [
             pl.BlockSpec(
-                (batch, chunk_rows, tw), lambda i, w: (0, 0, jnp.minimum(i, steps - 1) % per)
+                (batch, 1, chunk_rows, tw),
+                lambda i, w: (0, which, 0, jnp.minimum(i, steps - 1) % per),
             ),
             pl.BlockSpec(
-                (batch, chunk_rows, tw), lambda i, w: (0, 0, jnp.maximum(i - steps, 0) % per)
+                (batch, 1, chunk_rows, tw),
+                lambda i, w: (0, which, 0, jnp.maximum(i - steps, 0) % per),
             ),
         ],
         [
-            pl.BlockSpec((rows, tw), column(first, last))
+            pl.BlockSpec((tw, rows) if flip else (rows, tw), column(first, last))
             for first, last in zip(splits[:-1], splits[1:])
         ],
-        [jax.ShapeDtypeStruct((rows, width), F32) for width in widths],
+        [jax.ShapeDtypeStruct((width, rows) if flip else (rows, width), F32) for width in widths],
         (2 * steps,),
         "spread_near",
         cost(8), limit=24 * 2**20,
         prefetch=[where],
+        scratch=[pltpu.VMEM((rows, tw) if flip else (8, 128), F32)],
     )
 
 
@@ -1107,14 +1083,13 @@
         up.fold()
     attn = Sum(*outer(where, lefts, grads, batch))
     up.fold(micros=25)
-    down_all = share(rounded(down_sum))
     attn.fold()
-    up_all = Gather(up.finish(), batch)
+    mlp_all = Gather(up.finish_with(down_sum), batch)
     gpos, gtime, ggain_a, gwin, grows, gscale = input_back(
         scal, gmid, grads, stream, noisy, word, gpred, gain_attn, w_qkv, w_in, length
     )
     attn.fold()
-    up_all.join()
+    mlp_all.join()
     small = Sum(
         *pack(
             where, buckets, gpos, gwin, ghead, gtime, ggain_a, ggain_m, gscale, home, grows, batch,
@@ -1122,18 +1097,16 @@
         )
     )
     attn.fold()
-    up_all.join(micros=25)
+    mlp_all.join(micros=25)
     small.fold(F32)
     output = mend(where, ours, swap(theirs))
     small.fold(F32)
     attn.fold()
-    up_all.join()
     small.fold(F32)
     attn_all = Gather(attn.finish(), batch)
-    grad_down = spread(down_all, batch, model, inner, True)
+    mlp_all.join()
+    small.fold(F32)
     attn_all.join()
-    small.fold(F32)
-    up_own, up_other = up_all.finish()
     mine = small.finish(F32)
     cut = mine.shape[0] - span
     small_all = Gather(mine[:cut].astype(BF), batch)
@@ -1141,11 +1114,16 @@
     small_all.join()
     small_all.join()
     attn_all.join()
-    (grad_up,) = spread_near(where, up_own, up_other, model, (inner,))
+    mlp_own, mlp_other = mlp_all.finish()
     small_all.join()
+    (grad_up,) = spread_near(where, mlp_own, mlp_other, 1, model, (inner,))
+    (grad_down,) = spread_near(where, mlp_own, mlp_other, 0, model, (inner,), True)
+    small_all.join(micros=25)
     attn_own, attn_other = attn_all.finish()
     small_own, small_other = small_all.finish()
-    grad_qkv, grad_out = spread_near(where, attn_own, attn_other, model, (3 * model, model))
+    grad_qkv, grad_out = spread_near(
+        where, attn_own[:, None], attn_other[:, None], 0, model, (3 * model, model)
+    )
     pos_sum, win_sum, head_sum, time_sum, gain_a_sum, gain_m_sum, grad_table = unpack(
         where, small_own, small_other, mine[cut:], table, scal, length, model, bucket_count, vocab
     )

time: 484 us -> 478 us (0.988)
  starting transfers between devices: 48.1 us -> 39.3 us
  Pallas kernels: 315 us -> 321 us
    pallas_call x45 -> x44, Pallas kernels: 315 us -> 321 us  [launch(): pl.pallas_call(body, grid_spec=pltpu.PrefetchScalarGridSpec(num_scalar_pr...]
    ppermute x28, starting transfers between devices: 42.2 us -> 36.3 us  [hop(): return lax.ppermute(array, ('batch', 'seq'), pairs)]
  transfers between devices with their start and end apart: 40 -> 39, of which waited for: 18 -> 19; matrix products, arithmetic and copies ran while one was open for 1% -> 1% of each run, Pallas kernels for 38% -> 40%
where the time goes in v4:
time: 478 us; the launch traced here: 468 us
  Pallas kernels  321 us (67%)
  waiting for transfers between devices  78.9 us (17%)
  starting transfers between devices  39.3 us (8%)
  between operations  15.1 us (3%)
  local copies, waits for them, and re-layouts  10.3 us (2%)
    pallas_call x44, Pallas kernels, launch(): pl.pallas_call(body, grid_spec=pltpu.PrefetchScalarGridSpec(num_scalar_pr...  321 us
    ppermute x28, waiting for transfers between devices, hop(): return lax.ppermute(array, ('batch', 'seq'), pairs)  73.3 us
    ppermute x28, starting transfers between devices, hop(): return lax.ppermute(array, ('batch', 'seq'), pairs)  36.3 us
  transfers between devices with their start and end apart: 39, of which 19 were waited for; matrix products, arithmetic and copies ran while one was open for 1% of the time, Pallas kernels for 40%

profile of v4, /device:TPU:0, one launch (start us, length us, event | category | flops | bytes accessed | tf_op | source)
XLA Modules:
  0.0 468.4 jit_solution(4581711919752669216)
XLA Ops:
  10.0 3.6 collective-permute-start.1
  13.6 1.0 constant_dynamic-slice_fusion
  16.4 1.6 collective-permute-start.2
  18.1 2.7 collective-permute-done.2
  20.7 1.6 collective-permute-start.3
  22.4 3.4 collective-permute-done.3
  25.8 1.6 collective-permute-start.4
  27.4 4.8 %collective-permute-done.4 = bf16[8,128,128]{2,1,0:T(8,128)(2,1)S(1)} collective-permute-done((bf16[8,128,128]{2,1,0:T(8,128)(2,1)S(1)}, bf16[8,128,128]{2,1,0:T(8,128)(2,1)S(1)}, u32[]{:S(2)}, u32[]{:S(2)}) %collective-permute-start.4) | collective-permute-done | bytes 262176 | tf_op jit(solution)/shard_map/ppermute | solution.py:622
  32.5 1.0 broadcast_select_fusion.1
  34.3 25.3 %embed.1 = (bf16[2048,128]{1,0:T(8,128)(2,1)S(1)}, bf16[2048,128]{1,0:T(8,128)(2,1)S(1)}, f32[2048,768]{1,0:T(8,128)}, bf16[2,2048,768]{2,1,0:T(8,128)(2,1)}, bf...) custom-call(s32[2]{0:T(128)S(1)} %pad_add_fusion.refs_0_, s32[4]{0:T(128)S(1)} %copy-done.12, ...), custom_call_target="tpu_custom_call" | custom-call | flops 30720000000 | tf_op jit(solution)/shard_map/embed/pallas_call | solution.py:72
  59.6 41.9 %attend.1 = (bf16[2,2048,768]{2,1,0:T(8,128)(2,1)}, bf16[24,1024,1024]{2,1,0:T(8,128)(2,1)}, f32[2048,768]{1,0:T(8,128)}, f32[8,128]{1,0:T(8,128)S(1)}) custom-call(bf16[2048,2304]{1,0:T(8,128)(2,1)} %get-tuple-element.147.refs_0_.refs_1_.refs_2_, bf16[2048,2304]{1,0:T(8,128)(2,1)} %get-tuple-element.147.refs_0_.refs_1_.refs_2_, ...), custom_call_target="tpu_custom_call", output_to_operand_aliasing={{0}: (3, {})} | custom-call | flops 50400002048 | tf_op jit(solution)/shard_map/attend/pallas_call | solution.py:72
  101.5 46.1 %feed_forward.1 = (f32[2048,768]{1,0:T(8,128)}, bf16[2048,768]{1,0:T(8,128)(2,1)}, bf16[2048,3072]{1,0:T(8,128)(2,1)}, bf16[2048,3072]{1,0:T(8,128)(2,1)}, bf16[...) custom-call(s32[2]{0:T(128)S(1)} %pad_add_fusion.refs_0_, ...), custom_call_target="tpu_custom_call" | custom-call | flops 54613331968 | tf_op jit(solution)/shard_map/feed_forward/pallas_call | solution.py:72
  148.4 2.3 copy-done.14
  150.7 15.3 %weight_grad.3 = (f32[16,2,48,1536]{3,2,1,0:T(8,128)}, f32[8,128]{1,0:T(8,128)S(1)}) custom-call(s32[2]{0:T(128)S(1)} %pad_add_fusion.refs_0_, bf16[1,2048,768]{2,1,0:T(8,128)(2,1)S(1)} %bitcast.36, bf16[1,2048,3072]{2,1,0:T(8,128)(2,1)} %bitcast.44, f32[8,128]{1,0:T(8,128)S(1)} %get-tuple-element.161.refs_3_), custom_call_target="tpu_custom_call" | custom-call | flops 20480000000 | tf_op jit(solution)/shard_map/weight_grad/pallas_call | solution.py:72
  166.0 37.0 %feed_forward_back.1 = (bf16[2048,3072]{1,0:T(8,128)(2,1)}, f32[2048,768]{1,0:T(8,128)}, bf16[4,2048,768]{2,1,0:T(8,128)(2,1)}, bf16[2048,768]{1,0:T(8,128)(2,1)...) custom-call(f32[2048,768]{1,0:T(8,128)} %get-tuple-element.156.refs_0_, bf16[2048,3072]{1,0:T(8,128)(2,1)} %get-tuple-element.157.refs_1_, ...), custom_call_target="tpu_custom_call" | custom-call | flops 44683636736 | tf_op jit(solution)/shard_map/feed_forward_back/pallas_call | solution.py:72
  203.1 17.1 %weight_grad.4 = (bf16[16,48,1536]{2,1,0:T(8,128)(2,1)S(1)}, bf16[16,48,1536]{2,1,0:T(8,128)(2,1)}, f32[8,128]{1,0:T(8,128)S(1)}) custom-call(s32[2]{0:T(128)S(1)} %pad_add_fusion.refs_0_, bf16[1,2048,768]{2,1,0:T(8,128)(2,1)} %bitcast.45, bf16[1,2048,3072]{2,1,0:T(8,128)(2,1)} %bitcast.43, f32[8,128]{1,0:T(8,128)S(1)} %get-tuple-element.170.refs_3_), custom_call_target="tpu_custom_call" | custom-call | flops 20480000000 | tf_op jit(solution)/shard_map/weight_grad/pallas_call | solution.py:72
  220.3 2.8 copy-done
  223.1 20.0 %attend_back.3 = (bf16[4,2048,768]{2,1,0:T(8,128)(2,1)}, f32[8,128]{1,0:T(8,128)S(1)}) custom-call(bf16[2048,2304]{1,0:T(8,128)(2,1)} %get-tuple-element.147.refs_0_.refs_1_.refs_2_, bf16[2048,2304]{1,0:T(8,128)(2,1)} %get-tuple-element.147.refs_0_.refs_1_.refs_2_, ...), custom_call_target="tpu_custom_call", output_to_operand_aliasing={{0}: (7, {})} | custom-call | flops 21600000000 | tf_op jit(solution)/shard_map/attend_back/pallas_call | solution.py:72
  243.6 1.6 collective-permute-start.9
  245.2 20.5 %attend_back.4 = (bf16[4,2048,768]{2,1,0:T(8,128)(2,1)}, f32[8,128]{1,0:T(8,128)S(1)}) custom-call(bf16[2048,2304]{1,0:T(8,128)(2,1)} %get-tuple-element.147.refs_0_.refs_1_.refs_2_, bf16[2048,2304]{1,0:T(8,128)(2,1)} %get-tuple-element.147.refs_0_.refs_1_.refs_2_, ...), custom_call_target="tpu_custom_call", output_to_operand_aliasing={{0}: (7, {})} | custom-call | flops 21600000000 | tf_op jit(solution)/shard_map/attend_back/pallas_call | solution.py:72
  265.9 1.6 collective-permute-start.10
  267.5 20.0 %attend_back.5 = (bf16[4,2048,768]{2,1,0:T(8,128)(2,1)}, f32[8,128]{1,0:T(8,128)S(1)}) custom-call(bf16[2048,2304]{1,0:T(8,128)(2,1)} %get-tuple-element.147.refs_0_.refs_1_.refs_2_, bf16[2048,2304]{1,0:T(8,128)(2,1)} %get-tuple-element.147.refs_0_.refs_1_.refs_2_, ...), custom_call_target="tpu_custom_call", output_to_operand_aliasing={{0}: (7, {})} | custom-call | flops 21600000000 | tf_op jit(solution)/shard_map/attend_back/pallas_call | solution.py:72
  287.6 1.6 collective-permute-start.11
  289.3 16.3 %weight_grad.5 = (bf16[16,48,1536]{2,1,0:T(8,128)(2,1)S(1)}, bf16[16,48,1536]{2,1,0:T(8,128)(2,1)}, f32[8,128]{1,0:T(8,128)S(1)}) custom-call(s32[2]{0:T(128)S(1)} %pad_add_fusion.refs_0_, bf16[2,2048,768]{2,1,0:T(8,128)(2,1)} %get-tuple-element.150.refs_2_.refs_4_.refs_1_, bf16[4,2048,768]{2,1,0:T(8,128)(2,1)} %get-tuple-element.182.refs_2_.refs_3_.refs_4_, ...), custom_call_target="tpu_custom_call" | custom-call | flops 20480000000 | tf_op jit(solution)/shard_map/weight_grad/pallas_call | solution.py:72
  306.3 2.5 collective-permute-start.12
  309.0 1.2 collective-permute-done.13.refs_1_
  310.3 1.4 fold.18
  312.3 0.8 collective-permute-start.15
  313.1 3.5 collective-permute-done.12.refs_1_
  316.6 1.9 both.1
  318.5 23.7 %input_back.1 = (f32[1024,768]{1,0:T(8,128)}, f32[2,768]{1,0:T(2,128)}, f32[1,768]{1,0:T(1,128)}, f32[128,768]{1,0:T(8,128)}, bf16[2048,128]{1,0:T(8,128)(2,1)}, /*index=5*/f32[1,128]{1,0:T(1,128)}, f32[8,128]{1,0:T(8,128)}) custom-call(f32[8,128]{1,0:T(8,128)} %copy-done.15, f32[2048,768]{1,0:T(8,128)} %get-tuple-element.163.refs_1_, ...), custom_call_target="tpu_custom_call" | custom-call | flops 27306665984 | tf_op jit(solution)/shard_map/input_back/pallas_call | solution.py:72
  343.2 1.0 collective-permute-start.18
  344.2 1.1 join.12
  345.3 2.7 collective-permute-start.17
  348.1 6.5 %pack_small.1 = (f32[16,416,128]{2,1,0:T(8,128)S(1)}, bf16[16,416,128]{2,1,0:T(8,128)(2,1)S(1)}, f32[8,128]{1,0:T(8,128)S(1)}) custom-call(s32[2]{0:T(128)S(1)} %pad_add_fusion.refs_0_, s32[4]{0:T(128)S(1)} %copy-done.13, f32[1024,768]{1,0:T(8,128)S(1)} %copy-done.19, f32[128,768]{1,0:T(8,128)S(1)} %copy-done.24, f32[128,768]{1,0:T(8,128)S(1)} %copy-done.26, ...), custom_call_target="tpu_custom_call" | custom-call | flops 14400000000 | tf_op jit(solution)/shard_map/pack_small/pallas_call | solution.py:72
  354.8 3.7 collective-permute-done.17.refs_1_
  359.0 1.3 collective-permute-start.19
  360.3 1.7 collective-permute-start.21
  362.8 4.7 %mend.1 = (bf16[4,512,768]{2,1,0:T(8,128)(2,1)}, f32[8,128]{1,0:T(8,128)S(1)}) custom-call(s32[2]{0:T(128)S(1)} %pad_add_fusion.refs_0_, bf16[2,512,768]{2,1,0:T(8,128)(2,1)S(1)} %copy-done.18, bf16[2,512,768]{2,1,0:T(8,128)(2,1)} %collective-permute-done.7.refs_2_, f32[8,128]{1,0:T(8,128)S(1)} %get-tuple-element.221.refs_3_), custom_call_target="tpu_custom_call" | custom-call | flops 7200000000 | tf_op jit(solution)/shard_map/mend/pallas_call | solution.py:72
  367.5 6.9 %collective-permute-done.19.refs_1_ = bf16[8,416,128]{2,1,0:T(8,128)(2,1)S(1)} collective-permute-done((bf16[8,416,128]{2,1,0:T(8,128)(2,1)S(1)}, bf16[8,416,128]{2,1,0:T(8,128)(2,1)S(1)}, u32[]{:S(2)}, u32[]{:S(2)}) %collective-permute-start.19) | collective-permute-done | bytes 852000 | tf_op jit(solution)/shard_map/ppermute | solution.py:622
  374.6 1.1 collective-permute-start.20
  376.1 11.7 %collective-permute-done.20.refs_1_ = bf16[4,416,128]{2,1,0:T(8,128)(2,1)S(1)} collective-permute-done((bf16[4,416,128]{2,1,0:T(8,128)(2,1)S(1)}, bf16[4,416,128]{2,1,0:T(8,128)(2,1)S(1)}, u32[]{:S(2)}, u32[]{:S(2)}) %collective-permute-start.20) | collective-permute-done | bytes 426016 | tf_op jit(solution)/shard_map/ppermute | solution.py:622
  388.1 1.0 collective-permute-start.31
  389.1 2.3 collective-permute-start.26
  391.4 6.6 %collective-permute-done.22.refs_1_ = bf16[2,416,128]{2,1,0:T(8,128)(2,1)S(1)} collective-permute-done((bf16[2,416,128]{2,1,0:T(8,128)(2,1)S(1)}, bf16[2,416,128]{2,1,0:T(8,128)(2,1)S(1)}, u32[]{:S(2)}, u32[]{:S(2)}) %collective-permute-start.22) | collective-permute-done | bytes 213024 | tf_op jit(solution)/shard_map/ppermute | solution.py:622
  398.1 2.5 collective-permute-start.25
  400.6 4.1 collective-permute-done.25.refs_1_
  404.7 2.3 collective-permute-done.28.refs_1_
  407.1 1.0 collective-permute-start.32
  408.4 5.8 %collective-permute-done.27.refs_1_ = bf16[1,288,128]{2,1,0:T(8,128)(2,1)S(1)} collective-permute-done((bf16[1,288,128]{2,1,0:T(8,128)(2,1)S(1)}, bf16[1,288,128]{2,1,0:T(8,128)(2,1)S(1)}, u32[]{:S(2)}, u32[]{:S(2)}) %collective-permute-start.27) | collective-permute-done | bytes 73760 | tf_op jit(solution)/shard_map/ppermute | solution.py:622
  414.5 4.8 %collective-permute-done.29.refs_1_ = bf16[2,288,128]{2,1,0:T(8,128)(2,1)S(1)} collective-permute-done((bf16[2,288,128]{2,1,0:T(8,128)(2,1)S(1)}, bf16[2,288,128]{2,1,0:T(8,128)(2,1)S(1)}, u32[]{:S(2)}, u32[]{:S(2)}) %collective-permute-start.29) | collective-permute-done | bytes 147488 | tf_op jit(solution)/shard_map/ppermute | solution.py:622
  419.4 1.5 collective-permute-done.32.refs_1_
  421.0 1.4 collective-permute-done.31.refs_1_
  422.8 1.0 collective-permute-start.30
  423.8 1.1 collective-permute-start.36
  425.0 7.7 %collective-permute-done.30.refs_1_ = bf16[4,288,128]{2,1,0:T(8,128)(2,1)S(1)} collective-permute-done((bf16[4,288,128]{2,1,0:T(8,128)(2,1)S(1)}, bf16[4,288,128]{2,1,0:T(8,128)(2,1)S(1)}, u32[]{:S(2)}, u32[]{:S(2)}) %collective-permute-start.30) | collective-permute-done | bytes 294944 | tf_op jit(solution)/shard_map/ppermute | solution.py:622
  432.8 1.2 collective-permute-start.33
  433.9 4.8 %spread_near.3 = (f32[768,3072]{1,0:T(8,128)}, f32[8,128]{1,0:T(8,128)S(1)}) custom-call(s32[2]{0:T(128)S(1)} %pad_add_fusion.refs_0_, bf16[16,2,48,1536]{3,2,1,0:T(8,128)(2,1)S(1)} %get-tuple-element.258.refs_1_, bf16[16,2,48,1536]{3,2,1,0:T(8,128)(2,1)S(1)} %collective-permute-done.34.refs_2_, f32[8,128]{1,0:T(8,128)S(1)} %get-tuple-element.259.refs_3_), custom_call_target="tpu_custom_call" | custom-call | flops 9600000000 | tf_op jit(solution)/shard_map/spread_near/pallas_call | solution.py:72
  438.8 5.3 %spread_near.4 = (f32[3072,768]{1,0:T(8,128)}, f32[8,128]{1,0:T(8,128)S(1)}) custom-call(s32[2]{0:T(128)S(1)} %pad_add_fusion.refs_0_, bf16[16,2,48,1536]{3,2,1,0:T(8,128)(2,1)S(1)} %get-tuple-element.258.refs_1_, bf16[16,2,48,1536]{3,2,1,0:T(8,128)(2,1)S(1)} %collective-permute-done.34.refs_2_, f32[8,128]{1,0:T(8,128)S(1)} %get-tuple-element.260.refs_3_), custom_call_target="tpu_custom_call" | custom-call | flops 9600000000 | tf_op jit(solution)/shard_map/spread_near/pallas_call | solution.py:72
  444.1 2.3 collective-permute-done.33.refs_1_
  446.6 1.6 collective-permute-start.37
  448.9 3.5 collective-permute-done.37
  452.3 5.6 %spread_near.5 = (f32[768,2304]{1,0:T(8,128)}, f32[768,768]{1,0:T(8,128)}, f32[8,128]{1,0:T(8,128)S(1)}) custom-call(s32[2]{0:T(128)S(1)} %pad_add_fusion.refs_0_, bf16[16,1,48,1536]{3,2,1,0:T(8,128)(2,1)S(1)} %bitcast.30, bf16[16,1,48,1536]{3,2,1,0:T(8,128)(2,1)S(1)} %bitcast.31, f32[8,128]{1,0:T(8,128)S(1)} %get-tuple-element.266.refs_3_), custom_call_target="tpu_custom_call" | custom-call | flops 9600000000 | tf_op jit(solution)/shard_map/spread_near/pallas_call | solution.py:72
  458.0 3.1 unpack_small.1
  (147 shorter events, 14.5 us)
Async XLA Ops:
  7.2 27.1 %copy-start.12 = (s32[4]{0:T(128)S(1)}, s32[4]{0:T(128)}, u32[]{:S(2)}) copy-start(s32[4]{0:T(128)} %refs_1_.3) | copy-start | bytes 52
  7.2 27.1 %copy-start.10 = (f32[768]{0:T(1024)S(1)}, f32[768]{0:T(1024)}, u32[]{:S(2)}) copy-start(f32[768]{0:T(1024)} %refs_9_.5) | copy-start | bytes 9220
  7.2 27.1 %copy-start.7 = (bf16[128,768]{1,0:T(8,128)(2,1)S(1)}, bf16[128,768]{1,0:T(8,128)(2,1)}, u32[]{:S(2)}) copy-start(bf16[128,768]{1,0:T(8,128)(2,1)} %refs_11_.1) | copy-start | bytes 589828
  7.2 27.1 %copy-start.8 = (f32[8,768]{1,0:T(8,128)S(1)}, f32[8,768]{1,0:T(8,128)}, u32[]{:S(2)}) copy-start(f32[8,768]{1,0:T(8,128)} %refs_7_.3) | copy-start | bytes 73732
  7.2 309.4 %reduce-scatter.2.cloned.1.call-start = ((), (), s32[]{:S(2)}) async-start(), calls=%async_computation.1 | async-start | bytes 9732096 | tf_op jit(solution)/shard_map/reduce_scatter | solution.py:1073
  8.0 7.6 %collective-permute-start = (s32[2,512]{1,0:T(2,128)S(1)}, s32[2,512]{1,0:T(2,128)S(1)}, u32[]{:S(2)}, u32[]{:S(2)}) collective-permute-start(s32[2,512]{1,0:T(2,128)S(1)} %constant_dynamic-slice_fusion.1), channel_id=1, source_target_pairs={{0,1},{1,0},{2,3},{3,2},{4,5},{5,4},{6,7},{7,6},{8,9},{9,8},{10,11... | collective-permute-start | bytes 12296 | tf_op jit(solution)/shard_map/ppermute | solution.py:611
  10.0 6.4 %collective-permute-start.1 = (bf16[1,128,128]{2,1,0:T(8,128)(2,1)S(1)}, bf16[1,128,128]{2,1,0:T(8,128)(2,1)S(1)}, u32[]{:S(2)}, u32[]{:S(2)}) collective-permute-start(bf16[1,128,128]{2,1,0:T(8,128)(2,1)S(1)} %fusion.3), channel_id=1, source_target_pairs={{0,16},{1,17},{2,18},{3,19},{4,20},{5,21},{6,22},{7,23},{8,24},{9,... | collective-permute-start | bytes 98312 | tf_op jit(solution)/shard_map/ppermute | solution.py:622
  14.5 17.9 %collective-permute-start.6 = (bf16[2,512,128]{2,1,0:T(8,128)(2,1)S(1)}, bf16[2,512,128]{2,1,0:T(8,128)(2,1)S(1)}, u32[]{:S(2)}, u32[]{:S(2)}) collective-permute-start(bf16[2,512,128]{2,1,0:T(8,128)(2,1)S(1)} %constant_dynamic-slice_fusion), channel_id=1, source_target_pairs={{0,1},{1,0},{2,3},{3,2},{4,5},{5,4},{6,7},{7,6},{8,9},{9,8},{10,11... | collective-permute-start | bytes 786440 | tf_op jit(solution)/shard_map/ppermute | solution.py:611
  16.4 4.3 collective-permute-start.2
  20.7 5.0 %collective-permute-start.3 = (bf16[4,128,128]{2,1,0:T(8,128)(2,1)S(1)}, bf16[4,128,128]{2,1,0:T(8,128)(2,1)S(1)}, u32[]{:S(2)}, u32[]{:S(2)}) collective-permute-start(bf16[4,128,128]{2,1,0:T(8,128)(2,1)S(1)} %pad_maximum_fusion.2), channel_id=1, source_target_pairs={{0,4},{1,9},{2,6},{3,11},{4,0},{5,13},{6,2},{7,15},{8,12},{9,1},{1... | collective-permute-start | bytes 393224 | tf_op jit(solution)/shard_map/ppermute | solution.py:622
  25.8 6.4 %collective-permute-start.4 = (bf16[8,128,128]{2,1,0:T(8,128)(2,1)S(1)}, bf16[8,128,128]{2,1,0:T(8,128)(2,1)S(1)}, u32[]{:S(2)}, u32[]{:S(2)}) collective-permute-start(bf16[8,128,128]{2,1,0:T(8,128)(2,1)S(1)} %pad_maximum_fusion.1), channel_id=1, source_target_pairs={{0,2},{1,5},{2,0},{3,7},{4,6},{5,1},{6,4},{7,3},{8,10},{9,13},{10,... | collective-permute-start | bytes 786440 | tf_op jit(solution)/shard_map/ppermute | solution.py:622
  32.3 2.0 collective-permute-start.5
  59.6 41.9 %copy-start.22 = (bf16[2048,128]{1,0:T(8,128)(2,1)}, bf16[2048,128]{1,0:T(8,128)(2,1)S(1)}, u32[]{:S(2)}) copy-start(bf16[2048,128]{1,0:T(8,128)(2,1)S(1)} %get-tuple-element.183.refs_6_) | copy-start | bytes 1572868
  59.6 41.9 %copy-start.15 = (f32[8,128]{1,0:T(8,128)}, f32[8,128]{1,0:T(8,128)S(1)}, u32[]{:S(2)}) copy-start(f32[8,128]{1,0:T(8,128)S(1)} %get-tuple-element.146.refs_1_.refs_0_.refs_5_) | copy-start | bytes 12292
  59.6 41.9 %copy-start.21 = (bf16[2048,128]{1,0:T(8,128)(2,1)}, bf16[2048,128]{1,0:T(8,128)(2,1)S(1)}, u32[]{:S(2)}) copy-start(bf16[2048,128]{1,0:T(8,128)(2,1)S(1)} %get-tuple-element.152.refs_4_.refs_7_) | copy-start | bytes 1572868
  59.6 41.9 %copy-start.4 = (bf16[768,768]{1,0:T(8,128)(2,1)S(1)}, bf16[768,768]{1,0:T(8,128)(2,1)}, u32[]{:S(2)}) copy-start(bf16[768,768]{1,0:T(8,128)(2,1)} %refs_4_.2) | copy-start | bytes 3538948
  59.6 41.9 %copy-start.6 = (bf16[768,128]{1,0:T(8,128)(2,1)S(1)}, bf16[768,128]{1,0:T(8,128)(2,1)}, u32[]{:S(2)}) copy-start(bf16[768,128]{1,0:T(8,128)(2,1)} %refs_8_.5) | copy-start | bytes 589828
  59.6 41.9 %copy-start.9 = (f32[768]{0:T(1024)S(1)}, f32[768]{0:T(1024)}, u32[]{:S(2)}) copy-start(f32[768]{0:T(1024)} %refs_5_.3) | copy-start | bytes 9220
  148.4 17.6 %copy-start.20 = (f32[2048,128]{1,0:T(8,128)}, f32[2048,128]{1,0:T(8,128)S(1)}, u32[]{:S(2)}) copy-start(f32[2048,128]{1,0:T(8,128)S(1)} %get-tuple-element.158.refs_2_.refs_8_) | copy-start | bytes 3145732
  203.1 17.3 %slice-start = ((s8[6291456]{0:T(1024)(128)(4,1)}), s8[4194304]{0:T(1024)(128)(4,1)S(1)}, s32[]{:S(2)}) async-start(s8[6291456]{0:T(1024)(128)(4,1)} %bitcast.27), calls=%async_computation.2 | async-start | bytes 8388608
  203.1 17.3 %slice-start.1 = ((s8[6291456]{0:T(1024)(128)(4,1)}), s8[2097152]{0:T(1024)(128)(4,1)S(1)}, s32[]{:S(2)}) async-start(s8[6291456]{0:T(1024)(128)(4,1)} %bitcast.27), calls=%async_computation.3 | async-start | bytes 4194304
  203.1 17.3 %copy-start.1 = (bf16[2048,768]{1,0:T(8,128)(2,1)S(1)}, bf16[2048,768]{1,0:T(8,128)(2,1)}, u32[]{:S(2)}) copy-start(bf16[2048,768]{1,0:T(8,128)(2,1)} %get-tuple-element.164.refs_3_) | copy-start | bytes 9437188
  220.2 22.9 %collective-permute-start.8 = (bf16[16,48,1536]{2,1,0:T(8,128)(2,1)}, bf16[16,48,1536]{2,1,0:T(8,128)(2,1)S(1)}, u32[]{:S(2)}, u32[]{:S(2)}) collective-permute-start(bf16[16,48,1536]{2,1,0:T(8,128)(2,1)} %get-tuple-element.174), channel_id=1, source_target_pairs={{0,1},{1,0},{2,3},{3,2},{4,5},{5,4},{6,7},{7,6},{8,9},{9,8},{10,11... | collective-permute-start | bytes 7077896 | tf_op jit(solution)/shard_map/ppermute | solution.py:611
  243.6 22.0 %collective-permute-start.9 = (bf16[8,48,1536]{2,1,0:T(8,128)(2,1)S(1)}, bf16[8,48,1536]{2,1,0:T(8,128)(2,1)S(1)}, u32[]{:S(2)}, u32[]{:S(2)}) collective-permute-start(bf16[8,48,1536]{2,1,0:T(8,128)(2,1)S(1)} %get-tuple-element.179), channel_id=1, source_target_pairs={{0,2},{1,5},{2,0},{3,7},{4,6},{5,1},{6,4},{7,3},{8,10},{9,13},{10,... | collective-permute-start | bytes 3538952 | tf_op jit(solution)/shard_map/ppermute | solution.py:622
  265.9 21.6 %collective-permute-start.10 = (bf16[4,48,1536]{2,1,0:T(8,128)(2,1)S(1)}, bf16[4,48,1536]{2,1,0:T(8,128)(2,1)S(1)}, u32[]{:S(2)}, u32[]{:S(2)}) collective-permute-start(bf16[4,48,1536]{2,1,0:T(8,128)(2,1)S(1)} %get-tuple-element.185), channel_id=1, source_target_pairs={{0,4},{1,9},{2,6},{3,11},{4,0},{5,13},{6,2},{7,15},{8,12},{9,1},{1... | collective-permute-start | bytes 1769480 | tf_op jit(solution)/shard_map/ppermute | solution.py:622
  287.6 17.9 %collective-permute-start.11 = (bf16[2,48,1536]{2,1,0:T(8,128)(2,1)S(1)}, bf16[2,48,1536]{2,1,0:T(8,128)(2,1)S(1)}, u32[]{:S(2)}, u32[]{:S(2)}) collective-permute-start(bf16[2,48,1536]{2,1,0:T(8,128)(2,1)S(1)} %get-tuple-element.188), channel_id=1, source_target_pairs={{0,8},{1,3},{2,10},{3,1},{4,12},{5,7},{6,14},{7,5},{8,0},{9,11},{1... | collective-permute-start | bytes 884744 | tf_op jit(solution)/shard_map/ppermute | solution.py:622
  305.5 4.7 %collective-permute-start.13 = (bf16[16,48,1536]{2,1,0:T(8,128)(2,1)}, bf16[16,48,1536]{2,1,0:T(8,128)(2,1)S(1)}, u32[]{:S(2)}, u32[]{:S(2)}) collective-permute-start(bf16[16,48,1536]{2,1,0:T(8,128)(2,1)} %get-tuple-element.195), channel_id=1, source_target_pairs={{0,1},{1,0},{2,3},{3,2},{4,5},{5,4},{6,7},{7,6},{8,9},{9,8},{10,11... | collective-permute-start | bytes 7077896 | tf_op jit(solution)/shard_map/ppermute | solution.py:611
  306.3 10.3 %collective-permute-start.12 = (bf16[1,48,1536]{2,1,0:T(8,128)(2,1)S(1)}, bf16[1,48,1536]{2,1,0:T(8,128)(2,1)}, u32[]{:S(2)}, u32[]{:S(2)}) collective-permute-start(bf16[1,48,1536]{2,1,0:T(8,128)(2,1)S(1)} %get-tuple-element.192), channel_id=1, source_target_pairs={{0,16},{1,17},{2,18},{3,19},{4,20},{5,21},{6,22},{7,23},{8,24},{9,... | collective-permute-start | bytes 442376 | tf_op jit(solution)/shard_map/ppermute | solution.py:622
  308.8 54.0 %collective-permute-start.7 = (bf16[2,512,768]{2,1,0:T(8,128)(2,1)}, bf16[2,512,768]{2,1,0:T(8,128)(2,1)}, u32[]{:S(2)}, u32[]{:S(2)}) collective-permute-start(bf16[2,512,768]{2,1,0:T(8,128)(2,1)} %get-tuple-element.155), channel_id=1, source_target_pairs={{0,1},{1,0},{2,3},{3,2},{4,5},{5,4},{6,7},{7,6},{8,9},{9,8},{10,11... | collective-permute-start | bytes 4718600 | tf_op jit(solution)/shard_map/ppermute | solution.py:611
  312.3 30.0 %collective-permute-start.15 = (bf16[8,48,1536]{2,1,0:T(8,128)(2,1)}, bf16[8,48,1536]{2,1,0:T(8,128)(2,1)S(1)}, u32[]{:S(2)}, u32[]{:S(2)}) collective-permute-start(bf16[8,48,1536]{2,1,0:T(8,128)(2,1)} %get-tuple-element.209), channel_id=1, source_target_pairs={{0,2},{1,5},{2,0},{3,7},{4,6},{5,1},{6,4},{7,3},{8,10},{9,13},{10,... | collective-permute-start | bytes 3538952 | tf_op jit(solution)/shard_map/ppermute | solution.py:622
  318.5 25.7 %collective-permute-start.14 = (bf16[1,2,48,1536]{3,2,1,0:T(8,128)(2,1)}, bf16[1,2,48,1536]{3,2,1,0:T(8,128)(2,1)}, u32[]{:S(2)}, u32[]{:S(2)}) collective-permute-start(bf16[1,2,48,1536]{3,2,1,0:T(8,128)(2,1)} %bitcast.32), channel_id=1, source_target_pairs={{0,16},{1,17},{2,18},{3,19},{4,20},{5,21},{6,22},{7,23},{8,24},{9,... | collective-permute-start | bytes 884744 | tf_op jit(solution)/shard_map/ppermute | solution.py:622
  318.5 25.7 %copy-start.5 = (bf16[2,48,1536]{2,1,0:T(8,128)(2,1)S(1)}, bf16[2,48,1536]{2,1,0:T(8,128)(2,1)}, u32[]{:S(2)}) copy-start(bf16[2,48,1536]{2,1,0:T(8,128)(2,1)} %get-tuple-element.207) | copy-start | bytes 884740
  342.2 5.8 %copy-start.13 = (s32[4]{0:T(128)S(1)}, s32[4]{0:T(128)}, u32[]{:S(2)}) copy-start(s32[4]{0:T(128)} %refs_1_.3) | copy-start | bytes 52
  342.3 5.8 %copy-start.28 = (f32[1,768]{1,0:T(1,128)S(1)}, f32[1,768]{1,0:T(1,128)}, u32[]{:S(2)}) copy-start(f32[1,768]{1,0:T(1,128)} %get-tuple-element.203.refs_6_) | copy-start | bytes 9220
  343.0 5.1 %copy-start.19 = (f32[1024,768]{1,0:T(8,128)S(1)}, f32[1024,768]{1,0:T(8,128)}, u32[]{:S(2)}) copy-start(f32[1024,768]{1,0:T(8,128)} %get-tuple-element.199.refs_2_) | copy-start | bytes 9437188
  343.0 5.1 %copy-start.23 = (bf16[2048,128]{1,0:T(8,128)(2,1)S(1)}, bf16[2048,128]{1,0:T(8,128)(2,1)}, u32[]{:S(2)}) copy-start(bf16[2048,128]{1,0:T(8,128)(2,1)} %get-tuple-element.206.refs_10_) | copy-start | bytes 1572868
  343.0 5.1 %copy-start.24 = (f32[128,768]{1,0:T(8,128)S(1)}, f32[128,768]{1,0:T(8,128)}, u32[]{:S(2)}) copy-start(f32[128,768]{1,0:T(8,128)} %get-tuple-element.200.refs_3_) | copy-start | bytes 1179652
  343.0 5.1 %copy-start.26 = (f32[128,768]{1,0:T(8,128)S(1)}, f32[128,768]{1,0:T(8,128)}, u32[]{:S(2)}) copy-start(f32[128,768]{1,0:T(8,128)} %copy-done.25) | copy-start | bytes 1179652
  343.0 5.1 %copy-start.27 = (f32[2,768]{1,0:T(2,128)S(1)}, f32[2,768]{1,0:T(2,128)}, u32[]{:S(2)}) copy-start(f32[2,768]{1,0:T(2,128)} %get-tuple-element.202.refs_5_) | copy-start | bytes 18436
  343.0 5.1 %copy-start.29 = (f32[1,128]{1,0:T(1,128)S(1)}, f32[1,128]{1,0:T(1,128)}, u32[]{:S(2)}) copy-start(f32[1,128]{1,0:T(1,128)} %get-tuple-element.205.refs_8_) | copy-start | bytes 1540
  343.2 11.5 %collective-permute-start.18 = (bf16[4,48,1536]{2,1,0:T(8,128)(2,1)S(1)}, bf16[4,48,1536]{2,1,0:T(8,128)(2,1)S(1)}, u32[]{:S(2)}, u32[]{:S(2)}) collective-permute-start(bf16[4,48,1536]{2,1,0:T(8,128)(2,1)S(1)} %get-tuple-element.217), channel_id=1, source_target_pairs={{0,4},{1,9},{2,6},{3,11},{4,0},{5,13},{6,2},{7,15},{8,12},{9,1},{1... | collective-permute-start | bytes 1769480 | tf_op jit(solution)/shard_map/ppermute | solution.py:622
  345.3 13.2 %collective-permute-start.17 = (bf16[2,2,48,1536]{3,2,1,0:T(8,128)(2,1)S(1)}, bf16[2,2,48,1536]{3,2,1,0:T(8,128)(2,1)S(1)}, u32[]{:S(2)}, u32[]{:S(2)}) collective-permute-start(bf16[2,2,48,1536]{3,2,1,0:T(8,128)(2,1)S(1)} %get-tuple-element.215.refs_0_), channel_id=1, source_target_pairs={{0,8},{1,3},{2,10},{3,1},{4,12},{5,7},{6,14},{7,5},{8,0},{9,11},{1... | collective-permute-start | bytes 1769480 | tf_op jit(solution)/shard_map/ppermute | solution.py:622
  354.6 4.0 collective-permute-start.16
  358.7 4.1 copy-start.18
  359.0 15.4 %collective-permute-start.19 = (bf16[8,416,128]{2,1,0:T(8,128)(2,1)S(1)}, bf16[8,416,128]{2,1,0:T(8,128)(2,1)S(1)}, u32[]{:S(2)}, u32[]{:S(2)}) collective-permute-start(bf16[8,416,128]{2,1,0:T(8,128)(2,1)S(1)} %get-tuple-element.224), channel_id=1, source_target_pairs={{0,2},{1,5},{2,0},{3,7},{4,6},{5,1},{6,4},{7,3},{8,10},{9,13},{10,... | collective-permute-start | bytes 2555912 | tf_op jit(solution)/shard_map/ppermute | solution.py:622
  360.3 15.4 %collective-permute-start.21 = (bf16[2,48,1536]{2,1,0:T(8,128)(2,1)S(1)}, bf16[2,48,1536]{2,1,0:T(8,128)(2,1)S(1)}, u32[]{:S(2)}, u32[]{:S(2)}) collective-permute-start(bf16[2,48,1536]{2,1,0:T(8,128)(2,1)S(1)} %get-tuple-element.229), channel_id=1, source_target_pairs={{0,8},{1,3},{2,10},{3,1},{4,12},{5,7},{6,14},{7,5},{8,0},{9,11},{1... | collective-permute-start | bytes 884744 | tf_op jit(solution)/shard_map/ppermute | solution.py:622
  362.0 25.9 %collective-permute-start.23 = (bf16[4,2,48,1536]{3,2,1,0:T(8,128)(2,1)S(1)}, bf16[4,2,48,1536]{3,2,1,0:T(8,128)(2,1)S(1)}, u32[]{:S(2)}, u32[]{:S(2)}) collective-permute-start(bf16[4,2,48,1536]{3,2,1,0:T(8,128)(2,1)S(1)} %get-tuple-element.234.refs_0_), channel_id=1, source_target_pairs={{0,4},{1,9},{2,6},{3,11},{4,0},{5,13},{6,2},{7,15},{8,12},{9,1},{1... | collective-permute-start | bytes 3538952 | tf_op jit(solution)/shard_map/ppermute | solution.py:622
  374.6 13.2 %collective-permute-start.20 = (bf16[4,416,128]{2,1,0:T(8,128)(2,1)S(1)}, bf16[4,416,128]{2,1,0:T(8,128)(2,1)S(1)}, u32[]{:S(2)}, u32[]{:S(2)}) collective-permute-start(bf16[4,416,128]{2,1,0:T(8,128)(2,1)S(1)} %get-tuple-element.227), channel_id=1, source_target_pairs={{0,4},{1,9},{2,6},{3,11},{4,0},{5,13},{6,2},{7,15},{8,12},{9,1},{1... | collective-permute-start | bytes 1277960 | tf_op jit(solution)/shard_map/ppermute | solution.py:622
  375.8 12.1 %collective-permute-start.24 = (bf16[1,48,1536]{2,1,0:T(8,128)(2,1)S(1)}, bf16[1,48,1536]{2,1,0:T(8,128)(2,1)S(1)}, u32[]{:S(2)}, u32[]{:S(2)}) collective-permute-start(bf16[1,48,1536]{2,1,0:T(8,128)(2,1)S(1)} %get-tuple-element.236), channel_id=1, source_target_pairs={{0,16},{1,17},{2,18},{3,19},{4,20},{5,21},{6,22},{7,23},{8,24},{9,... | collective-permute-start | bytes 442376 | tf_op jit(solution)/shard_map/ppermute | solution.py:622
  388.1 34.4 %collective-permute-start.31 = (bf16[8,2,48,1536]{3,2,1,0:T(8,128)(2,1)S(1)}, bf16[8,2,48,1536]{3,2,1,0:T(8,128)(2,1)S(1)}, u32[]{:S(2)}, u32[]{:S(2)}) collective-permute-start(bf16[8,2,48,1536]{3,2,1,0:T(8,128)(2,1)S(1)} %get-tuple-element.252.refs_0_), channel_id=1, source_target_pairs={{0,2},{1,5},{2,0},{3,7},{4,6},{5,1},{6,4},{7,3},{8,10},{9,13},{10,... | collective-permute-start | bytes 7077896 | tf_op jit(solution)/shard_map/ppermute | solution.py:622
  389.0 8.9 %collective-permute-start.22 = (bf16[2,416,128]{2,1,0:T(8,128)(2,1)S(1)}, bf16[2,416,128]{2,1,0:T(8,128)(2,1)S(1)}, u32[]{:S(2)}, u32[]{:S(2)}) collective-permute-start(bf16[2,416,128]{2,1,0:T(8,128)(2,1)S(1)} %get-tuple-element.233), channel_id=1, source_target_pairs={{0,8},{1,3},{2,10},{3,1},{4,12},{5,7},{6,14},{7,5},{8,0},{9,11},{1... | collective-permute-start | bytes 638984 | tf_op jit(solution)/shard_map/ppermute | solution.py:622
  389.1 8.9 %collective-permute-start.26 = (bf16[1,48,1536]{2,1,0:T(8,128)(2,1)S(1)}, bf16[1,48,1536]{2,1,0:T(8,128)(2,1)S(1)}, u32[]{:S(2)}, u32[]{:S(2)}) collective-permute-start(bf16[1,48,1536]{2,1,0:T(8,128)(2,1)S(1)} %bitcast.34), channel_id=1, source_target_pairs={{0,16},{1,17},{2,18},{3,19},{4,20},{5,21},{6,22},{7,23},{8,24},{9,... | collective-permute-start | bytes 442376 | tf_op jit(solution)/shard_map/ppermute | solution.py:622
  398.0 9.0 %collective-permute-start.28 = (bf16[2,48,1536]{2,1,0:T(8,128)(2,1)S(1)}, bf16[2,48,1536]{2,1,0:T(8,128)(2,1)S(1)}, u32[]{:S(2)}, u32[]{:S(2)}) collective-permute-start(bf16[2,48,1536]{2,1,0:T(8,128)(2,1)S(1)} %get-tuple-element.246.refs_0_), channel_id=1, source_target_pairs={{0,8},{1,3},{2,10},{3,1},{4,12},{5,7},{6,14},{7,5},{8,0},{9,11},{1... | collective-permute-start | bytes 884744 | tf_op jit(solution)/shard_map/ppermute | solution.py:622
  398.1 6.6 %collective-permute-start.25 = (bf16[1,416,128]{2,1,0:T(8,128)(2,1)S(1)}, bf16[1,416,128]{2,1,0:T(8,128)(2,1)S(1)}, u32[]{:S(2)}, u32[]{:S(2)}) collective-permute-start(bf16[1,416,128]{2,1,0:T(8,128)(2,1)S(1)} %get-tuple-element.241), channel_id=1, source_target_pairs={{0,16},{1,17},{2,18},{3,19},{4,20},{5,21},{6,22},{7,23},{8,24},{9,... | collective-permute-start | bytes 319496 | tf_op jit(solution)/shard_map/ppermute | solution.py:622
  407.1 13.9 %collective-permute-start.32 = (bf16[4,48,1536]{2,1,0:T(8,128)(2,1)S(1)}, bf16[4,48,1536]{2,1,0:T(8,128)(2,1)S(1)}, u32[]{:S(2)}, u32[]{:S(2)}) collective-permute-start(bf16[4,48,1536]{2,1,0:T(8,128)(2,1)S(1)} %get-tuple-element.253.refs_0_), channel_id=1, source_target_pairs={{0,4},{1,9},{2,6},{3,11},{4,0},{5,13},{6,2},{7,15},{8,12},{9,1},{1... | collective-permute-start | bytes 1769480 | tf_op jit(solution)/shard_map/ppermute | solution.py:622
  408.1 6.1 %collective-permute-start.27 = (bf16[1,288,128]{2,1,0:T(8,128)(2,1)S(1)}, bf16[1,288,128]{2,1,0:T(8,128)(2,1)S(1)}, u32[]{:S(2)}, u32[]{:S(2)}) collective-permute-start(bf16[1,288,128]{2,1,0:T(8,128)(2,1)S(1)} %fusion.refs_0_), channel_id=1, source_target_pairs={{0,16},{1,17},{2,18},{3,19},{4,20},{5,21},{6,22},{7,23},{8,24},{9,... | collective-permute-start | bytes 221192 | tf_op jit(solution)/shard_map/ppermute | solution.py:622
  414.2 5.2 %collective-permute-start.29 = (bf16[2,288,128]{2,1,0:T(8,128)(2,1)S(1)}, bf16[2,288,128]{2,1,0:T(8,128)(2,1)S(1)}, u32[]{:S(2)}, u32[]{:S(2)}) collective-permute-start(bf16[2,288,128]{2,1,0:T(8,128)(2,1)S(1)} %get-tuple-element.249.refs_0_), channel_id=1, source_target_pairs={{0,8},{1,3},{2,10},{3,1},{4,12},{5,7},{6,14},{7,5},{8,0},{9,11},{1... | collective-permute-start | bytes 442376 | tf_op jit(solution)/shard_map/ppermute | solution.py:622
  422.8 11.2 %collective-permute-start.34 = (bf16[16,2,48,1536]{3,2,1,0:T(8,128)(2,1)S(1)}, bf16[16,2,48,1536]{3,2,1,0:T(8,128)(2,1)S(1)}, u32[]{:S(2)}, u32[]{:S(2)}) collective-permute-start(bf16[16,2,48,1536]{3,2,1,0:T(8,128)(2,1)S(1)} %get-tuple-element.258.refs_1_), channel_id=1, source_target_pairs={{0,1},{1,0},{2,3},{3,2},{4,5},{5,4},{6,7},{7,6},{8,9},{9,8},{10,11... | collective-permute-start | bytes 14155784 | tf_op jit(solution)/shard_map/ppermute | solution.py:611
  422.8 9.9 %collective-permute-start.30 = (bf16[4,288,128]{2,1,0:T(8,128)(2,1)S(1)}, bf16[4,288,128]{2,1,0:T(8,128)(2,1)S(1)}, u32[]{:S(2)}, u32[]{:S(2)}) collective-permute-start(bf16[4,288,128]{2,1,0:T(8,128)(2,1)S(1)} %get-tuple-element.251.refs_0_), channel_id=1, source_target_pairs={{0,4},{1,9},{2,6},{3,11},{4,0},{5,13},{6,2},{7,15},{8,12},{9,1},{1... | collective-permute-start | bytes 884744 | tf_op jit(solution)/shard_map/ppermute | solution.py:622
  423.8 22.6 %collective-permute-start.36 = (bf16[8,48,1536]{2,1,0:T(8,128)(2,1)S(1)}, bf16[8,48,1536]{2,1,0:T(8,128)(2,1)S(1)}, u32[]{:S(2)}, u32[]{:S(2)}) collective-permute-start(bf16[8,48,1536]{2,1,0:T(8,128)(2,1)S(1)} %get-tuple-element.263.refs_0_), channel_id=1, source_target_pairs={{0,2},{1,5},{2,0},{3,7},{4,6},{5,1},{6,4},{7,3},{8,10},{9,13},{10,... | collective-permute-start | bytes 3538952 | tf_op jit(solution)/shard_map/ppermute | solution.py:622
  432.8 13.6 %collective-permute-start.33 = (bf16[8,288,128]{2,1,0:T(8,128)(2,1)S(1)}, bf16[8,288,128]{2,1,0:T(8,128)(2,1)S(1)}, u32[]{:S(2)}, u32[]{:S(2)}) collective-permute-start(bf16[8,288,128]{2,1,0:T(8,128)(2,1)S(1)} %get-tuple-element.257.refs_0_), channel_id=1, source_target_pairs={{0,2},{1,5},{2,0},{3,7},{4,6},{5,1},{6,4},{7,3},{8,10},{9,13},{10,... | collective-permute-start | bytes 1769480 | tf_op jit(solution)/shard_map/ppermute | solution.py:622
  446.6 5.7 %collective-permute-start.37 = (bf16[16,48,1536]{2,1,0:T(8,128)(2,1)S(1)}, bf16[16,48,1536]{2,1,0:T(8,128)(2,1)S(1)}, u32[]{:S(2)}, u32[]{:S(2)}) collective-permute-start(bf16[16,48,1536]{2,1,0:T(8,128)(2,1)S(1)} %get-tuple-element.265), channel_id=1, source_target_pairs={{0,1},{1,0},{2,3},{3,2},{4,5},{5,4},{6,7},{7,6},{8,9},{9,8},{10,11... | collective-permute-start | bytes 7077896 | tf_op jit(solution)/shard_map/ppermute | solution.py:611
  448.2 9.8 %collective-permute-start.35 = (bf16[16,288,128]{2,1,0:T(8,128)(2,1)S(1)}, bf16[16,288,128]{2,1,0:T(8,128)(2,1)S(1)}, u32[]{:S(2)}, u32[]{:S(2)}) collective-permute-start(bf16[16,288,128]{2,1,0:T(8,128)(2,1)S(1)} %get-tuple-element.262.refs_1_), channel_id=1, source_target_pairs={{0,1},{1,0},{2,3},{3,2},{4,5},{5,4},{6,7},{7,6},{8,9},{9,8},{10,11... | collective-permute-start | bytes 3538952 | tf_op jit(solution)/shard_map/ppermute | solution.py:611
  452.3 5.6 %copy-start.2 = (bf16[120,128]{1,0:T(8,128)(2,1)S(1)}, bf16[120,128]{1,0:T(8,128)(2,1)}, u32[]{:S(2)}) copy-start(bf16[120,128]{1,0:T(8,128)(2,1)} %refs_4_.3) | copy-start | bytes 92164
  (7 other events, 9.7 us)
Sparse Core Ops, SparseCore 0:
  166.1 144.0 reduce-scatter.1
